TPU v7x, 1024 devices: a whole 4x8x16 slice. The times are simulated.
1024 devices in a mesh: uv: 64 (over z, y_hi), tm: 16 (over x, y_lo, core).
Axes of the slice: x: 4, y: 8 (y_hi: 4, y_lo: 2; y = y_hi * 2 + y_lo), z: 16, core: 2. Of those that a mesh axis runs over, the one named last changes fastest.
Arguments:
- visibility: bfloat16 [3, 64, 256, 8, 128], P(None, 'uv', 'tm'), may hold values from -0.15625 to 0.15625
- coordinate: bfloat16 [3, 64, 256, 2, 128], P(None, 'uv', 'tm'), may hold values from 0 to 64
- block_count: int32 [3, 64, 256], P(None, 'uv', 'tm'), may hold values from 1 to 128
- owner_index: int32 [3, 64, 256, 1], P(None, 'uv', 'tm'), may hold values from 0 to 15; in each aligned block of 16 rows (0 to 15, 16 to 31, ..., all dimensions but the last counted through in order) at most 2 rows name the same one
- subgrid_index: int32 [3, 64, 256], P(None, 'uv', 'tm'), may hold values from 0 to 3
- offsets: int32 [64, 64, 2], P('uv', 'tm'), may hold values from 0 to 31
- station_pair: int32 [64, 64, 2], P('uv', 'tm'), may hold values from 0 to 63
- screens: bfloat16 [64, 64, 8, 1024], P('uv'), may hold values from -3 to 3
- slot_owner: int32 [3], replicated, may hold values from 0 to 63
Outputs:
- gridded: float32 [64, 64, 8, 1024], P('uv', 'tm')
Inputs may be any that keep to these rules, and one draw needn't show every extreme that they name: `owner_index`: in each slot, at most 2 of the 16 blocks of one device name the same owner, and that many do on some device.
All inputs are finite; a program needn't handle non-finite values.
Results may differ from a plain program's by a relative error of at most 0.0035.
Values may be sent and summed in bfloat16 or wider, within the bound.
No kernel may reach another device: no remote copies, remote signals or barrier semaphores. Data moves between devices by JAX's collectives and lax.ppermute only.
A program may use at most 32 MiB of HBM per device.

v0:
```python
import math

import jax
import jax.numpy as jnp
from jax import lax
from jax.sharding import PartitionSpec as P

SIDE = 32


full_turn = 2.0 * math.pi


def from_root(array, axis, root):
    mine = lax.axis_index(axis) == root
    return lax.psum(jnp.where(mine, array, jnp.zeros_like(array)), axis)


def grid_terms(packed, shift_u, shift_v):
    centred = jnp.arange(SIDE, dtype=jnp.float32) - jnp.float32(SIDE // 2)
    values = packed[:, 0:8, :].astype(jnp.float32)
    delta_u = packed[:, 8, :].astype(jnp.float32) - shift_u[:, None]
    delta_v = packed[:, 9, :].astype(jnp.float32) - shift_v[:, None]
    angle_u = full_turn / SIDE * centred[None, :, None] * delta_u[:, None, :]
    angle_v = full_turn / SIDE * centred[None, :, None] * delta_v[:, None, :]
    left_table = jnp.concatenate([jnp.cos(angle_u), jnp.sin(angle_u)], axis=1).astype(jnp.bfloat16)
    cos_v = jnp.cos(angle_v)[:, None, :, :]
    sin_v = jnp.sin(angle_v)[:, None, :, :]
    real_vis = values[:, 0:4, None, :]
    imag_vis = values[:, 4:8, None, :]
    real_w = real_vis * cos_v - imag_vis * sin_v
    imag_w = real_vis * sin_v + imag_vis * cos_v
    right_table = jnp.concatenate([real_w, imag_w], axis=1)
    right_table = right_table.reshape(packed.shape[0], 8 * SIDE, packed.shape[2]).astype(
        jnp.bfloat16
    )
    return jnp.einsum("blr,bkr->blk", left_table, right_table, preferred_element_type=jnp.float32)


def arrange(summed):
    count_sub = summed.shape[0]
    upper = summed[:, :SIDE, :]
    lower = summed[:, SIDE:, :]
    half_cols = 4 * SIDE
    real_part = upper[:, :, :half_cols] - lower[:, :, half_cols:]
    imag_part = upper[:, :, half_cols:] + lower[:, :, :half_cols]
    stacked = jnp.stack([real_part, imag_part], axis=1)
    stacked = stacked.reshape(count_sub, 2, SIDE, 4, SIDE).transpose(0, 1, 3, 2, 4)
    return stacked.reshape(count_sub, 8, SIDE * SIDE)


def matrix_product(first, second, conjugate_right):
    real_list = []
    imag_list = []
    for i in range(2):
        for j in range(2):
            real_sum = jnp.zeros_like(first[:, 0, :])
            imag_sum = jnp.zeros_like(first[:, 0, :])
            for k in range(2):
                left_real = first[:, 2 * i + k, :]
                left_imag = first[:, 4 + 2 * i + k, :]
                if conjugate_right:
                    right_real = second[:, 2 * j + k, :]
                    right_imag = -second[:, 4 + 2 * j + k, :]
                else:
                    right_real = second[:, 2 * k + j, :]
                    right_imag = second[:, 4 + 2 * k + j, :]
                real_sum = real_sum + left_real * right_real - left_imag * right_imag
                imag_sum = imag_sum + left_real * right_imag + left_imag * right_real
            real_list.append(real_sum)
            imag_list.append(imag_sum)
    return jnp.stack(real_list + imag_list, axis=1)


def apply_screens(subgrid_image, jones_table, pairs):
    first = jnp.take(jones_table, pairs[:, 0], axis=0).astype(jnp.float32)
    second = jnp.take(jones_table, pairs[:, 1], axis=0).astype(jnp.float32)
    return matrix_product(matrix_product(first, subgrid_image, False), second, True)


def on_device(
    visibility,
    coordinate,
    block_count,
    owner_index,
    subgrid_index,
    offsets,
    station_pair,
    screens,
    slot_owner,
):
    slot_number = visibility.shape[0]
    blocks = visibility.shape[2]
    row_count = visibility.shape[4]
    peers = lax.axis_size("tm")
    capacity = 2 * blocks // peers
    local_subs = offsets.shape[1]
    shift_table = offsets[0].astype(jnp.float32)
    pairs = station_pair[0]
    jones_local = screens[0]
    earlier = (jnp.arange(blocks)[:, None] > jnp.arange(blocks)[None, :]).astype(jnp.float32)
    accumulated = jnp.zeros((local_subs, 8, SIDE * SIDE), jnp.float32)
    for slot_id in range(slot_number):
        live_rows = jnp.arange(row_count)[None, :] < block_count[slot_id, 0][:, None]
        samples = jnp.where(
            live_rows[:, None, :], visibility[slot_id, 0], jnp.zeros((), jnp.bfloat16)
        )
        packed = jnp.concatenate([samples, coordinate[slot_id, 0]], axis=1)
        owner_row = owner_index[slot_id, 0, :, 0]
        chosen = (owner_row[:, None] == jnp.arange(peers)[None, :]).astype(jnp.float32)
        before = jnp.dot(earlier, chosen, precision=lax.Precision.HIGHEST)
        rank_within = jnp.sum(before * chosen, axis=1).astype(jnp.int32)
        position = owner_row * capacity + rank_within
        send_rows = (
            jnp.zeros((peers * capacity, 10, row_count), jnp.bfloat16).at[position].set(packed)
        )
        send_rows = send_rows.reshape(peers, capacity, 10, row_count)
        send_subs = (
            jnp.zeros((peers * capacity,), jnp.int32).at[position].set(subgrid_index[slot_id, 0])
        )
        send_subs = send_subs.reshape(peers, capacity)
        rows_in = lax.all_to_all(send_rows, "tm", split_axis=0, concat_axis=0, tiled=True)
        subs_in = lax.all_to_all(send_subs, "tm", split_axis=0, concat_axis=0, tiled=True)
        flat_rows = rows_in.reshape((-1,) + rows_in.shape[2:])
        anchor = jnp.take(shift_table, subs_in.reshape(-1), axis=0)
        block_terms = grid_terms(flat_rows, anchor[:, 0], anchor[:, 1])
        block_terms, arrived = (
            block_terms.reshape(rows_in.shape[:2] + block_terms.shape[1:]),
            subs_in,
        )
        flat_terms = block_terms.reshape((-1,) + block_terms.shape[2:])
        member = (arrived.reshape(-1)[:, None] == jnp.arange(local_subs)[None, :]).astype(
            jnp.float32
        )
        summed = jnp.einsum("bs,blk->slk", member, flat_terms, precision=lax.Precision.HIGHEST)
        subgrid_image = arrange(summed)
        root_owner = slot_owner[slot_id]
        jones_table = from_root(jones_local, "uv", root_owner)
        accumulated = accumulated + apply_screens(subgrid_image, jones_table, pairs)
    return accumulated[None]


def solution(mesh):
    placed = (
        P(None, "uv", "tm", None, None),
        P(None, "uv", "tm", None, None),
        P(None, "uv", "tm"),
        P(None, "uv", "tm", None),
        P(None, "uv", "tm"),
        P("uv", "tm", None),
        P("uv", "tm", None),
        P("uv", None, None, None),
        P(),
    )
    return jax.shard_map(
        on_device, mesh=mesh, in_specs=placed, out_specs=P("uv", "tm", None, None), check_vma=False
    )
```

profile of v0, /device:TPU:6, one launch (start us, length us, event | category | flops | bytes accessed | tf_op | source)
XLA Modules:
  0.0 688.3 jit_solution(2610258452613896607)
XLA Ops:
  10.4 16.4 %all-to-all-start.2 = ((s32[16,1,2]{2,1,0:T(1,128)}), s32[16,1,2]{2,1,0:T(1,128)S(1)}, u32[]{:S(2)}, u32[]{:S(2)}) async-start(s32[16,1,2]{2,1,0:T(1,128)} %bitcast.37), calls=%async_computation.2 | async-start | bytes 16384 | tf_op jit(solution)/shard_map/all_to_all | solution.py:123
  26.8 1.4 fusion.54
  30.1 3.0 select_bitcast_fusion.1
  42.7 5.7 all-to-all-start
  49.7 2.8 all-to-all-done
  52.5 5.5 all-to-all-start.4
  58.8 3.2 all-to-all-done.4
  62.0 5.4 all-to-all-start.5
  71.6 5.7 all-to-all-start.1
  77.5 4.0 all-to-all-done.1
  81.5 5.7 all-to-all-start.3
  87.4 4.1 all-to-all-done.3
  91.6 12.1 %fusion.11 = (bf16[32,32,128]{2,1,0:T(8,128)(2,1)S(1)}, bf16[32,32,128]{2,1,0:T(8,128)(2,1)}, f32[32,32,128]{2,1,0:T(8,128)}, f32[32,32,128]{2,1,0:T(8,128)}, f3...) fusion(f32[32,128]{1,0:T(8,128)S(1)} %get-tuple-element.92, ...), kind=kLoop, calls=%fused_computation.53 | loop fusion | flops 1572864 | bytes 4817024 | tf_op jit(solution)/shard_map/convert.6
  105.4 2.0 fusion
  109.3 1.9 subtract_convert_fusion.2
  115.5 2.0 fusion.4
  121.0 2.2 fusion.2
  124.2 542.3 %all-reduce.3.cloned.1.call-done = (bf16[64,8,1024]{2,1,0:T(8,128)(2,1)}, bf16[64,8,1024]{2,1,0:T(8,128)(2,1)}, bf16[64,8,1024]{2,1,0:T(8,128)(2,1)}) async-done(((bf16[64,8,1024]{2,1,0:T(8,128)(2,1)}, bf16[64,8,1024]{2,1,0:T(8,128)(2,1)}, bf16[64,8,1024]{2,1,0:T(8,128)(2,1)}), (bf16[64,8,1024]{2,1,0:T(8,128)(2,1)}, bf16[64,8,1024]{2,1,0:T(8,128)(2,1)}, ...) | async-done | bytes 3145744 | tf_op jit(solution)/shard_map/psum | solution.py:16
  666.5 1.8 gather_fusion.8
  668.3 1.8 gather_fusion.2
  670.1 1.8 gather_fusion
  671.9 1.8 gather_fusion.6
  673.7 1.8 gather_fusion.5
  675.4 1.8 gather_fusion.3
  (153 shorter events, 36.4 us)
Async XLA Ops:
  10.4 32.4 %all-to-all-start.2 = ((s32[16,1,2]{2,1,0:T(1,128)}), s32[16,1,2]{2,1,0:T(1,128)S(1)}, u32[]{:S(2)}, u32[]{:S(2)}) async-start(s32[16,1,2]{2,1,0:T(1,128)} %bitcast.37), calls=%async_computation.2 | async-start | bytes 16384 | tf_op jit(solution)/shard_map/all_to_all | solution.py:123
  26.8 639.7 %all-reduce.3.cloned.1.call-start = ((), (), s32[]{:S(2)}) async-start(), calls=%async_computation.6 | async-start | bytes 6291456 | tf_op jit(solution)/shard_map/psum | solution.py:16
  33.1 0.7 copy-start.12
  33.1 1.2 copy-start.8
  33.1 1.3 copy-start.11
  33.1 1.5 copy-start.7
  33.1 3.3 copy-start.13
  42.7 9.8 %all-to-all-start = ((s32[16,1,2]{2,1,0:T(1,128)}), s32[16,1,2]{2,1,0:T(1,128)S(1)}, u32[]{:S(2)}, u32[]{:S(2)}) async-start(s32[16,1,2]{2,1,0:T(1,128)} %bitcast.9), calls=%async_computation | async-start | bytes 16384 | tf_op jit(solution)/shard_map/all_to_all | solution.py:123
  52.5 9.4 %all-to-all-start.4 = ((s32[16,1,2]{2,1,0:T(1,128)}), s32[16,1,2]{2,1,0:T(1,128)S(1)}, u32[]{:S(2)}, u32[]{:S(2)}) async-start(s32[16,1,2]{2,1,0:T(1,128)} %bitcast.63), calls=%async_computation.4 | async-start | bytes 16384 | tf_op jit(solution)/shard_map/all_to_all | solution.py:123
  62.0 9.7 %all-to-all-start.5 = ((bf16[16,2,10,128]{3,1,2,0:T(2,128)(2,1)}), bf16[16,2,10,128]{3,1,2,0:T(2,128)(2,1)S(1)}, u32[]{:S(2)}, u32[]{:S(2)}) async-start(bf16[16,2,10,128]{3,1,2,0:T(2,128)(2,1)} %copy.66), calls=%async_computation.5 | async-start | bytes 163840 | tf_op jit(solution)/shard_map/all_to_all | solution.py:122
  71.6 9.9 %all-to-all-start.1 = ((bf16[16,2,10,128]{3,1,2,0:T(2,128)(2,1)}), bf16[16,2,10,128]{3,1,2,0:T(2,128)(2,1)S(1)}, u32[]{:S(2)}, u32[]{:S(2)}) async-start(bf16[16,2,10,128]{3,1,2,0:T(2,128)(2,1)} %copy.50), calls=%async_computation.1 | async-start | bytes 163840 | tf_op jit(solution)/shard_map/all_to_all | solution.py:122
  81.5 10.0 %all-to-all-start.3 = ((bf16[16,2,10,128]{3,1,2,0:T(2,128)(2,1)}), bf16[16,2,10,128]{3,1,2,0:T(2,128)(2,1)S(1)}, u32[]{:S(2)}, u32[]{:S(2)}) async-start(bf16[16,2,10,128]{3,1,2,0:T(2,128)(2,1)} %copy.58), calls=%async_computation.3 | async-start | bytes 163840 | tf_op jit(solution)/shard_map/all_to_all | solution.py:122
  91.5 12.2 %copy-start.5 = (bf16[16,2,10,128]{3,1,0,2:T(2,128)(2,1)}, bf16[16,2,10,128]{3,1,0,2:T(2,128)(2,1)S(1)}, u32[]{:S(2)}) copy-start(bf16[16,2,10,128]{3,1,0,2:T(2,128)(2,1)S(1)} %copy.59) | copy-start | bytes 245764
  109.2 2.0 copy-start.3
  109.2 2.0 copy-start.4
  113.6 1.0 copy-start.1
  113.6 1.0 copy-start.2
  117.5 1.0 copy-start.6
  119.2 1.0 copy-start
  123.3 554.0 %copy-start.9 = (pred[4]{0:T(512)(128)(4,1)S(1)}, pred[4]{0:T(512)(128)(4,1)}, u32[]{:S(2)}) copy-start(pred[4]{0:T(512)(128)(4,1)} %get-tuple-element.48) | copy-start | bytes 16
  123.3 554.0 %copy-start.10 = (pred[4]{0:T(512)(128)(4,1)S(1)}, pred[4]{0:T(512)(128)(4,1)}, u32[]{:S(2)}) copy-start(pred[4]{0:T(512)(128)(4,1)} %get-tuple-element.125) | copy-start | bytes 16
Sparse Core Ops, SparseCore 0:
  33.3 633.2 all-reduce.2
where the time goes:
time: 689 us; the launch traced here: 688 us
  waiting for transfers between devices  557 us (81%)
  starting transfers between devices  44.4 us (6%)
  local copies, waits for them, and re-layouts  34.5 us (5%)
  other arithmetic  26.9 us (4%)
  between operations  16.1 us (2%)
  matrix products  9.06 us (1%)
    psum x1, waiting for transfers between devices, from_root(): return lax.psum(jnp.where(mine, array, jnp.zeros_like(array)), axis)  542 us
    all_to_all x3, starting transfers between devices, on_device(): lax.all_to_all(send_subs, 'tm', split_axis=0, concat_axis=0, tiled=True)  27.6 us
    all_to_all x3, starting transfers between devices, on_device(): lax.all_to_all(send_rows, 'tm', split_axis=0, concat_axis=0, tiled=True)  16.8 us
    another operation x4, other arithmetic  15.3 us
  transfers between devices with their start and end apart: 7, of which 6 were waited for; matrix products, arithmetic and copies ran while one was open for 7% of the time, Pallas kernels for 0%

commit v1 on v0

v1 whole, which is shorter than its diff:
```python
import jax
import jax.numpy as jnp
from jax import lax
from jax.experimental import pallas as pl
from jax.experimental.pallas import tpu as pltpu
from jax.sharding import PartitionSpec as P

SLOTS = 3
SIDE = 32
BLOCKS = 16
PEERS = 16
CAP = 2
SUBS = 4
STATIONS = 64
PER = SLOTS * CAP
Z_PART = 16
Y_PART = 4
ST_PIECE = STATIONS // Z_PART
REQS = 2 * SUBS
LANES = 128
F32 = jnp.float32
BF16 = jnp.bfloat16

OWNER = 0
SUB = OWNER + SLOTS * BLOCKS
COUNT = SUB + SLOTS * BLOCKS
PAIRS = COUNT + SLOTS * BLOCKS
ROOTS = PAIRS + REQS
OFFS = ROOTS + SLOTS
META = 16

COS_POLY = (1.0, -19.73920440673828, 64.93911743164062, -85.45014190673828, 60.167633056640625,
            -25.967601776123047, 6.528658866882324)
SIN_POLY = (6.283185005187988, -41.341590881347656, 81.59994506835938, -76.6144790649414,
            41.34288787841797, -12.471244812011719)


def smem():
    return pl.BlockSpec(memory_space=pltpu.SMEM)


def vmem():
    return pl.BlockSpec(memory_space=pltpu.VMEM)


def horner(x, poly):
    total = jnp.full_like(x, poly[-1])
    for coefficient in poly[-2::-1]:
        total = total * x + coefficient
    return total


def cis(turns):
    part = turns - jnp.floor(turns + 0.5)
    square = part * part
    return horner(square, COS_POLY), horner(square, SIN_POLY) * part


def times(a, b):
    return a[0] * b[0] - a[1] * b[1], a[0] * b[1] + a[1] * b[0]


def pack_kernel(ints, vis_ref, coord_ref, out_ref, taken):
    lane = lax.broadcasted_iota(jnp.int32, (1, LANES), 1)
    pairs = jnp.zeros((1, LANES), F32)
    for j in range(REQS):
        pairs = jnp.where(lane == META // 2 + j, ints[PAIRS + j].astype(F32), pairs)
    empty = jnp.concatenate([jnp.zeros((10, LANES), F32), pairs, jnp.zeros((5, LANES), F32)], axis=0)
    empty = empty.astype(BF16)

    @pl.loop(0, PEERS)
    def _(o):
        for k in range(PER):
            out_ref[o, k] = empty

    for slot in range(SLOTS):
        for o in range(PEERS):
            taken[o] = 0

        @pl.loop(0, BLOCKS)
        def _(i):
            spot = slot * BLOCKS + i
            owner = ints[OWNER + spot]
            rank = taken[owner]
            taken[owner] = rank + 1
            values = vis_ref[slot, 0, i].astype(F32)
            values = jnp.where(lane < ints[COUNT + spot], values, 0.0)
            meta = jnp.where(lane == 0, ints[SUB + spot].astype(F32), jnp.where(lane == 1, 1.0, pairs))
            rows = jnp.concatenate(
                [values, coord_ref[slot, 0, i].astype(F32), meta, jnp.zeros((5, LANES), F32)], axis=0
            )
            out_ref[owner, slot * CAP + rank] = rows.astype(BF16)


def pack(ints, visibility, coordinate, **kw):
    return pl.pallas_call(
        pack_kernel,
        out_shape=jax.ShapeDtypeStruct((PEERS, PER, 16, LANES), BF16),
        in_specs=[smem(), vmem(), vmem()],
        out_specs=vmem(),
        scratch_shapes=[pltpu.SMEM((PEERS,), jnp.int32)],
        name="pack_blocks",
        cost_estimate=pl.CostEstimate(flops=2000000, bytes_accessed=600000, transcendentals=0),
        **kw,
    )(ints, visibility, coordinate)


def block_transpose(rows):
    lane = lax.broadcasted_iota(jnp.int32, (8, LANES), 1)
    rows = list(rows)
    for bit in range(2):
        step = SIDE << bit
        upper = (lane & step) != 0
        for low in range(4):
            if low >> bit & 1:
                continue
            high = low | 1 << bit
            x, y = rows[low], rows[high]
            rows[low] = jnp.where(upper, pltpu.roll(y, step, 1), x)
            rows[high] = jnp.where(upper, y, pltpu.roll(x, LANES - step, 1))
    return rows


BATCH = 4


def grid_kernel(meta, ints, rows_ref, x_ref, acc, order, bucket):
    acc[...] = jnp.zeros_like(acc)

    def gather(t, carry):
        count, spare = carry
        for k in range(PER):
            b = t * PER + k
            sub = meta[b * META]
            live = meta[b * META + 1]
            order[count] = b
            bucket[count] = (k // CAP) * SUBS + sub
            spare = jnp.where(live == 0, b, spare)
            count = count + live
        return count, spare

    count, spare = lax.fori_loop(0, PEERS, gather, (jnp.int32(0), jnp.int32(0)))
    for j in range(BATCH):
        order[count + j] = spare
        bucket[count + j] = 0

    sublane = lax.broadcasted_iota(jnp.int32, (8, LANES), 0).astype(F32)
    seed_l = (sublane * 4.0 - 16.0) * (1.0 / SIDE)
    seed_m = (sublane - 16.0) * (1.0 / SIDE)

    @pl.loop(0, (count + (BATCH - 1)) // BATCH)
    def _(step):
        for j in range(BATCH):
            b = order[step * BATCH + j]
            key = bucket[step * BATCH + j]
            sub = key % SUBS
            tile = rows_ref[b].astype(F32)
            du = tile[8:9, :] - ints[OFFS + 2 * sub].astype(F32)
            dv = tile[9:10, :] - ints[OFFS + 2 * sub + 1].astype(F32)
            du = jnp.broadcast_to(du, (8, LANES))
            dv = jnp.broadcast_to(dv, (8, LANES))
            turn_l = cis(du * (1.0 / SIDE))
            turn_m = cis(dv * (8.0 / SIDE))
            current = cis(du * seed_l)
            cos_rows, sin_rows = [current[0]], [current[1]]
            for _ in range(3):
                current = times(current, turn_l)
                cos_rows.append(current[0])
                sin_rows.append(current[1])
            left = jnp.concatenate(cos_rows + sin_rows, axis=0).astype(BF16)
            phase = [cis(dv * seed_m)]
            for _ in range(3):
                phase.append(times(phase[-1], turn_m))
            real_rows, imag_rows = [], []
            for p in range(4):
                vis = tile[p:p + 1, :], tile[4 + p:5 + p, :]
                for m in range(4):
                    real, imag = times(vis, phase[m])
                    real_rows.append(real)
                    imag_rows.append(imag)
            right = jnp.concatenate(real_rows + imag_rows, axis=0).astype(BF16)
            acc[key] += lax.dot_general(
                left, right, (((1,), (1,)), ((), ())), preferred_element_type=F32
            )

    @pl.loop(0, SLOTS * SUBS)
    def _(key):
        upper = acc[key, 0:SIDE, :]
        lower = acc[key, SIDE:2 * SIDE, :]
        real = upper[:, :LANES] - lower[:, LANES:]
        imag = upper[:, LANES:] + lower[:, :LANES]
        for part, image in enumerate((real, imag)):
            for p, plane in enumerate(block_transpose([image[8 * b:8 * b + 8] for b in range(4)])):
                x_ref[key, 4 * part + p] = plane


def grid_blocks(meta, ints, rows, **kw):
    return pl.pallas_call(
        grid_kernel,
        out_shape=jax.ShapeDtypeStruct((SLOTS * SUBS, 8, 8, LANES), F32),
        in_specs=[smem(), smem(), vmem()],
        out_specs=vmem(),
        scratch_shapes=[
            pltpu.VMEM((SLOTS * SUBS, 2 * SIDE, 8 * SIDE), F32),
            pltpu.SMEM((PEERS * PER + BATCH,), jnp.int32),
            pltpu.SMEM((PEERS * PER + BATCH,), jnp.int32),
        ],
        name="grid_blocks",
        cost_estimate=pl.CostEstimate(flops=800000000, bytes_accessed=800000, transcendentals=0),
        **kw,
    )(meta, ints, rows)


def pick_z_kernel(ints, in_ref, out_ref):
    for s in range(SLOTS):
        piece = in_ref[ints[ROOTS + s] // Y_PART]
        for y in range(Y_PART):
            out_ref[y, s] = piece


def pick_z(ints, pieces, **kw):
    return pl.pallas_call(
        pick_z_kernel,
        out_shape=jax.ShapeDtypeStruct((Y_PART, SLOTS, 16, LANES), BF16),
        in_specs=[smem(), vmem()],
        out_specs=vmem(),
        name="pick_along_z",
        **kw,
    )(ints, pieces)


def pick_y_kernel(ints, in_ref, out_ref):
    pieces = [in_ref[ints[ROOTS + s] % Y_PART, s].astype(F32) for s in range(SLOTS)]
    rows = jnp.concatenate(
        [pieces[s][4 * i:4 * i + 4] for i in range(ST_PIECE) for s in range(SLOTS)], axis=0
    ).astype(BF16)
    for z in range(Z_PART):
        out_ref[z] = rows


def pick_y(ints, pieces, **kw):
    return pl.pallas_call(
        pick_y_kernel,
        out_shape=jax.ShapeDtypeStruct((Z_PART, ST_PIECE * SLOTS * 4, LANES), BF16),
        in_specs=[smem(), vmem()],
        out_specs=vmem(),
        name="pick_along_y",
        **kw,
    )(ints, pieces)


ROWS_ST = SLOTS * 4


def asked_kernel(meta, in_ref, out_ref, table, stage):
    for z in range(Z_PART):
        wide = in_ref[z].astype(F32)
        for i in range(ST_PIECE):
            table[z * ST_PIECE + i, 0:ROWS_ST, :] = wide[ROWS_ST * i:ROWS_ST * (i + 1)]

    @pl.loop(0, PEERS)
    def _(t):
        for r in range(REQS):
            station = meta[t * (PER * META) + META // 2 + r]
            stage[ROWS_ST * r:ROWS_ST * (r + 1), :] = table[station, 0:ROWS_ST, :]
        out_ref[t] = stage[...].astype(BF16)


def asked(meta, pieces, **kw):
    return pl.pallas_call(
        asked_kernel,
        out_shape=jax.ShapeDtypeStruct((PEERS, REQS * ROWS_ST, LANES), BF16),
        in_specs=[smem(), vmem()],
        out_specs=vmem(),
        scratch_shapes=[
            pltpu.VMEM((STATIONS, 16, LANES), F32),
            pltpu.VMEM((REQS * ROWS_ST, LANES), F32),
        ],
        name="asked_stations",
        cost_estimate=pl.CostEstimate(flops=1000000, bytes_accessed=600000, transcendentals=0),
        **kw,
    )(meta, pieces)


def screen_kernel(x_ref, in_ref, out_ref, wide, tmp):
    rows = REQS * ROWS_ST
    for t in range(PEERS):
        wide[rows * t:rows * (t + 1), :] = in_ref[t].astype(F32)

    def entry(request, slot, p, half):
        start = half * rows + request * ROWS_ST + slot * 4 + p
        return wide[pl.ds(start, 8, stride=2 * rows), :]

    def product(first, second):
        result = []
        for i in range(2):
            for j in range(2):
                one = times(first[2 * i], second[j])
                two = times(first[2 * i + 1], second[2 + j])
                result.append((one[0] + two[0], one[1] + two[1]))
        return result

    for sub in range(SUBS):
        total = None
        for slot in range(SLOTS):
            first = [(entry(2 * sub, slot, p, 0), entry(2 * sub, slot, p, 1)) for p in range(4)]
            second = [(entry(2 * sub + 1, slot, p, 0), -entry(2 * sub + 1, slot, p, 1)) for p in (0, 2, 1, 3)]
            key = slot * SUBS + sub
            image = [(x_ref[key, p], x_ref[key, 4 + p]) for p in range(4)]
            part = product(product(first, image), second)
            if total is None:
                total = part
            else:
                total = [(a[0] + b[0], a[1] + b[1]) for a, b in zip(total, part)]
        for p in range(4):
            tmp[8 * p:8 * p + 8, :] = total[p][0]
            tmp[32 + 8 * p:40 + 8 * p, :] = total[p][1]
        for a in range(8):
            out_ref[0, sub, :, LANES * a:LANES * (a + 1)] = tmp[pl.ds(a, 8, stride=8), :]


def screen_product(x, screens, **kw):
    return pl.pallas_call(
        screen_kernel,
        out_shape=jax.ShapeDtypeStruct((1, SUBS, 8, SIDE * SIDE), F32),
        in_specs=[vmem(), vmem()],
        out_specs=vmem(),
        scratch_shapes=[
            pltpu.VMEM((PEERS * REQS * ROWS_ST, LANES), F32),
            pltpu.VMEM((64, LANES), F32),
        ],
        name="screen_product",
        cost_estimate=pl.CostEstimate(flops=3000000, bytes_accessed=1000000, transcendentals=0),
        **kw,
    )(x, screens)


def pack_ints(block_count, owner_index, subgrid_index, offsets, station_pair, slot_owner):
    return jnp.concatenate([
        owner_index.reshape(-1), subgrid_index.reshape(-1), block_count.reshape(-1),
        station_pair.reshape(-1), slot_owner, offsets.reshape(-1),
    ])


def chunk_of(screens, t):
    part = lax.dynamic_slice(screens[0], (0, 4 * (t % 2), LANES * (t // 2)), (STATIONS, 4, LANES))
    return part.reshape(Z_PART, ST_PIECE * 4, LANES)


def meta_of(arrived):
    return arrived[:, :, 10, :META].astype(jnp.int32).reshape(-1)


def on_device(visibility, coordinate, block_count, owner_index, subgrid_index, offsets,
              station_pair, screens, slot_owner):
    z_groups = [[z * Y_PART + y for z in range(Z_PART)] for y in range(Y_PART)]
    y_groups = [[z * Y_PART + y for y in range(Y_PART)] for z in range(Z_PART)]

    def exchange(array, axis, groups=None):
        return lax.all_to_all(array, axis, 0, 0, axis_index_groups=groups, tiled=True)

    ints = pack_ints(block_count, owner_index, subgrid_index, offsets, station_pair, slot_owner)
    sent = pack(ints, visibility, coordinate)
    arrived = exchange(sent, "tm")
    meta = meta_of(arrived)
    pieces = exchange(chunk_of(screens, lax.axis_index("tm")), "uv", z_groups)
    pieces = exchange(pick_z(ints, pieces), "uv", y_groups)
    pieces = exchange(pick_y(ints, pieces), "uv", z_groups)
    x = grid_blocks(meta, ints, arrived.reshape(PEERS * PER, 16, LANES))
    wanted = exchange(asked(meta, pieces), "tm")
    return screen_product(x, wanted)


def solution(mesh):
    placed = (
        P(None, "uv", "tm", None, None),
        P(None, "uv", "tm", None, None),
        P(None, "uv", "tm"),
        P(None, "uv", "tm", None),
        P(None, "uv", "tm"),
        P("uv", "tm", None),
        P("uv", "tm", None),
        P("uv", None, None, None),
        P(),
    )
    return jax.shard_map(
        on_device, mesh=mesh, in_specs=placed, out_specs=P("uv", "tm", None, None), check_vma=False
    )
```

time: 689 us -> 107 us (0.16)
  the two profiles are of different devices: /device:TPU:6 before, /device:TPU:14 now
where the time goes in v1:
time: 107 us; the launch traced here: 106 us
  starting transfers between devices  41.9 us (39%)
  waiting for transfers between devices  33.6 us (31%)
  Pallas kernels  20.8 us (19%)
  local copies, waits for them, and re-layouts  9.54 us (9%)
    all_to_all x5, starting transfers between devices, exchange(): lax.all_to_all(array, axis, 0, 0, axis_index_groups=groups, tiled=True)  41.9 us
    all_to_all x5, waiting for transfers between devices, exchange(): lax.all_to_all(array, axis, 0, 0, axis_index_groups=groups, tiled=True)  33.6 us
    pallas_call x1, Pallas kernels, grid_blocks(): pl.pallas_call(grid_kernel, out_shape=jax.ShapeDtypeStruct((SLOTS * SUBS,...  11.2 us
    unnamed x26, local copies, waits for them, and re-layouts  7.04 us
    pallas_call x1, Pallas kernels, screen_product(): pl.pallas_call(screen_kernel, out_shape=jax.ShapeDtypeStruct((1, SUBS, 8,...  2.31 us
    pallas_call x1, Pallas kernels, pack(): pl.pallas_call(pack_kernel, out_shape=jax.ShapeDtypeStruct((PEERS, PER, 1...  2.24 us
  transfers between devices with their start and end apart: 5, of which 4 were waited for; matrix products, arithmetic and copies ran while one was open for 2% of the time, Pallas kernels for 14%

profile of v1, /device:TPU:14, one launch (start us, length us, event | category | flops | bytes accessed | tf_op | source)
XLA Modules:
  0.0 106.1 jit_solution(11758827322208526220)
XLA Ops:
  0.0 1.2 %copy-done = bf16[1,64,8,1024]{3,2,1,0:T(8,128)(2,1)S(1)} copy-done((bf16[1,64,8,1024]{3,2,1,0:T(8,128)(2,1)S(1)}, bf16[1,64,8,1024]{3,2,1,0:T(8,128)(2,1)}, u32[]{:S(2)}) %copy-start) | copy-done | bytes 1048600
  1.2 0.7 constant_dynamic-slice_fusion
  2.0 19.0 %all-to-all-start.1 = ((bf16[16,16,128]{2,1,0:T(8,128)(2,1)}), bf16[16,16,128]{2,1,0:T(8,128)(2,1)S(1)}, u32[]{:S(2)}, u32[]{:S(2)}) async-start(bf16[16,16,128]{2,1,0:T(8,128)(2,1)} %bitcast.1), calls=%async_computation.1 | async-start | bytes 131072 | tf_op jit(solution)/shard_map/all_to_all | solution.py:360
  21.8 0.6 copy-done.8
  24.6 0.7 concatenate.3.ints
  25.3 8.4 %all-to-all-done.1.in_ref = bf16[16,16,128]{2,1,0:T(8,128)(2,1)S(1)} async-done(((bf16[16,16,128]{2,1,0:T(8,128)(2,1)}), bf16[16,16,128]{2,1,0:T(8,128)(2,1)S(1)}, u32[]{:S(2)}, u32[]{:S(2)}) %all-to-all-start.1) | async-done | bytes 65568 | tf_op jit(solution)/shard_map/all_to_all | solution.py:360
  33.7 0.6 copy-done.4
  34.3 1.5 %pick_along_z.1 = bf16[4,3,16,128]{3,2,1,0:T(8,128)(2,1)} custom-call(s32[163]{0:T(256)} %concatenate.3.ints, bf16[16,16,128]{2,1,0:T(8,128)(2,1)} %copy-done.4), custom_call_target="tpu_custom_call" | custom-call | tf_op jit(solution)/shard_map/pick_along_z/pallas_call | solution.py:222
  35.8 6.2 %all-to-all-start.2 = ((bf16[4,3,16,128]{3,2,1,0:T(8,128)(2,1)}), bf16[4,3,16,128]{3,2,1,0:T(8,128)(2,1)S(1)}, u32[]{:S(2)}, u32[]{:S(2)}) async-start(bf16[4,3,16,128]{3,2,1,0:T(8,128)(2,1)} %pick_along_z.1), calls=%async_computation.2 | async-start | bytes 98304 | tf_op jit(solution)/shard_map/all_to_all | solution.py:360
  42.0 2.2 %pack_blocks.1 = bf16[16,6,16,128]{3,2,1,0:T(8,128)(2,1)} custom-call(s32[163]{0:T(256)} %concatenate.3.ints, bf16[3,1,16,8,128]{4,3,2,1,0:T(8,128)(2,1)} %vis_ref.1, bf16[3,1,16,2,128]{4,3,2,1,0:T(2,128)(2,1)} %coord_ref.1), custom_call_target="tpu_custom_call" | custom-call | flops 2000000 | bytes 600000 | tf_op jit(solution)/shard_map/pack_blocks/pallas_call | solution.py:96
  44.3 5.8 %all-to-all-done.2.in_ref = bf16[4,3,16,128]{3,2,1,0:T(8,128)(2,1)S(1)} async-done(((bf16[4,3,16,128]{3,2,1,0:T(8,128)(2,1)}), bf16[4,3,16,128]{3,2,1,0:T(8,128)(2,1)S(1)}, u32[]{:S(2)}, u32[]{:S(2)}) %all-to-all-start.2) | async-done | bytes 49184 | tf_op jit(solution)/shard_map/all_to_all | solution.py:360
  50.1 0.6 copy-done.5
  50.7 5.7 %all-to-all-start = ((bf16[16,6,16,128]{3,2,1,0:T(8,128)(2,1)}), bf16[16,6,16,128]{3,2,1,0:T(8,128)(2,1)S(1)}, u32[]{:S(2)}, u32[]{:S(2)}) async-start(bf16[16,6,16,128]{3,2,1,0:T(8,128)(2,1)} %pack_blocks.1), calls=%async_computation | async-start | bytes 786432 | tf_op jit(solution)/shard_map/all_to_all | solution.py:360
  56.4 1.5 %pick_along_y.1 = bf16[16,48,128]{2,1,0:T(8,128)(2,1)} custom-call(s32[163]{0:T(256)} %concatenate.3.ints, bf16[4,3,16,128]{3,2,1,0:T(8,128)(2,1)} %copy-done.5), custom_call_target="tpu_custom_call" | custom-call | tf_op jit(solution)/shard_map/pick_along_y/pallas_call | solution.py:242
  57.9 4.5 %all-to-all-done = bf16[16,6,16,128]{3,2,1,0:T(8,128)(2,1)S(1)} async-done(((bf16[16,6,16,128]{3,2,1,0:T(8,128)(2,1)}), bf16[16,6,16,128]{3,2,1,0:T(8,128)(2,1)S(1)}, u32[]{:S(2)}, u32[]{:S(2)}) %all-to-all-start) | async-done | bytes 393248 | tf_op jit(solution)/shard_map/all_to_all | solution.py:360
  62.4 3.6 %all-to-all-start.3 = ((bf16[16,48,128]{2,1,0:T(8,128)(2,1)}), bf16[16,48,128]{2,1,0:T(8,128)(2,1)S(1)}, u32[]{:S(2)}, u32[]{:S(2)}) async-start(bf16[16,48,128]{2,1,0:T(8,128)(2,1)} %pick_along_y.1), calls=%async_computation.3 | async-start | bytes 393216 | tf_op jit(solution)/shard_map/all_to_all | solution.py:360
  66.2 0.7 reshape.34.meta
  66.9 14.8 %all-to-all-done.3.in_ref = bf16[16,48,128]{2,1,0:T(8,128)(2,1)S(1)} async-done(((bf16[16,48,128]{2,1,0:T(8,128)(2,1)}), bf16[16,48,128]{2,1,0:T(8,128)(2,1)S(1)}, u32[]{:S(2)}, u32[]{:S(2)}) %all-to-all-start.3) | async-done | bytes 196640 | tf_op jit(solution)/shard_map/all_to_all | solution.py:360
  81.7 0.7 copy-done.2
  82.4 2.0 %asked_stations.1 = bf16[16,96,128]{2,1,0:T(8,128)(2,1)} custom-call(s32[1536]{0:T(1024)} %reshape.34.meta, bf16[16,48,128]{2,1,0:T(8,128)(2,1)} %copy-done.2), custom_call_target="tpu_custom_call" | custom-call | flops 1000000 | bytes 600000 | tf_op jit(solution)/shard_map/asked_stations/pallas_call | solution.py:270
  84.4 7.4 %all-to-all-start.4 = ((bf16[16,96,128]{2,1,0:T(8,128)(2,1)}), bf16[16,96,128]{2,1,0:T(8,128)(2,1)S(1)}, u32[]{:S(2)}, u32[]{:S(2)}) async-start(bf16[16,96,128]{2,1,0:T(8,128)(2,1)} %asked_stations.1), calls=%async_computation.4 | async-start | bytes 786432 | tf_op jit(solution)/shard_map/all_to_all | solution.py:360
  91.8 11.2 %grid_blocks.1.x_ref = f32[12,8,8,128]{3,2,1,0:T(8,128)} custom-call(s32[1536]{0:T(1024)} %reshape.34.meta, s32[163]{0:T(256)} %concatenate.3.ints, bf16[96,16,128]{2,1,0:T(8,128)(2,1)} %bitcast.2), custom_call_target="tpu_custom_call" | custom-call | flops 800000000 | bytes 800000 | tf_op jit(solution)/shard_map/grid_blocks/pallas_call | solution.py:198
  103.0 0.7 copy-done.1
  103.8 2.3 %screen_product.1 = f32[1,4,8,1024]{3,2,1,0:T(8,128)} custom-call(f32[12,8,8,128]{3,2,1,0:T(8,128)} %grid_blocks.1.x_ref, bf16[16,96,128]{2,1,0:T(8,128)(2,1)} %copy-done.1), custom_call_target="tpu_custom_call" | custom-call | flops 3000000 | bytes 1000000 | tf_op jit(solution)/shard_map/screen_product/pallas_call | solution.py:323
  (30 shorter events, 3.2 us)
Async XLA Ops:
  0.0 1.2 %copy-start = (bf16[1,64,8,1024]{3,2,1,0:T(8,128)(2,1)S(1)}, bf16[1,64,8,1024]{3,2,1,0:T(8,128)(2,1)}, u32[]{:S(2)}) copy-start(bf16[1,64,8,1024]{3,2,1,0:T(8,128)(2,1)} %param.16) | copy-start | bytes 3145732
  2.0 19.0 %copy-start.6 = (s32[3,1,16]{2,1,0:T(1,128)S(1)}, s32[3,1,16]{2,1,0:T(1,128)}, u32[]{:S(2)}) copy-start(s32[3,1,16]{2,1,0:T(1,128)} %param.11) | copy-start | bytes 580
  2.0 31.7 %all-to-all-start.1 = ((bf16[16,16,128]{2,1,0:T(8,128)(2,1)}), bf16[16,16,128]{2,1,0:T(8,128)(2,1)S(1)}, u32[]{:S(2)}, u32[]{:S(2)}) async-start(bf16[16,16,128]{2,1,0:T(8,128)(2,1)} %bitcast.1), calls=%async_computation.1 | async-start | bytes 131072 | tf_op jit(solution)/shard_map/all_to_all | solution.py:360
  21.0 0.7 copy-start.7
  21.7 0.7 copy-start.8
  22.4 0.7 copy-start.9
  23.2 0.7 copy-start.10
  24.0 0.7 copy-start.11
  33.7 0.6 copy-start.4
  35.8 14.3 %all-to-all-start.2 = ((bf16[4,3,16,128]{3,2,1,0:T(8,128)(2,1)}), bf16[4,3,16,128]{3,2,1,0:T(8,128)(2,1)S(1)}, u32[]{:S(2)}, u32[]{:S(2)}) async-start(bf16[4,3,16,128]{3,2,1,0:T(8,128)(2,1)} %pick_along_z.1), calls=%async_computation.2 | async-start | bytes 98304 | tf_op jit(solution)/shard_map/all_to_all | solution.py:360
  50.1 0.6 copy-start.5
  50.7 11.7 %all-to-all-start = ((bf16[16,6,16,128]{3,2,1,0:T(8,128)(2,1)}), bf16[16,6,16,128]{3,2,1,0:T(8,128)(2,1)S(1)}, u32[]{:S(2)}, u32[]{:S(2)}) async-start(bf16[16,6,16,128]{3,2,1,0:T(8,128)(2,1)} %pack_blocks.1), calls=%async_computation | async-start | bytes 786432 | tf_op jit(solution)/shard_map/all_to_all | solution.py:360
  62.4 22.0 %copy-start.3 = (bf16[16,6,16,128]{3,2,1,0:T(8,128)(2,1)}, bf16[16,6,16,128]{3,2,1,0:T(8,128)(2,1)S(1)}, u32[]{:S(2)}) copy-start(bf16[16,6,16,128]{3,2,1,0:T(8,128)(2,1)S(1)} %all-to-all-done) | copy-start | bytes 1179652
  62.4 19.3 %all-to-all-start.3 = ((bf16[16,48,128]{2,1,0:T(8,128)(2,1)}), bf16[16,48,128]{2,1,0:T(8,128)(2,1)S(1)}, u32[]{:S(2)}, u32[]{:S(2)}) async-start(bf16[16,48,128]{2,1,0:T(8,128)(2,1)} %pick_along_y.1), calls=%async_computation.3 | async-start | bytes 393216 | tf_op jit(solution)/shard_map/all_to_all | solution.py:360
  81.7 0.7 copy-start.2
  84.4 18.6 %all-to-all-start.4 = ((bf16[16,96,128]{2,1,0:T(8,128)(2,1)}), bf16[16,96,128]{2,1,0:T(8,128)(2,1)S(1)}, u32[]{:S(2)}, u32[]{:S(2)}) async-start(bf16[16,96,128]{2,1,0:T(8,128)(2,1)} %asked_stations.1), calls=%async_computation.4 | async-start | bytes 786432 | tf_op jit(solution)/shard_map/all_to_all | solution.py:360
  103.0 0.7 copy-start.1

commit v2 on v1

--- a/solution.py
+++ b/solution.py
@@ -15,6 +15,7 @@
 PER = SLOTS * CAP
 Z_PART = 16
 Y_PART = 4
+NDEV = Z_PART * Y_PART
 ST_PIECE = STATIONS // Z_PART
 REQS = 2 * SUBS
 LANES = 128
@@ -26,7 +27,8 @@
 COUNT = SUB + SLOTS * BLOCKS
 PAIRS = COUNT + SLOTS * BLOCKS
 ROOTS = PAIRS + REQS
-OFFS = ROOTS + SLOTS
+ME = ROOTS + SLOTS
+OFFS = ME + 1
 META = 16
 
 COS_POLY = (1.0, -19.73920440673828, 64.93911743164062, -85.45014190673828, 60.167633056640625,
@@ -41,6 +43,10 @@
 
 def vmem():
     return pl.BlockSpec(memory_space=pltpu.VMEM)
+
+
+def room():
+    return pltpu.CompilerParams(vmem_limit_bytes=8 * 1024 * 1024)
 
 
 def horner(x, poly):
@@ -101,6 +107,7 @@
         scratch_shapes=[pltpu.SMEM((PEERS,), jnp.int32)],
         name="pack_blocks",
         cost_estimate=pl.CostEstimate(flops=2000000, bytes_accessed=600000, transcendentals=0),
+        compiler_params=room(),
         **kw,
     )(ints, visibility, coordinate)
 
@@ -207,30 +214,37 @@
         ],
         name="grid_blocks",
         cost_estimate=pl.CostEstimate(flops=800000000, bytes_accessed=800000, transcendentals=0),
+        compiler_params=room(),
         **kw,
     )(meta, ints, rows)
 
 
 def pick_z_kernel(ints, in_ref, out_ref):
     for s in range(SLOTS):
-        piece = in_ref[ints[ROOTS + s] // Y_PART]
-        for y in range(Y_PART):
-            out_ref[y, s] = piece
+        out_ref[s] = in_ref[ints[ROOTS + s] // Y_PART]
 
 
 def pick_z(ints, pieces, **kw):
     return pl.pallas_call(
         pick_z_kernel,
-        out_shape=jax.ShapeDtypeStruct((Y_PART, SLOTS, 16, LANES), BF16),
+        out_shape=jax.ShapeDtypeStruct((SLOTS, 16, LANES), BF16),
         in_specs=[smem(), vmem()],
         out_specs=vmem(),
         name="pick_along_z",
+        compiler_params=room(),
         **kw,
     )(ints, pieces)
 
 
-def pick_y_kernel(ints, in_ref, out_ref):
-    pieces = [in_ref[ints[ROOTS + s] % Y_PART, s].astype(F32) for s in range(SLOTS)]
+def pick_y_kernel(ints, *refs):
+    out_ref = refs[Y_PART]
+    pieces = []
+    for s in range(SLOTS):
+        shift = (ints[ME] - ints[ROOTS + s] + NDEV) % Y_PART
+        piece = refs[0][s].astype(F32)
+        for y in range(1, Y_PART):
+            piece = jnp.where(shift == y, refs[y][s].astype(F32), piece)
+        pieces.append(piece)
     rows = jnp.concatenate(
         [pieces[s][4 * i:4 * i + 4] for i in range(ST_PIECE) for s in range(SLOTS)], axis=0
     ).astype(BF16)
@@ -242,11 +256,12 @@
     return pl.pallas_call(
         pick_y_kernel,
         out_shape=jax.ShapeDtypeStruct((Z_PART, ST_PIECE * SLOTS * 4, LANES), BF16),
-        in_specs=[smem(), vmem()],
+        in_specs=[smem()] + [vmem()] * Y_PART,
         out_specs=vmem(),
         name="pick_along_y",
-        **kw,
-    )(ints, pieces)
+        compiler_params=room(),
+        **kw,
+    )(ints, *pieces)
 
 
 ROWS_ST = SLOTS * 4
@@ -278,6 +293,7 @@
         ],
         name="asked_stations",
         cost_estimate=pl.CostEstimate(flops=1000000, bytes_accessed=600000, transcendentals=0),
+        compiler_params=room(),
         **kw,
     )(meta, pieces)
 
@@ -331,14 +347,15 @@
         ],
         name="screen_product",
         cost_estimate=pl.CostEstimate(flops=3000000, bytes_accessed=1000000, transcendentals=0),
+        compiler_params=room(),
         **kw,
     )(x, screens)
 
 
-def pack_ints(block_count, owner_index, subgrid_index, offsets, station_pair, slot_owner):
+def pack_ints(block_count, owner_index, subgrid_index, offsets, station_pair, slot_owner, me):
     return jnp.concatenate([
         owner_index.reshape(-1), subgrid_index.reshape(-1), block_count.reshape(-1),
-        station_pair.reshape(-1), slot_owner, offsets.reshape(-1),
+        station_pair.reshape(-1), slot_owner, me.reshape(-1), offsets.reshape(-1),
     ])
 
 
@@ -354,17 +371,22 @@
 def on_device(visibility, coordinate, block_count, owner_index, subgrid_index, offsets,
               station_pair, screens, slot_owner):
     z_groups = [[z * Y_PART + y for z in range(Z_PART)] for y in range(Y_PART)]
-    y_groups = [[z * Y_PART + y for y in range(Y_PART)] for z in range(Z_PART)]
+    y_shifts = [
+        [(z * Y_PART + y, z * Y_PART + (y + shift) % Y_PART) for z in range(Z_PART) for y in range(Y_PART)]
+        for shift in range(1, Y_PART)
+    ]
 
     def exchange(array, axis, groups=None):
         return lax.all_to_all(array, axis, 0, 0, axis_index_groups=groups, tiled=True)
 
-    ints = pack_ints(block_count, owner_index, subgrid_index, offsets, station_pair, slot_owner)
+    ints = pack_ints(block_count, owner_index, subgrid_index, offsets, station_pair, slot_owner,
+                     lax.axis_index("uv"))
     sent = pack(ints, visibility, coordinate)
     arrived = exchange(sent, "tm")
     meta = meta_of(arrived)
     pieces = exchange(chunk_of(screens, lax.axis_index("tm")), "uv", z_groups)
-    pieces = exchange(pick_z(ints, pieces), "uv", y_groups)
+    piece = pick_z(ints, pieces)
+    pieces = [piece] + [lax.ppermute(piece, "uv", shift) for shift in y_shifts]
     pieces = exchange(pick_y(ints, pieces), "uv", z_groups)
     x = grid_blocks(meta, ints, arrived.reshape(PEERS * PER, 16, LANES))
     wanted = exchange(asked(meta, pieces), "tm")

time: 107 us -> 98.5 us (0.921)
  the two profiles are of different devices: /device:TPU:14 before, /device:TPU:1 now
where the time goes in v2:
time: 98.5 us; the launch traced here: 96.6 us
  starting transfers between devices  54.4 us (55%)
  waiting for transfers between devices  24.8 us (25%)
  Pallas kernels  12.6 us (13%)
  local copies, waits for them, and re-layouts  4.6 us (5%)
    all_to_all x4, starting transfers between devices, exchange(): lax.all_to_all(array, axis, 0, 0, axis_index_groups=groups, tiled=True)  41.6 us
    all_to_all x4, waiting for transfers between devices, exchange(): lax.all_to_all(array, axis, 0, 0, axis_index_groups=groups, tiled=True)  21.5 us
    ppermute x3, starting transfers between devices, on_device(): pieces = [piece] + [lax.ppermute(piece, 'uv', shift) for shift in y_shifts]  12.8 us
    pallas_call x1, Pallas kernels, grid_blocks(): pl.pallas_call(grid_kernel, out_shape=jax.ShapeDtypeStruct((SLOTS * SUBS,...  5.92 us
    unnamed x20, local copies, waits for them, and re-layouts  3.27 us
    ppermute x3, waiting for transfers between devices, on_device(): pieces = [piece] + [lax.ppermute(piece, 'uv', shift) for shift in y_shifts]  3.21 us
  transfers between devices with their start and end apart: 7, of which 5 were waited for; matrix products, arithmetic and copies ran while one was open for 1% of the time, Pallas kernels for 10%

profile of v2, /device:TPU:1, one launch (start us, length us, event | category | flops | bytes accessed | tf_op | source)
XLA Modules:
  0.0 96.6 jit_solution(8241472937719484501)
XLA Ops:
  0.0 1.2 %copy-done = bf16[1,64,8,1024]{3,2,1,0:T(8,128)(2,1)S(1)} copy-done((bf16[1,64,8,1024]{3,2,1,0:T(8,128)(2,1)S(1)}, bf16[1,64,8,1024]{3,2,1,0:T(8,128)(2,1)}, u32[]{:S(2)}) %copy-start) | copy-done | bytes 1048600
  1.2 0.7 constant_dynamic-slice_fusion
  2.0 19.6 %all-to-all-start.1 = ((bf16[16,16,128]{2,1,0:T(8,128)(2,1)}), bf16[16,16,128]{2,1,0:T(8,128)(2,1)S(1)}, u32[]{:S(2)}, u32[]{:S(2)}) async-start(bf16[16,16,128]{2,1,0:T(8,128)(2,1)} %bitcast.2), calls=%async_computation.1 | async-start | bytes 131072 | tf_op jit(solution)/shard_map/all_to_all | solution.py:380
  21.9 0.6 copy-done.6
  22.7 0.6 copy-done.7
  23.4 0.7 copy-done.8
  24.2 1.9 %pack_blocks.1 = bf16[16,6,16,128]{3,2,1,0:T(8,128)(2,1)} custom-call(s32[164]{0:T(256)S(1)} %concatenate.3.ints, bf16[3,1,16,8,128]{4,3,2,1,0:T(8,128)(2,1)S(1)} %copy-done.1, bf16[3,1,16,2,128]{4,3,2,1,0:T(2,128)(2,1)S(1)} %copy-done.2), custom_call_target="tpu_custom_call" | custom-call | flops 2000000 | bytes 600000 | tf_op jit(solution)/shard_map/pack_blocks/pallas_call | solution.py:102
  26.1 7.0 %all-to-all-done.1.in_ref = bf16[16,16,128]{2,1,0:T(8,128)(2,1)S(1)} async-done(((bf16[16,16,128]{2,1,0:T(8,128)(2,1)}), bf16[16,16,128]{2,1,0:T(8,128)(2,1)S(1)}, u32[]{:S(2)}, u32[]{:S(2)}) %all-to-all-start.1) | async-done | bytes 65568 | tf_op jit(solution)/shard_map/all_to_all | solution.py:380
  33.1 7.4 %all-to-all-start = ((bf16[16,6,16,128]{3,2,1,0:T(8,128)(2,1)}), bf16[16,6,16,128]{3,2,1,0:T(8,128)(2,1)S(1)}, u32[]{:S(2)}, u32[]{:S(2)}) async-start(bf16[16,6,16,128]{3,2,1,0:T(8,128)(2,1)} %pack_blocks.1), calls=%async_computation | async-start | bytes 786432 | tf_op jit(solution)/shard_map/all_to_all | solution.py:380
  40.6 0.6 pick_along_z.1.refs_0_
  41.1 5.0 %collective-permute-start.2 = (bf16[3,16,128]{2,1,0:T(8,128)(2,1)S(1)}, bf16[3,16,128]{2,1,0:T(8,128)(2,1)S(1)}, u32[]{:S(2)}, u32[]{:S(2)}) collective-permute-start(bf16[3,16,128]{2,1,0:T(8,128)(2,1)S(1)} %pick_along_z.1.refs_0_), channel_id=1, source_target_pairs={{0,48},{16,0},{32,16},{48,32},{64,112},{80,64},{96,80},{112,96},{1... | collective-permute-start | bytes 36872 | tf_op jit(solution)/shard_map/ppermute | solution.py:389
  46.1 4.4 %collective-permute-start.1 = (bf16[3,16,128]{2,1,0:T(8,128)(2,1)S(1)}, bf16[3,16,128]{2,1,0:T(8,128)(2,1)S(1)}, u32[]{:S(2)}, u32[]{:S(2)}) collective-permute-start(bf16[3,16,128]{2,1,0:T(8,128)(2,1)S(1)} %pick_along_z.1.refs_0_), channel_id=1, source_target_pairs={{0,32},{16,48},{32,0},{48,16},{64,96},{80,112},{96,64},{112,80},{1... | collective-permute-start | bytes 36872 | tf_op jit(solution)/shard_map/ppermute | solution.py:389
  50.6 3.3 %collective-permute-start = (bf16[3,16,128]{2,1,0:T(8,128)(2,1)S(1)}, bf16[3,16,128]{2,1,0:T(8,128)(2,1)S(1)}, u32[]{:S(2)}, u32[]{:S(2)}) collective-permute-start(bf16[3,16,128]{2,1,0:T(8,128)(2,1)S(1)} %pick_along_z.1.refs_0_), channel_id=1, source_target_pairs={{0,16},{16,32},{32,48},{48,0},{64,80},{80,96},{96,112},{112,64},{1... | collective-permute-start | bytes 36872 | tf_op jit(solution)/shard_map/ppermute | solution.py:389
  53.9 0.6 collective-permute-done.1.refs_2_
  54.5 2.6 %collective-permute-done.refs_1_ = bf16[3,16,128]{2,1,0:T(8,128)(2,1)S(1)} collective-permute-done((bf16[3,16,128]{2,1,0:T(8,128)(2,1)S(1)}, bf16[3,16,128]{2,1,0:T(8,128)(2,1)S(1)}, u32[]{:S(2)}, u32[]{:S(2)}) %collective-permute-start) | collective-permute-done | bytes 12320 | tf_op jit(solution)/shard_map/ppermute | solution.py:389
  57.1 1.3 %pick_along_y.1 = bf16[16,48,128]{2,1,0:T(8,128)(2,1)} custom-call(s32[164]{0:T(256)S(1)} %concatenate.3.ints, bf16[3,16,128]{2,1,0:T(8,128)(2,1)S(1)} %pick_along_z.1.refs_0_, bf16[3,16,128]{2,1,0:T(8,128)(2,1)S(1)} %collective-permute-done.refs_1_, bf16[3,16,128]{2,1,0:T(8,128)(2,1)S(1)} %collective-permute-done.1.refs_2_, ...), custom_call_target="tpu_custom_call" | custom-call | tf_op jit(solution)/shard_map/pick_along_y/pallas_call | solution.py:256
  58.4 3.6 %all-to-all-start.2 = ((bf16[16,48,128]{2,1,0:T(8,128)(2,1)}), bf16[16,48,128]{2,1,0:T(8,128)(2,1)S(1)}, u32[]{:S(2)}, u32[]{:S(2)}) async-start(bf16[16,48,128]{2,1,0:T(8,128)(2,1)} %pick_along_y.1), calls=%async_computation.2 | async-start | bytes 393216 | tf_op jit(solution)/shard_map/all_to_all | solution.py:380
  62.0 0.2 fusion
  62.2 12.1 %all-to-all-done.2.in_ref = bf16[16,48,128]{2,1,0:T(8,128)(2,1)S(1)} async-done(((bf16[16,48,128]{2,1,0:T(8,128)(2,1)}), bf16[16,48,128]{2,1,0:T(8,128)(2,1)S(1)}, u32[]{:S(2)}, u32[]{:S(2)}) %all-to-all-start.2) | async-done | bytes 196640 | tf_op jit(solution)/shard_map/all_to_all | solution.py:380
  74.3 1.7 %asked_stations.1 = bf16[16,96,128]{2,1,0:T(8,128)(2,1)} custom-call(s32[1536]{0:T(1024)S(1)} %reshape.38.meta, bf16[16,48,128]{2,1,0:T(8,128)(2,1)S(1)} %all-to-all-done.2.in_ref), custom_call_target="tpu_custom_call" | custom-call | flops 1000000 | bytes 600000 | tf_op jit(solution)/shard_map/asked_stations/pallas_call | solution.py:285
  76.0 11.0 %all-to-all-start.3 = ((bf16[16,96,128]{2,1,0:T(8,128)(2,1)}), bf16[16,96,128]{2,1,0:T(8,128)(2,1)S(1)}, u32[]{:S(2)}, u32[]{:S(2)}) async-start(bf16[16,96,128]{2,1,0:T(8,128)(2,1)} %asked_stations.1), calls=%async_computation.3 | async-start | bytes 786432 | tf_op jit(solution)/shard_map/all_to_all | solution.py:380
  87.1 5.9 %grid_blocks.1.x_ref = f32[12,8,8,128]{3,2,1,0:T(8,128)S(1)} custom-call(s32[1536]{0:T(1024)S(1)} %reshape.38.meta, s32[164]{0:T(256)S(1)} %concatenate.3.ints, bf16[96,16,128]{2,1,0:T(8,128)(2,1)S(1)} %bitcast.3), custom_call_target="tpu_custom_call" | custom-call | flops 800000000 | bytes 800000 | tf_op jit(solution)/shard_map/grid_blocks/pallas_call | solution.py:205
  93.0 2.5 %all-to-all-done.3.in_ref = bf16[16,96,128]{2,1,0:T(8,128)(2,1)S(1)} async-done(((bf16[16,96,128]{2,1,0:T(8,128)(2,1)}), bf16[16,96,128]{2,1,0:T(8,128)(2,1)S(1)}, u32[]{:S(2)}, u32[]{:S(2)}) %all-to-all-start.3) | async-done | bytes 393248 | tf_op jit(solution)/shard_map/all_to_all | solution.py:380
  95.4 1.2 %screen_product.1 = f32[1,4,8,1024]{3,2,1,0:T(8,128)} custom-call(f32[12,8,8,128]{3,2,1,0:T(8,128)S(1)} %grid_blocks.1.x_ref, bf16[16,96,128]{2,1,0:T(8,128)(2,1)S(1)} %all-to-all-done.3.in_ref), custom_call_target="tpu_custom_call" | custom-call | flops 3000000 | bytes 1000000 | tf_op jit(solution)/shard_map/screen_product/pallas_call | solution.py:339
  (28 shorter events, 0.9 us)
Async XLA Ops:
  0.0 1.2 %copy-start = (bf16[1,64,8,1024]{3,2,1,0:T(8,128)(2,1)S(1)}, bf16[1,64,8,1024]{3,2,1,0:T(8,128)(2,1)}, u32[]{:S(2)}) copy-start(bf16[1,64,8,1024]{3,2,1,0:T(8,128)(2,1)} %param.16) | copy-start | bytes 3145732
  2.0 22.2 %copy-start.1 = (bf16[3,1,16,8,128]{4,3,2,1,0:T(8,128)(2,1)S(1)}, bf16[3,1,16,8,128]{4,3,2,1,0:T(8,128)(2,1)}, u32[]{:S(2)}) copy-start(bf16[3,1,16,8,128]{4,3,2,1,0:T(8,128)(2,1)} %vis_ref.1) | copy-start | bytes 294916
  2.0 19.6 %copy-start.3 = (s32[3,1,16]{2,1,0:T(1,128)S(1)}, s32[3,1,16]{2,1,0:T(1,128)}, u32[]{:S(2)}) copy-start(s32[3,1,16]{2,1,0:T(1,128)} %param.11) | copy-start | bytes 580
  2.0 19.7 %copy-start.4 = (s32[3,1,16,1]{2,3,1,0:T(1,128)S(1)}, s32[3,1,16,1]{2,3,1,0:T(1,128)}, u32[]{:S(2)}) copy-start(s32[3,1,16,1]{2,3,1,0:T(1,128)} %param.12) | copy-start | bytes 580
  2.0 19.8 %copy-start.5 = (s32[3,1,16]{2,1,0:T(1,128)S(1)}, s32[3,1,16]{2,1,0:T(1,128)}, u32[]{:S(2)}) copy-start(s32[3,1,16]{2,1,0:T(1,128)} %param.13) | copy-start | bytes 580
  2.0 31.1 %all-to-all-start.1 = ((bf16[16,16,128]{2,1,0:T(8,128)(2,1)}), bf16[16,16,128]{2,1,0:T(8,128)(2,1)S(1)}, u32[]{:S(2)}, u32[]{:S(2)}) async-start(bf16[16,16,128]{2,1,0:T(8,128)(2,1)} %bitcast.2), calls=%async_computation.1 | async-start | bytes 131072 | tf_op jit(solution)/shard_map/all_to_all | solution.py:380
  21.5 2.6 %copy-start.2 = (bf16[3,1,16,2,128]{4,3,2,1,0:T(2,128)(2,1)S(1)}, bf16[3,1,16,2,128]{4,3,2,1,0:T(2,128)(2,1)}, u32[]{:S(2)}) copy-start(bf16[3,1,16,2,128]{4,3,2,1,0:T(2,128)(2,1)} %coord_ref.1) | copy-start | bytes 73732
  21.8 0.7 copy-start.6
  22.6 0.7 copy-start.7
  23.4 0.7 copy-start.8
  33.1 25.3 %all-to-all-start = ((bf16[16,6,16,128]{3,2,1,0:T(8,128)(2,1)}), bf16[16,6,16,128]{3,2,1,0:T(8,128)(2,1)S(1)}, u32[]{:S(2)}, u32[]{:S(2)}) async-start(bf16[16,6,16,128]{3,2,1,0:T(8,128)(2,1)} %pack_blocks.1), calls=%async_computation | async-start | bytes 786432 | tf_op jit(solution)/shard_map/all_to_all | solution.py:380
  41.1 12.8 %collective-permute-start.2 = (bf16[3,16,128]{2,1,0:T(8,128)(2,1)S(1)}, bf16[3,16,128]{2,1,0:T(8,128)(2,1)S(1)}, u32[]{:S(2)}, u32[]{:S(2)}) collective-permute-start(bf16[3,16,128]{2,1,0:T(8,128)(2,1)S(1)} %pick_along_z.1.refs_0_), channel_id=1, source_target_pairs={{0,48},{16,0},{32,16},{48,32},{64,112},{80,64},{96,80},{112,96},{1... | collective-permute-start | bytes 36872 | tf_op jit(solution)/shard_map/ppermute | solution.py:389
  46.1 8.3 %collective-permute-start.1 = (bf16[3,16,128]{2,1,0:T(8,128)(2,1)S(1)}, bf16[3,16,128]{2,1,0:T(8,128)(2,1)S(1)}, u32[]{:S(2)}, u32[]{:S(2)}) collective-permute-start(bf16[3,16,128]{2,1,0:T(8,128)(2,1)S(1)} %pick_along_z.1.refs_0_), channel_id=1, source_target_pairs={{0,32},{16,48},{32,0},{48,16},{64,96},{80,112},{96,64},{112,80},{1... | collective-permute-start | bytes 36872 | tf_op jit(solution)/shard_map/ppermute | solution.py:389
  50.6 6.5 %collective-permute-start = (bf16[3,16,128]{2,1,0:T(8,128)(2,1)S(1)}, bf16[3,16,128]{2,1,0:T(8,128)(2,1)S(1)}, u32[]{:S(2)}, u32[]{:S(2)}) collective-permute-start(bf16[3,16,128]{2,1,0:T(8,128)(2,1)S(1)} %pick_along_z.1.refs_0_), channel_id=1, source_target_pairs={{0,16},{16,32},{32,48},{48,0},{64,80},{80,96},{96,112},{112,64},{1... | collective-permute-start | bytes 36872 | tf_op jit(solution)/shard_map/ppermute | solution.py:389
  58.4 15.9 %all-to-all-start.2 = ((bf16[16,48,128]{2,1,0:T(8,128)(2,1)}), bf16[16,48,128]{2,1,0:T(8,128)(2,1)S(1)}, u32[]{:S(2)}, u32[]{:S(2)}) async-start(bf16[16,48,128]{2,1,0:T(8,128)(2,1)} %pick_along_y.1), calls=%async_computation.2 | async-start | bytes 393216 | tf_op jit(solution)/shard_map/all_to_all | solution.py:380
  76.0 19.4 %all-to-all-start.3 = ((bf16[16,96,128]{2,1,0:T(8,128)(2,1)}), bf16[16,96,128]{2,1,0:T(8,128)(2,1)S(1)}, u32[]{:S(2)}, u32[]{:S(2)}) async-start(bf16[16,96,128]{2,1,0:T(8,128)(2,1)} %asked_stations.1), calls=%async_computation.3 | async-start | bytes 786432 | tf_op jit(solution)/shard_map/all_to_all | solution.py:380

commit v3 on v2

--- a/solution.py
+++ b/solution.py
@@ -13,10 +13,10 @@
 SUBS = 4
 STATIONS = 64
 PER = SLOTS * CAP
-Z_PART = 16
-Y_PART = 4
-NDEV = Z_PART * Y_PART
-ST_PIECE = STATIONS // Z_PART
+NEAR = 16
+FAR = 4
+NDEV = NEAR * FAR
+ST_PIECE = STATIONS // NEAR
 REQS = 2 * SUBS
 LANES = 128
 F32 = jnp.float32
@@ -219,46 +219,45 @@
     )(meta, ints, rows)
 
 
-def pick_z_kernel(ints, in_ref, out_ref):
+def pick_near_kernel(ints, in_ref, out_ref):
     for s in range(SLOTS):
-        out_ref[s] = in_ref[ints[ROOTS + s] // Y_PART]
-
-
-def pick_z(ints, pieces, **kw):
-    return pl.pallas_call(
-        pick_z_kernel,
+        out_ref[s] = in_ref[ints[ROOTS + s] % NEAR]
+
+
+def pick_near(ints, pieces, **kw):
+    return pl.pallas_call(
+        pick_near_kernel,
         out_shape=jax.ShapeDtypeStruct((SLOTS, 16, LANES), BF16),
         in_specs=[smem(), vmem()],
         out_specs=vmem(),
-        name="pick_along_z",
+        name="pick_near",
         compiler_params=room(),
         **kw,
     )(ints, pieces)
 
 
-def pick_y_kernel(ints, *refs):
-    out_ref = refs[Y_PART]
+def pick_far_kernel(ints, *refs):
+    both_ref, later_ref, out_ref = refs
     pieces = []
     for s in range(SLOTS):
-        shift = (ints[ME] - ints[ROOTS + s] + NDEV) % Y_PART
-        piece = refs[0][s].astype(F32)
-        for y in range(1, Y_PART):
-            piece = jnp.where(shift == y, refs[y][s].astype(F32), piece)
+        shift = (ints[ME] // NEAR - ints[ROOTS + s] // NEAR + FAR) % FAR
+        k = shift % 2 * SLOTS + s
+        piece = jnp.where(shift < 2, both_ref[k].astype(F32), later_ref[k].astype(F32))
         pieces.append(piece)
     rows = jnp.concatenate(
         [pieces[s][4 * i:4 * i + 4] for i in range(ST_PIECE) for s in range(SLOTS)], axis=0
     ).astype(BF16)
-    for z in range(Z_PART):
+    for z in range(NEAR):
         out_ref[z] = rows
 
 
-def pick_y(ints, pieces, **kw):
-    return pl.pallas_call(
-        pick_y_kernel,
-        out_shape=jax.ShapeDtypeStruct((Z_PART, ST_PIECE * SLOTS * 4, LANES), BF16),
-        in_specs=[smem()] + [vmem()] * Y_PART,
-        out_specs=vmem(),
-        name="pick_along_y",
+def pick_far(ints, pieces, **kw):
+    return pl.pallas_call(
+        pick_far_kernel,
+        out_shape=jax.ShapeDtypeStruct((NEAR, ST_PIECE * SLOTS * 4, LANES), BF16),
+        in_specs=[smem(), vmem(), vmem()],
+        out_specs=vmem(),
+        name="pick_far",
         compiler_params=room(),
         **kw,
     )(ints, *pieces)
@@ -268,7 +267,7 @@
 
 
 def asked_kernel(meta, in_ref, out_ref, table, stage):
-    for z in range(Z_PART):
+    for z in range(NEAR):
         wide = in_ref[z].astype(F32)
         for i in range(ST_PIECE):
             table[z * ST_PIECE + i, 0:ROWS_ST, :] = wide[ROWS_ST * i:ROWS_ST * (i + 1)]
@@ -361,7 +360,7 @@
 
 def chunk_of(screens, t):
     part = lax.dynamic_slice(screens[0], (0, 4 * (t % 2), LANES * (t // 2)), (STATIONS, 4, LANES))
-    return part.reshape(Z_PART, ST_PIECE * 4, LANES)
+    return part.reshape(NEAR, ST_PIECE * 4, LANES)
 
 
 def meta_of(arrived):
@@ -370,10 +369,10 @@
 
 def on_device(visibility, coordinate, block_count, owner_index, subgrid_index, offsets,
               station_pair, screens, slot_owner):
-    z_groups = [[z * Y_PART + y for z in range(Z_PART)] for y in range(Y_PART)]
-    y_shifts = [
-        [(z * Y_PART + y, z * Y_PART + (y + shift) % Y_PART) for z in range(Z_PART) for y in range(Y_PART)]
-        for shift in range(1, Y_PART)
+    near = [[k * NEAR + j for j in range(NEAR)] for k in range(FAR)]
+    shifts = [
+        [(k * NEAR + j, (k + shift) % FAR * NEAR + j) for k in range(FAR) for j in range(NEAR)]
+        for shift in (1, 2)
     ]
 
     def exchange(array, axis, groups=None):
@@ -384,11 +383,13 @@
     sent = pack(ints, visibility, coordinate)
     arrived = exchange(sent, "tm")
     meta = meta_of(arrived)
-    pieces = exchange(chunk_of(screens, lax.axis_index("tm")), "uv", z_groups)
-    piece = pick_z(ints, pieces)
-    pieces = [piece] + [lax.ppermute(piece, "uv", shift) for shift in y_shifts]
-    pieces = exchange(pick_y(ints, pieces), "uv", z_groups)
+    pieces = exchange(chunk_of(screens, lax.axis_index("tm")), "uv", near)
+    piece = pick_near(ints, pieces)
+    both = jnp.concatenate([piece, lax.ppermute(piece, "uv", shifts[0])], axis=0)
+    later = lax.ppermute(both, "uv", shifts[1])
+    pieces = exchange(pick_far(ints, (both, later)), "uv", near)
     x = grid_blocks(meta, ints, arrived.reshape(PEERS * PER, 16, LANES))
+    meta, x = lax.optimization_barrier((meta, x))
     wanted = exchange(asked(meta, pieces), "tm")
     return screen_product(x, wanted)
 

time: 98.5 us -> 97.6 us (level); the launches traced: 96.6 us -> 97.1 us
  blocking collectives: 0 us -> 16.5 us
  starting transfers between devices: 54.4 us -> 43.5 us
  waiting for transfers between devices: 24.8 us -> 19.9 us
    all_to_all x0 -> x1, blocking collectives: none -> 16.5 us  [exchange(): lax.all_to_all(array, axis, 0, 0, axis_index_groups=groups, tiled=True)]
    all_to_all x4 -> x3, starting transfers between devices: 41.6 us -> 26.8 us  [exchange(): lax.all_to_all(array, axis, 0, 0, axis_index_groups=groups, tiled=True)]
    all_to_all x4 -> x3, waiting for transfers between devices: 21.5 us -> 9.45 us  [exchange(): lax.all_to_all(array, axis, 0, 0, axis_index_groups=groups, tiled=True)]
    ppermute x3 -> x2, waiting for transfers between devices: 3.21 us -> 10.4 us  [the longest x1 5.63 us: on_device(): lax.ppermute(piece, 'uv', shifts[0])]
    ppermute x3 -> x2, starting transfers between devices: 12.8 us -> 16.7 us  [the longest x1 8.45 us: on_device(): later = lax.ppermute(both, 'uv', shifts[1])]
  transfers between devices with their start and end apart: 7 -> 5, of which waited for: 5 -> 4; matrix products, arithmetic and copies ran while one was open for 1% -> 1% of each run, Pallas kernels for 10% -> 10%
where the time goes in v3:
time: 97.6 us; the launch traced here: 97.1 us
  starting transfers between devices  43.5 us (45%)
  waiting for transfers between devices  19.9 us (20%)
  blocking collectives  16.5 us (17%)
  Pallas kernels  12.1 us (12%)
  local copies, waits for them, and re-layouts  4.6 us (5%)
    all_to_all x3, starting transfers between devices, exchange(): lax.all_to_all(array, axis, 0, 0, axis_index_groups=groups, tiled=True)  26.8 us
    all_to_all x1, blocking collectives, exchange(): lax.all_to_all(array, axis, 0, 0, axis_index_groups=groups, tiled=True)  16.5 us
    all_to_all x3, waiting for transfers between devices, exchange(): lax.all_to_all(array, axis, 0, 0, axis_index_groups=groups, tiled=True)  9.45 us
    ppermute x1, starting transfers between devices, on_device(): later = lax.ppermute(both, 'uv', shifts[1])  8.45 us
    ppermute x1, starting transfers between devices, on_device(): lax.ppermute(piece, 'uv', shifts[0])  8.3 us
    pallas_call x1, Pallas kernels, grid_blocks(): pl.pallas_call(grid_kernel, out_shape=jax.ShapeDtypeStruct((SLOTS * SUBS,...  6.23 us
    ppermute x1, waiting for transfers between devices, on_device(): lax.ppermute(piece, 'uv', shifts[0])  5.63 us
    ppermute x1, waiting for transfers between devices, on_device(): later = lax.ppermute(both, 'uv', shifts[1])  4.82 us
  transfers between devices with their start and end apart: 5, of which 4 were waited for; matrix products, arithmetic and copies ran while one was open for 1% of the time, Pallas kernels for 10%

profile of v3, /device:TPU:1, one launch (start us, length us, event | category | flops | bytes accessed | tf_op | source)
XLA Modules:
  0.0 97.1 jit_solution(4362184650489288991)
XLA Ops:
  0.0 1.2 %copy-done = bf16[1,64,8,1024]{3,2,1,0:T(8,128)(2,1)S(1)} copy-done((bf16[1,64,8,1024]{3,2,1,0:T(8,128)(2,1)S(1)}, bf16[1,64,8,1024]{3,2,1,0:T(8,128)(2,1)}, u32[]{:S(2)}) %copy-start) | copy-done | bytes 1048600
  1.2 0.7 constant_dynamic-slice_fusion
  2.0 13.3 %all-to-all-start.1 = ((bf16[16,16,128]{2,1,0:T(8,128)(2,1)}), bf16[16,16,128]{2,1,0:T(8,128)(2,1)S(1)}, u32[]{:S(2)}, u32[]{:S(2)}) async-start(bf16[16,16,128]{2,1,0:T(8,128)(2,1)} %bitcast.2), calls=%async_computation.1 | async-start | bytes 131072 | tf_op jit(solution)/shard_map/all_to_all | solution.py:379
  15.7 0.6 copy-done.6
  16.3 0.1 copy.13
  16.4 0.6 copy-done.7
  17.0 0.1 copy.12
  17.2 0.7 copy-done.8
  18.0 1.9 %pack_blocks.1 = bf16[16,6,16,128]{3,2,1,0:T(8,128)(2,1)} custom-call(s32[164]{0:T(256)S(1)} %concatenate.6.ints, bf16[3,1,16,8,128]{4,3,2,1,0:T(8,128)(2,1)S(1)} %copy-done.1, bf16[3,1,16,2,128]{4,3,2,1,0:T(2,128)(2,1)S(1)} %copy-done.2), custom_call_target="tpu_custom_call" | custom-call | flops 2000000 | bytes 600000 | tf_op jit(solution)/shard_map/pack_blocks/pallas_call | solution.py:102
  19.9 5.1 %all-to-all-done.1.in_ref = bf16[16,16,128]{2,1,0:T(8,128)(2,1)S(1)} async-done(((bf16[16,16,128]{2,1,0:T(8,128)(2,1)}), bf16[16,16,128]{2,1,0:T(8,128)(2,1)S(1)}, u32[]{:S(2)}, u32[]{:S(2)}) %all-to-all-start.1) | async-done | bytes 65568 | tf_op jit(solution)/shard_map/all_to_all | solution.py:379
  25.0 8.9 %all-to-all-start = ((bf16[16,6,16,128]{3,2,1,0:T(8,128)(2,1)}), bf16[16,6,16,128]{3,2,1,0:T(8,128)(2,1)S(1)}, u32[]{:S(2)}, u32[]{:S(2)}) async-start(bf16[16,6,16,128]{3,2,1,0:T(8,128)(2,1)} %pack_blocks.1), calls=%async_computation | async-start | bytes 786432 | tf_op jit(solution)/shard_map/all_to_all | solution.py:379
  33.9 0.6 pick_near.1
  34.5 8.3 %collective-permute-start = (bf16[3,16,128]{2,1,0:T(8,128)(2,1)S(1)}, bf16[3,16,128]{2,1,0:T(8,128)(2,1)S(1)}, u32[]{:S(2)}, u32[]{:S(2)}) collective-permute-start(bf16[3,16,128]{2,1,0:T(8,128)(2,1)S(1)} %pick_near.1), channel_id=1, source_target_pairs={{0,256},{16,272},{32,288},{48,304},{64,320},{80,336},{96,352},{112... | collective-permute-start | bytes 36872 | tf_op jit(solution)/shard_map/ppermute | solution.py:388
  42.8 5.6 %collective-permute-done = bf16[3,16,128]{2,1,0:T(8,128)(2,1)S(1)} collective-permute-done((bf16[3,16,128]{2,1,0:T(8,128)(2,1)S(1)}, bf16[3,16,128]{2,1,0:T(8,128)(2,1)S(1)}, u32[]{:S(2)}, u32[]{:S(2)}) %collective-permute-start) | collective-permute-done | bytes 12320 | tf_op jit(solution)/shard_map/ppermute | solution.py:388
  48.4 8.4 %collective-permute-start.1 = (bf16[6,16,128]{2,1,0:T(8,128)(2,1)S(1)}, bf16[6,16,128]{2,1,0:T(8,128)(2,1)S(1)}, u32[]{:S(2)}, u32[]{:S(2)}) collective-permute-start(bf16[6,16,128]{2,1,0:T(8,128)(2,1)S(1)} %pad_maximum_fusion.refs_0_), channel_id=1, source_target_pairs={{0,512},{16,528},{32,544},{48,560},{64,576},{80,592},{96,608},{112... | collective-permute-start | bytes 73736 | tf_op jit(solution)/shard_map/ppermute | solution.py:389
  56.9 4.8 %collective-permute-done.1.refs_1_ = bf16[6,16,128]{2,1,0:T(8,128)(2,1)S(1)} collective-permute-done((bf16[6,16,128]{2,1,0:T(8,128)(2,1)S(1)}, bf16[6,16,128]{2,1,0:T(8,128)(2,1)S(1)}, u32[]{:S(2)}, u32[]{:S(2)}) %collective-permute-start.1) | collective-permute-done | bytes 24608 | tf_op jit(solution)/shard_map/ppermute | solution.py:389
  61.7 1.3 %pick_far.1 = bf16[16,48,128]{2,1,0:T(8,128)(2,1)} custom-call(s32[164]{0:T(256)S(1)} %concatenate.6.ints, bf16[6,16,128]{2,1,0:T(8,128)(2,1)S(1)} %pad_maximum_fusion.refs_0_, bf16[6,16,128]{2,1,0:T(8,128)(2,1)S(1)} %collective-permute-done.1.refs_1_), custom_call_target="tpu_custom_call" | custom-call | tf_op jit(solution)/shard_map/pick_far/pallas_call | solution.py:255
  63.0 4.5 %all-to-all-start.2 = ((bf16[16,48,128]{2,1,0:T(8,128)(2,1)}), bf16[16,48,128]{2,1,0:T(8,128)(2,1)S(1)}, u32[]{:S(2)}, u32[]{:S(2)}) async-start(bf16[16,48,128]{2,1,0:T(8,128)(2,1)} %pick_far.1), calls=%async_computation.2 | async-start | bytes 393216 | tf_op jit(solution)/shard_map/all_to_all | solution.py:379
  67.5 0.2 fusion
  67.8 6.2 %grid_blocks.1.x_ref = f32[12,8,8,128]{3,2,1,0:T(8,128)S(1)} custom-call(s32[1536]{0:T(1024)S(1)} %reshape.38.meta, s32[164]{0:T(256)S(1)} %concatenate.6.ints, bf16[96,16,128]{2,1,0:T(8,128)(2,1)S(1)} %bitcast.3), custom_call_target="tpu_custom_call" | custom-call | flops 800000000 | bytes 800000 | tf_op jit(solution)/shard_map/grid_blocks/pallas_call | solution.py:205
  74.0 4.3 %all-to-all-done.2.in_ref = bf16[16,48,128]{2,1,0:T(8,128)(2,1)S(1)} async-done(((bf16[16,48,128]{2,1,0:T(8,128)(2,1)}), bf16[16,48,128]{2,1,0:T(8,128)(2,1)S(1)}, u32[]{:S(2)}, u32[]{:S(2)}) %all-to-all-start.2) | async-done | bytes 196640 | tf_op jit(solution)/shard_map/all_to_all | solution.py:379
  78.4 1.0 asked_stations.1
  79.3 16.5 %all_to_all.20.in_ref = bf16[16,96,128]{2,1,0:T(8,128)(2,1)S(1)} all-to-all(bf16[16,96,128]{2,1,0:T(8,128)(2,1)S(1)} %asked_stations.1), channel_id=1, replica_groups=mesh['uv'=64,'tm'=16] {'tm'}, dimensions={0} | all-to-all | bytes 786432 | tf_op jit(solution)/shard_map/all_to_all | solution.py:379
  95.9 1.2 %screen_product.1 = f32[1,4,8,1024]{3,2,1,0:T(8,128)} custom-call(f32[12,8,8,128]{3,2,1,0:T(8,128)S(1)} %grid_blocks.1.x_ref, bf16[16,96,128]{2,1,0:T(8,128)(2,1)S(1)} %all_to_all.20.in_ref), custom_call_target="tpu_custom_call" | custom-call | flops 3000000 | bytes 1000000 | tf_op jit(solution)/shard_map/screen_product/pallas_call | solution.py:338
  (26 shorter events, 0.7 us)
Async XLA Ops:
  0.0 1.2 %copy-start = (bf16[1,64,8,1024]{3,2,1,0:T(8,128)(2,1)S(1)}, bf16[1,64,8,1024]{3,2,1,0:T(8,128)(2,1)}, u32[]{:S(2)}) copy-start(bf16[1,64,8,1024]{3,2,1,0:T(8,128)(2,1)} %param.16) | copy-start | bytes 3145732
  2.0 16.0 %copy-start.1 = (bf16[3,1,16,8,128]{4,3,2,1,0:T(8,128)(2,1)S(1)}, bf16[3,1,16,8,128]{4,3,2,1,0:T(8,128)(2,1)}, u32[]{:S(2)}) copy-start(bf16[3,1,16,8,128]{4,3,2,1,0:T(8,128)(2,1)} %vis_ref.1) | copy-start | bytes 294916
  2.0 13.4 %copy-start.3 = (s32[3,1,16]{2,1,0:T(1,128)S(1)}, s32[3,1,16]{2,1,0:T(1,128)}, u32[]{:S(2)}) copy-start(s32[3,1,16]{2,1,0:T(1,128)} %param.11) | copy-start | bytes 580
  2.0 13.5 %copy-start.4 = (s32[3,1,16,1]{2,3,1,0:T(1,128)S(1)}, s32[3,1,16,1]{2,3,1,0:T(1,128)}, u32[]{:S(2)}) copy-start(s32[3,1,16,1]{2,3,1,0:T(1,128)} %param.12) | copy-start | bytes 580
  2.0 13.6 %copy-start.5 = (s32[3,1,16]{2,1,0:T(1,128)S(1)}, s32[3,1,16]{2,1,0:T(1,128)}, u32[]{:S(2)}) copy-start(s32[3,1,16]{2,1,0:T(1,128)} %param.13) | copy-start | bytes 580
  2.0 23.0 %all-to-all-start.1 = ((bf16[16,16,128]{2,1,0:T(8,128)(2,1)}), bf16[16,16,128]{2,1,0:T(8,128)(2,1)S(1)}, u32[]{:S(2)}, u32[]{:S(2)}) async-start(bf16[16,16,128]{2,1,0:T(8,128)(2,1)} %bitcast.2), calls=%async_computation.1 | async-start | bytes 131072 | tf_op jit(solution)/shard_map/all_to_all | solution.py:379
  15.3 2.6 %copy-start.2 = (bf16[3,1,16,2,128]{4,3,2,1,0:T(2,128)(2,1)S(1)}, bf16[3,1,16,2,128]{4,3,2,1,0:T(2,128)(2,1)}, u32[]{:S(2)}) copy-start(bf16[3,1,16,2,128]{4,3,2,1,0:T(2,128)(2,1)} %coord_ref.1) | copy-start | bytes 73732
  15.6 0.7 copy-start.6
  16.4 0.7 copy-start.7
  17.2 0.7 copy-start.8
  25.0 38.0 %all-to-all-start = ((bf16[16,6,16,128]{3,2,1,0:T(8,128)(2,1)}), bf16[16,6,16,128]{3,2,1,0:T(8,128)(2,1)S(1)}, u32[]{:S(2)}, u32[]{:S(2)}) async-start(bf16[16,6,16,128]{3,2,1,0:T(8,128)(2,1)} %pack_blocks.1), calls=%async_computation | async-start | bytes 786432 | tf_op jit(solution)/shard_map/all_to_all | solution.py:379
  34.5 13.9 %collective-permute-start = (bf16[3,16,128]{2,1,0:T(8,128)(2,1)S(1)}, bf16[3,16,128]{2,1,0:T(8,128)(2,1)S(1)}, u32[]{:S(2)}, u32[]{:S(2)}) collective-permute-start(bf16[3,16,128]{2,1,0:T(8,128)(2,1)S(1)} %pick_near.1), channel_id=1, source_target_pairs={{0,256},{16,272},{32,288},{48,304},{64,320},{80,336},{96,352},{112... | collective-permute-start | bytes 36872 | tf_op jit(solution)/shard_map/ppermute | solution.py:388
  48.4 13.3 %collective-permute-start.1 = (bf16[6,16,128]{2,1,0:T(8,128)(2,1)S(1)}, bf16[6,16,128]{2,1,0:T(8,128)(2,1)S(1)}, u32[]{:S(2)}, u32[]{:S(2)}) collective-permute-start(bf16[6,16,128]{2,1,0:T(8,128)(2,1)S(1)} %pad_maximum_fusion.refs_0_), channel_id=1, source_target_pairs={{0,512},{16,528},{32,544},{48,560},{64,576},{80,592},{96,608},{112... | collective-permute-start | bytes 73736 | tf_op jit(solution)/shard_map/ppermute | solution.py:389
  63.0 15.4 %all-to-all-start.2 = ((bf16[16,48,128]{2,1,0:T(8,128)(2,1)}), bf16[16,48,128]{2,1,0:T(8,128)(2,1)S(1)}, u32[]{:S(2)}, u32[]{:S(2)}) async-start(bf16[16,48,128]{2,1,0:T(8,128)(2,1)} %pick_far.1), calls=%async_computation.2 | async-start | bytes 393216 | tf_op jit(solution)/shard_map/all_to_all | solution.py:379

commit v4 on v3

--- a/solution.py
+++ b/solution.py
@@ -15,21 +15,18 @@
 PER = SLOTS * CAP
 NEAR = 16
 FAR = 4
-NDEV = NEAR * FAR
 ST_PIECE = STATIONS // NEAR
 REQS = 2 * SUBS
 LANES = 128
 F32 = jnp.float32
 BF16 = jnp.bfloat16
 
-OWNER = 0
-SUB = OWNER + SLOTS * BLOCKS
-COUNT = SUB + SLOTS * BLOCKS
-PAIRS = COUNT + SLOTS * BLOCKS
-ROOTS = PAIRS + REQS
-ME = ROOTS + SLOTS
-OFFS = ME + 1
-META = 16
+ROWS = 64
+U_ROW = PER * 8
+V_ROW = U_ROW + PER
+META_ROW = V_ROW + PER
+META = 32
+PAIR_LANE = 16
 
 COS_POLY = (1.0, -19.73920440673828, 64.93911743164062, -85.45014190673828, 60.167633056640625,
             -25.967601776123047, 6.528658866882324)
@@ -66,18 +63,20 @@
     return a[0] * b[0] - a[1] * b[1], a[0] * b[1] + a[1] * b[0]
 
 
-def pack_kernel(ints, vis_ref, coord_ref, out_ref, taken):
+def pack_kernel(owners, subs, counts, pair, vis_ref, coord_ref, out_ref, taken, stage):
     lane = lax.broadcasted_iota(jnp.int32, (1, LANES), 1)
     pairs = jnp.zeros((1, LANES), F32)
     for j in range(REQS):
-        pairs = jnp.where(lane == META // 2 + j, ints[PAIRS + j].astype(F32), pairs)
-    empty = jnp.concatenate([jnp.zeros((10, LANES), F32), pairs, jnp.zeros((5, LANES), F32)], axis=0)
-    empty = empty.astype(BF16)
+        pairs = jnp.where(lane == PAIR_LANE + j, pair[0, j % 2, j // 2].astype(F32), pairs)
+    last = lax.broadcasted_iota(jnp.int32, (8, LANES), 0) == META_ROW % 8
+    last = jnp.where(last, pairs, 0.0)
 
     @pl.loop(0, PEERS)
     def _(o):
-        for k in range(PER):
-            out_ref[o, k] = empty
+        stage[o, 0:ROWS - 16, :] = jnp.zeros((ROWS - 16, LANES), F32)
+        for half in (16, 8):
+            first = ROWS - half
+            stage[o, first:first + 8, :] = last if META_ROW // 8 * 8 == first else jnp.zeros_like(last)
 
     for slot in range(SLOTS):
         for o in range(PEERS):
@@ -85,31 +84,36 @@
 
         @pl.loop(0, BLOCKS)
         def _(i):
-            spot = slot * BLOCKS + i
-            owner = ints[OWNER + spot]
+            owner = owners[slot, 0, i]
             rank = taken[owner]
             taken[owner] = rank + 1
+            k = slot * CAP + rank
             values = vis_ref[slot, 0, i].astype(F32)
-            values = jnp.where(lane < ints[COUNT + spot], values, 0.0)
-            meta = jnp.where(lane == 0, ints[SUB + spot].astype(F32), jnp.where(lane == 1, 1.0, pairs))
-            rows = jnp.concatenate(
-                [values, coord_ref[slot, 0, i].astype(F32), meta, jnp.zeros((5, LANES), F32)], axis=0
-            )
-            out_ref[owner, slot * CAP + rank] = rows.astype(BF16)
-
-
-def pack(ints, visibility, coordinate, **kw):
+            values = jnp.where(lane < counts[slot, 0, i], values, 0.0)
+            stage[owner, pl.ds(pl.multiple_of(k * 8, 8), 8), :] = values
+            where = coord_ref[slot, 0, i].astype(F32)
+            stage[owner, pl.ds(U_ROW + k, 1), :] = where[0:1]
+            stage[owner, pl.ds(V_ROW + k, 1), :] = where[1:2]
+            meta = jnp.where(lane == 2 * k, subs[slot, 0, i].astype(F32), jnp.where(lane == 2 * k + 1, 1.0, 0.0))
+            stage[owner, META_ROW:META_ROW + 1, :] += meta
+
+    @pl.loop(0, PEERS)
+    def _(o):
+        out_ref[o] = stage[o].astype(BF16)
+
+
+def pack(owners, subs, counts, pair, visibility, coordinate, **kw):
     return pl.pallas_call(
         pack_kernel,
-        out_shape=jax.ShapeDtypeStruct((PEERS, PER, 16, LANES), BF16),
-        in_specs=[smem(), vmem(), vmem()],
-        out_specs=vmem(),
-        scratch_shapes=[pltpu.SMEM((PEERS,), jnp.int32)],
+        out_shape=jax.ShapeDtypeStruct((PEERS, ROWS, LANES), BF16),
+        in_specs=[smem()] * 4 + [vmem(), vmem()],
+        out_specs=vmem(),
+        scratch_shapes=[pltpu.SMEM((PEERS,), jnp.int32), pltpu.VMEM((PEERS, ROWS, LANES), F32)],
         name="pack_blocks",
         cost_estimate=pl.CostEstimate(flops=2000000, bytes_accessed=600000, transcendentals=0),
         compiler_params=room(),
         **kw,
-    )(ints, visibility, coordinate)
+    )(owners, subs, counts, pair, visibility, coordinate)
 
 
 def block_transpose(rows):
@@ -131,15 +135,17 @@
 BATCH = 4
 
 
-def grid_kernel(meta, ints, rows_ref, x_ref, acc, order, bucket):
+def grid_kernel(meta, offs, rows_ref, x_ref, acc, coords, order, bucket):
     acc[...] = jnp.zeros_like(acc)
+    for t in range(PEERS):
+        coords[t] = rows_ref[t, ROWS - 16:ROWS, :].astype(F32)
 
     def gather(t, carry):
         count, spare = carry
         for k in range(PER):
             b = t * PER + k
-            sub = meta[b * META]
-            live = meta[b * META + 1]
+            sub = meta[t * META + 2 * k]
+            live = meta[t * META + 2 * k + 1]
             order[count] = b
             bucket[count] = (k // CAP) * SUBS + sub
             spare = jnp.where(live == 0, b, spare)
@@ -161,11 +167,14 @@
             b = order[step * BATCH + j]
             key = bucket[step * BATCH + j]
             sub = key % SUBS
-            tile = rows_ref[b].astype(F32)
-            du = tile[8:9, :] - ints[OFFS + 2 * sub].astype(F32)
-            dv = tile[9:10, :] - ints[OFFS + 2 * sub + 1].astype(F32)
-            du = jnp.broadcast_to(du, (8, LANES))
-            dv = jnp.broadcast_to(dv, (8, LANES))
+            t = b // PER
+            k = b % PER
+            tile = rows_ref[t, pl.ds(pl.multiple_of(k // CAP * 16, 16), 16), :].astype(F32)
+            tile = jnp.where(k % CAP == 0, tile[0:8], tile[8:16])
+            u = coords[t, pl.ds(U_ROW - (ROWS - 16) + k, 1), :]
+            v = coords[t, pl.ds(V_ROW - (ROWS - 16) + k, 1), :]
+            du = jnp.broadcast_to(u - offs[0, 0, sub].astype(F32), (8, LANES))
+            dv = jnp.broadcast_to(v - offs[0, 1, sub].astype(F32), (8, LANES))
             turn_l = cis(du * (1.0 / SIDE))
             turn_m = cis(dv * (8.0 / SIDE))
             current = cis(du * seed_l)
@@ -201,7 +210,7 @@
                 x_ref[key, 4 * part + p] = plane
 
 
-def grid_blocks(meta, ints, rows, **kw):
+def grid_blocks(meta, offs, rows, **kw):
     return pl.pallas_call(
         grid_kernel,
         out_shape=jax.ShapeDtypeStruct((SLOTS * SUBS, 8, 8, LANES), F32),
@@ -209,6 +218,7 @@
         out_specs=vmem(),
         scratch_shapes=[
             pltpu.VMEM((SLOTS * SUBS, 2 * SIDE, 8 * SIDE), F32),
+            pltpu.VMEM((PEERS, 16, LANES), F32),
             pltpu.SMEM((PEERS * PER + BATCH,), jnp.int32),
             pltpu.SMEM((PEERS * PER + BATCH,), jnp.int32),
         ],
@@ -216,51 +226,77 @@
         cost_estimate=pl.CostEstimate(flops=800000000, bytes_accessed=800000, transcendentals=0),
         compiler_params=room(),
         **kw,
-    )(meta, ints, rows)
-
-
-def pick_near_kernel(ints, in_ref, out_ref):
+    )(meta, offs, rows)
+
+
+def chunk_kernel(t_ref, in_ref, out_ref):
+    odd = t_ref[0] % 2 == 1
+    low = lax.broadcasted_iota(jnp.int32, (8, LANES), 0) < 4
+
+    def two(first, second):
+        a, b = in_ref[0, first].astype(F32), in_ref[0, second].astype(F32)
+        a, b = jnp.where(odd, pltpu.roll(a, 4, 0), a), jnp.where(odd, b, pltpu.roll(b, 4, 0))
+        return jnp.where(low, a, b)
+
+    for j in range(NEAR):
+        first = j * ST_PIECE
+        out_ref[j] = jnp.concatenate([two(first, first + 1), two(first + 2, first + 3)], axis=0).astype(BF16)
+
+
+def chunk_of(screens, t, **kw):
+    return pl.pallas_call(
+        chunk_kernel,
+        out_shape=jax.ShapeDtypeStruct((NEAR, ST_PIECE * 4, LANES), BF16),
+        grid_spec=pltpu.PrefetchScalarGridSpec(
+            num_scalar_prefetch=1,
+            grid=(1,),
+            in_specs=[pl.BlockSpec((1, STATIONS, 8, LANES), lambda i, t: (0, 0, 0, t[0] // 2))],
+            out_specs=pl.BlockSpec((NEAR, ST_PIECE * 4, LANES), lambda i, t: (0, 0, 0)),
+        ),
+        name="cut_chunk",
+        compiler_params=room(),
+        **kw,
+    )(t.reshape(1), screens)
+
+
+def pick_near_kernel(roots, in_ref, out_ref):
     for s in range(SLOTS):
-        out_ref[s] = in_ref[ints[ROOTS + s] % NEAR]
-
-
-def pick_near(ints, pieces, **kw):
+        piece = in_ref[roots[s] % NEAR]
+        for k in range(FAR):
+            out_ref[k, s] = piece
+
+
+def pick_near(roots, pieces, **kw):
     return pl.pallas_call(
         pick_near_kernel,
-        out_shape=jax.ShapeDtypeStruct((SLOTS, 16, LANES), BF16),
+        out_shape=jax.ShapeDtypeStruct((FAR, SLOTS, 16, LANES), BF16),
         in_specs=[smem(), vmem()],
         out_specs=vmem(),
         name="pick_near",
         compiler_params=room(),
         **kw,
-    )(ints, pieces)
-
-
-def pick_far_kernel(ints, *refs):
-    both_ref, later_ref, out_ref = refs
-    pieces = []
-    for s in range(SLOTS):
-        shift = (ints[ME] // NEAR - ints[ROOTS + s] // NEAR + FAR) % FAR
-        k = shift % 2 * SLOTS + s
-        piece = jnp.where(shift < 2, both_ref[k].astype(F32), later_ref[k].astype(F32))
-        pieces.append(piece)
+    )(roots, pieces)
+
+
+def pick_far_kernel(roots, in_ref, out_ref):
+    pieces = [in_ref[roots[s] // NEAR, s].astype(F32) for s in range(SLOTS)]
     rows = jnp.concatenate(
         [pieces[s][4 * i:4 * i + 4] for i in range(ST_PIECE) for s in range(SLOTS)], axis=0
     ).astype(BF16)
-    for z in range(NEAR):
-        out_ref[z] = rows
-
-
-def pick_far(ints, pieces, **kw):
+    for j in range(NEAR):
+        out_ref[j] = rows
+
+
+def pick_far(roots, pieces, **kw):
     return pl.pallas_call(
         pick_far_kernel,
         out_shape=jax.ShapeDtypeStruct((NEAR, ST_PIECE * SLOTS * 4, LANES), BF16),
-        in_specs=[smem(), vmem(), vmem()],
+        in_specs=[smem(), vmem()],
         out_specs=vmem(),
         name="pick_far",
         compiler_params=room(),
         **kw,
-    )(ints, *pieces)
+    )(roots, pieces)
 
 
 ROWS_ST = SLOTS * 4
@@ -275,7 +311,7 @@
     @pl.loop(0, PEERS)
     def _(t):
         for r in range(REQS):
-            station = meta[t * (PER * META) + META // 2 + r]
+            station = meta[t * META + PAIR_LANE + r]
             stage[ROWS_ST * r:ROWS_ST * (r + 1), :] = table[station, 0:ROWS_ST, :]
         out_ref[t] = stage[...].astype(BF16)
 
@@ -351,44 +387,25 @@
     )(x, screens)
 
 
-def pack_ints(block_count, owner_index, subgrid_index, offsets, station_pair, slot_owner, me):
-    return jnp.concatenate([
-        owner_index.reshape(-1), subgrid_index.reshape(-1), block_count.reshape(-1),
-        station_pair.reshape(-1), slot_owner, me.reshape(-1), offsets.reshape(-1),
-    ])
-
-
-def chunk_of(screens, t):
-    part = lax.dynamic_slice(screens[0], (0, 4 * (t % 2), LANES * (t // 2)), (STATIONS, 4, LANES))
-    return part.reshape(NEAR, ST_PIECE * 4, LANES)
-
-
 def meta_of(arrived):
-    return arrived[:, :, 10, :META].astype(jnp.int32).reshape(-1)
+    return arrived[:, META_ROW, :META].astype(jnp.int32).reshape(-1)
 
 
 def on_device(visibility, coordinate, block_count, owner_index, subgrid_index, offsets,
               station_pair, screens, slot_owner):
     near = [[k * NEAR + j for j in range(NEAR)] for k in range(FAR)]
-    shifts = [
-        [(k * NEAR + j, (k + shift) % FAR * NEAR + j) for k in range(FAR) for j in range(NEAR)]
-        for shift in (1, 2)
-    ]
+    far = [[k * NEAR + j for k in range(FAR)] for j in range(NEAR)]
 
     def exchange(array, axis, groups=None):
         return lax.all_to_all(array, axis, 0, 0, axis_index_groups=groups, tiled=True)
 
-    ints = pack_ints(block_count, owner_index, subgrid_index, offsets, station_pair, slot_owner,
-                     lax.axis_index("uv"))
-    sent = pack(ints, visibility, coordinate)
+    pieces = exchange(chunk_of(screens, lax.axis_index("tm")), "uv", near)
+    pieces = exchange(pick_near(slot_owner, pieces), "uv", far)
+    sent = pack(owner_index[..., 0], subgrid_index, block_count, station_pair.swapaxes(1, 2), visibility, coordinate)
     arrived = exchange(sent, "tm")
     meta = meta_of(arrived)
-    pieces = exchange(chunk_of(screens, lax.axis_index("tm")), "uv", near)
-    piece = pick_near(ints, pieces)
-    both = jnp.concatenate([piece, lax.ppermute(piece, "uv", shifts[0])], axis=0)
-    later = lax.ppermute(both, "uv", shifts[1])
-    pieces = exchange(pick_far(ints, (both, later)), "uv", near)
-    x = grid_blocks(meta, ints, arrived.reshape(PEERS * PER, 16, LANES))
+    pieces = exchange(pick_far(slot_owner, pieces), "uv", near)
+    x = grid_blocks(meta, offsets.swapaxes(1, 2), arrived)
     meta, x = lax.optimization_barrier((meta, x))
     wanted = exchange(asked(meta, pieces), "tm")
     return screen_product(x, wanted)

time: 97.6 us -> 98.4 us (level)
  blocking collectives: 16.5 us -> 35.8 us
  starting transfers between devices: 43.5 us -> 27.1 us
  Pallas kernels: 12.1 us -> 17.2 us
  waiting for transfers between devices: 19.9 us -> 14.9 us
  local copies, waits for them, and re-layouts: 4.6 us -> 2.66 us
    all_to_all x1 -> x2, blocking collectives: 16.5 us -> 35.8 us  [exchange(): lax.all_to_all(array, axis, 0, 0, axis_index_groups=groups, tiled=True)]
    ppermute x2 -> x0, starting transfers between devices: 16.7 us -> none  [the longest x1 8.45 us: on_device(): later = lax.ppermute(both, 'uv', shifts[1])]
    ppermute x2 -> x0, waiting for transfers between devices: 10.4 us -> none  [the longest x1 5.63 us: on_device(): lax.ppermute(piece, 'uv', shifts[0])]
    all_to_all x3, waiting for transfers between devices: 9.45 us -> 14.9 us  [exchange(): lax.all_to_all(array, axis, 0, 0, axis_index_groups=groups, tiled=True)]
    pallas_call x1, Pallas kernels: 6.23 us -> 10.3 us  [grid_blocks(): pl.pallas_call(grid_kernel, out_shape=jax.ShapeDtypeStruct((SLOTS * SUBS,...]
    pallas_call x2 -> x3, Pallas kernels: 2.46 us -> 3.55 us  [the longest x1 2.3 us: pack(): pl.pallas_call(pack_kernel, out_shape=jax.ShapeDtypeStruct((PEERS, ROWS,...]
    unnamed x20 -> x18, local copies, waits for them, and re-layouts: 3.27 us -> 2.58 us
  transfers between devices with their start and end apart: 5 -> 3, of which waited for: 4 -> 2; matrix products, arithmetic and copies ran while one was open for 1% -> 0% of each run, Pallas kernels for 10% -> 14%
where the time goes in v4:
time: 98.4 us; the launch traced here: 97.8 us
  blocking collectives  35.8 us (36%)
  starting transfers between devices  27.1 us (28%)
  Pallas kernels  17.2 us (17%)
  waiting for transfers between devices  14.9 us (15%)
  local copies, waits for them, and re-layouts  2.66 us (3%)
    all_to_all x2, blocking collectives, exchange(): lax.all_to_all(array, axis, 0, 0, axis_index_groups=groups, tiled=True)  35.8 us
    all_to_all x3, starting transfers between devices, exchange(): lax.all_to_all(array, axis, 0, 0, axis_index_groups=groups, tiled=True)  27.1 us
    all_to_all x3, waiting for transfers between devices, exchange(): lax.all_to_all(array, axis, 0, 0, axis_index_groups=groups, tiled=True)  14.9 us
    pallas_call x1, Pallas kernels, grid_blocks(): pl.pallas_call(grid_kernel, out_shape=jax.ShapeDtypeStruct((SLOTS * SUBS,...  10.3 us
    unnamed x18, local copies, waits for them, and re-layouts  2.58 us
    pallas_call x1, Pallas kernels, pack(): pl.pallas_call(pack_kernel, out_shape=jax.ShapeDtypeStruct((PEERS, ROWS,...  2.3 us
  transfers between devices with their start and end apart: 3, of which 2 were waited for; matrix products, arithmetic and copies ran while one was open for 0% of the time, Pallas kernels for 14%

profile of v4, /device:TPU:1, one launch (start us, length us, event | category | flops | bytes accessed | tf_op | source)
XLA Modules:
  0.0 97.8 jit_solution(706242656299433340)
XLA Ops:
  0.0 1.2 %copy-done = bf16[1,64,8,1024]{3,2,1,0:T(8,128)(2,1)S(1)} copy-done((bf16[1,64,8,1024]{3,2,1,0:T(8,128)(2,1)S(1)}, bf16[1,64,8,1024]{3,2,1,0:T(8,128)(2,1)}, u32[]{:S(2)}) %copy-start) | copy-done | bytes 1048600
  1.2 0.1 cut_chunk.1
  1.3 0.0 copy-start.3
  1.3 22.6 %all_to_all.25.in_ref = bf16[16,16,128]{2,1,0:T(8,128)(2,1)S(1)} all-to-all(bf16[16,16,128]{2,1,0:T(8,128)(2,1)S(1)} %cut_chunk.1), channel_id=1, replica_groups={{0,16,32,48,64,80,96,112,128,144,160,176,192,208,224,240},{256,272,288,..., dimensions={0} | all-to-all | bytes 131072 | tf_op jit(solution)/shard_map/all_to_all | solution.py:400
  23.9 0.0 copy-done.3
  24.0 1.2 %pick_near.1 = bf16[4,3,16,128]{3,2,1,0:T(8,128)(2,1)} custom-call(s32[3]{0:T(128)S(1)} %copy-done.3, bf16[16,16,128]{2,1,0:T(8,128)(2,1)S(1)} %all_to_all.25.in_ref), custom_call_target="tpu_custom_call" | custom-call | tf_op jit(solution)/shard_map/pick_near/pallas_call | solution.py:270
  25.1 15.9 %all-to-all-start.2 = ((bf16[4,3,16,128]{3,2,1,0:T(8,128)(2,1)}), bf16[4,3,16,128]{3,2,1,0:T(8,128)(2,1)S(1)}, u32[]{:S(2)}, u32[]{:S(2)}) async-start(bf16[4,3,16,128]{3,2,1,0:T(8,128)(2,1)} %pick_near.1), calls=%async_computation.2 | async-start | bytes 98304 | tf_op jit(solution)/shard_map/all_to_all | solution.py:400
  41.0 0.0 copy-done.1
  41.0 0.0 copy-done.2
  41.0 0.6 copy-done.4
  41.7 0.0 copy-done.5
  41.7 2.3 %pack_blocks.1 = bf16[16,64,128]{2,1,0:T(8,128)(2,1)} custom-call(s32[3,1,16]{2,1,0:T(1,128)S(1)} %bitcast.4, s32[3,1,16]{2,1,0:T(1,128)S(1)} %copy-done.5, s32[3,1,16]{2,1,0:T(1,128)S(1)} %copy-done.6, s32[1,2,4]{2,1,0:T(2,128)S(1)} %bitcast.5, bf16[3,1,16,8,128]{4,3,2,1,0:T(8,128)(2,1)S(1)} %copy-done.1, bf16[3,1,16,2,128]{4,3,2,1,0:T(2,128)(2,1)S(1)} %copy-done.2), custom_call_target="tpu_custom_call" | custom-call | flops 2000000 | bytes 600000 | tf_op jit(solution)/shard_map/pack_blocks/pallas_call | solution.py:106
  44.0 9.0 %all-to-all-done.2.in_ref = bf16[4,3,16,128]{3,2,1,0:T(8,128)(2,1)S(1)} async-done(((bf16[4,3,16,128]{3,2,1,0:T(8,128)(2,1)}), bf16[4,3,16,128]{3,2,1,0:T(8,128)(2,1)S(1)}, u32[]{:S(2)}, u32[]{:S(2)}) %all-to-all-start.2) | async-done | bytes 49184 | tf_op jit(solution)/shard_map/all_to_all | solution.py:400
  53.0 7.7 %all-to-all-start = ((bf16[16,64,128]{2,1,0:T(8,128)(2,1)}), bf16[16,64,128]{2,1,0:T(8,128)(2,1)S(1)}, u32[]{:S(2)}, u32[]{:S(2)}) async-start(bf16[16,64,128]{2,1,0:T(8,128)(2,1)} %pack_blocks.1), calls=%async_computation | async-start | bytes 524288 | tf_op jit(solution)/shard_map/all_to_all | solution.py:400
  60.7 1.3 %pick_far.1 = bf16[16,48,128]{2,1,0:T(8,128)(2,1)} custom-call(s32[3]{0:T(128)S(1)} %copy-done.3, bf16[4,3,16,128]{3,2,1,0:T(8,128)(2,1)S(1)} %all-to-all-done.2.in_ref), custom_call_target="tpu_custom_call" | custom-call | tf_op jit(solution)/shard_map/pick_far/pallas_call | solution.py:291
  62.0 5.9 %all-to-all-done.rows_ref = bf16[16,64,128]{2,1,0:T(8,128)(2,1)S(1)} async-done(((bf16[16,64,128]{2,1,0:T(8,128)(2,1)}), bf16[16,64,128]{2,1,0:T(8,128)(2,1)S(1)}, u32[]{:S(2)}, u32[]{:S(2)}) %all-to-all-start) | async-done | bytes 262176 | tf_op jit(solution)/shard_map/all_to_all | solution.py:400
  67.9 3.5 %all-to-all-start.3 = ((bf16[16,48,128]{2,1,0:T(8,128)(2,1)}), bf16[16,48,128]{2,1,0:T(8,128)(2,1)S(1)}, u32[]{:S(2)}, u32[]{:S(2)}) async-start(bf16[16,48,128]{2,1,0:T(8,128)(2,1)} %pick_far.1), calls=%async_computation.3 | async-start | bytes 393216 | tf_op jit(solution)/shard_map/all_to_all | solution.py:400
  71.5 0.1 reshape.8.meta
  71.6 0.7 copy-done.8
  72.2 10.3 %grid_blocks.1.x_ref = f32[12,8,8,128]{3,2,1,0:T(8,128)S(1)} custom-call(s32[512]{0:T(512)S(1)} %reshape.8.meta, s32[1,2,4]{2,1,0:T(2,128)S(1)} %bitcast.6, bf16[16,64,128]{2,1,0:T(8,128)(2,1)S(1)} %all-to-all-done.rows_ref), custom_call_target="tpu_custom_call" | custom-call | flops 800000000 | bytes 800000 | tf_op jit(solution)/shard_map/grid_blocks/pallas_call | solution.py:214
  82.6 0.0 all-to-all-done.3.in_ref
  82.6 0.9 asked_stations.1
  83.5 13.1 %all_to_all.26.in_ref = bf16[16,96,128]{2,1,0:T(8,128)(2,1)S(1)} all-to-all(bf16[16,96,128]{2,1,0:T(8,128)(2,1)S(1)} %asked_stations.1), channel_id=1, replica_groups=mesh['uv'=64,'tm'=16] {'tm'}, dimensions={0} | all-to-all | bytes 786432 | tf_op jit(solution)/shard_map/all_to_all | solution.py:400
  96.6 1.2 %screen_product.1 = f32[1,4,8,1024]{3,2,1,0:T(8,128)} custom-call(f32[12,8,8,128]{3,2,1,0:T(8,128)S(1)} %grid_blocks.1.x_ref, bf16[16,96,128]{2,1,0:T(8,128)(2,1)S(1)} %all_to_all.26.in_ref), custom_call_target="tpu_custom_call" | custom-call | flops 3000000 | bytes 1000000 | tf_op jit(solution)/shard_map/screen_product/pallas_call | solution.py:374
  (11 shorter events, 0.1 us)
Async XLA Ops:
  0.0 1.2 %copy-start = (bf16[1,64,8,1024]{3,2,1,0:T(8,128)(2,1)S(1)}, bf16[1,64,8,1024]{3,2,1,0:T(8,128)(2,1)}, u32[]{:S(2)}) copy-start(bf16[1,64,8,1024]{3,2,1,0:T(8,128)(2,1)} %in_ref.1) | copy-start | bytes 3145732
  1.3 22.6 %copy-start.3 = (s32[3]{0:T(128)S(1)}, s32[3]{0:T(128)}, u32[]{:S(2)}) copy-start(s32[3]{0:T(128)} %roots.3) | copy-start | bytes 40
  23.9 17.1 %copy-start.1 = (bf16[3,1,16,8,128]{4,3,2,1,0:T(8,128)(2,1)S(1)}, bf16[3,1,16,8,128]{4,3,2,1,0:T(8,128)(2,1)}, u32[]{:S(2)}) copy-start(bf16[3,1,16,8,128]{4,3,2,1,0:T(8,128)(2,1)} %vis_ref.1) | copy-start | bytes 294916
  25.1 15.9 %copy-start.2 = (bf16[3,1,16,2,128]{4,3,2,1,0:T(2,128)(2,1)S(1)}, bf16[3,1,16,2,128]{4,3,2,1,0:T(2,128)(2,1)}, u32[]{:S(2)}) copy-start(bf16[3,1,16,2,128]{4,3,2,1,0:T(2,128)(2,1)} %coord_ref.1) | copy-start | bytes 73732
  25.1 15.9 %copy-start.6 = (s32[3,1,16]{2,1,0:T(1,128)S(1)}, s32[3,1,16]{2,1,0:T(1,128)}, u32[]{:S(2)}) copy-start(s32[3,1,16]{2,1,0:T(1,128)} %counts.1) | copy-start | bytes 580
  25.1 15.9 %copy-start.7 = (s32[1,4,2]{1,2,0:T(2,128)S(1)}, s32[1,4,2]{1,2,0:T(2,128)}, u32[]{:S(2)}) copy-start(s32[1,4,2]{1,2,0:T(2,128)} %param.15) | copy-start | bytes 100
  25.1 27.9 %all-to-all-start.2 = ((bf16[4,3,16,128]{3,2,1,0:T(8,128)(2,1)}), bf16[4,3,16,128]{3,2,1,0:T(8,128)(2,1)S(1)}, u32[]{:S(2)}, u32[]{:S(2)}) async-start(bf16[4,3,16,128]{3,2,1,0:T(8,128)(2,1)} %pick_near.1), calls=%async_computation.2 | async-start | bytes 98304 | tf_op jit(solution)/shard_map/all_to_all | solution.py:400
  41.0 0.7 copy-start.4
  41.0 0.7 copy-start.5
  53.0 14.9 %all-to-all-start = ((bf16[16,64,128]{2,1,0:T(8,128)(2,1)}), bf16[16,64,128]{2,1,0:T(8,128)(2,1)S(1)}, u32[]{:S(2)}, u32[]{:S(2)}) async-start(bf16[16,64,128]{2,1,0:T(8,128)(2,1)} %pack_blocks.1), calls=%async_computation | async-start | bytes 524288 | tf_op jit(solution)/shard_map/all_to_all | solution.py:400
  67.9 14.7 %all-to-all-start.3 = ((bf16[16,48,128]{2,1,0:T(8,128)(2,1)}), bf16[16,48,128]{2,1,0:T(8,128)(2,1)S(1)}, u32[]{:S(2)}, u32[]{:S(2)}) async-start(bf16[16,48,128]{2,1,0:T(8,128)(2,1)} %pick_far.1), calls=%async_computation.3 | async-start | bytes 393216 | tf_op jit(solution)/shard_map/all_to_all | solution.py:400
  71.6 0.7 copy-start.8

commit v5 on v4

--- a/solution.py
+++ b/solution.py
@@ -229,12 +229,16 @@
     )(meta, offs, rows)
 
 
-def chunk_kernel(t_ref, in_ref, out_ref):
+def chunk_kernel(t_ref, screens_ref, out_ref, in_ref, arrived):
+    lanes = pl.ds(pl.multiple_of(t_ref[0] // 2 * LANES, LANES), LANES)
+    copy = pltpu.make_async_copy(screens_ref.at[0, :, :, lanes], in_ref, arrived)
+    copy.start()
+    copy.wait()
     odd = t_ref[0] % 2 == 1
     low = lax.broadcasted_iota(jnp.int32, (8, LANES), 0) < 4
 
     def two(first, second):
-        a, b = in_ref[0, first].astype(F32), in_ref[0, second].astype(F32)
+        a, b = in_ref[first].astype(F32), in_ref[second].astype(F32)
         a, b = jnp.where(odd, pltpu.roll(a, 4, 0), a), jnp.where(odd, b, pltpu.roll(b, 4, 0))
         return jnp.where(low, a, b)
 
@@ -247,29 +251,23 @@
     return pl.pallas_call(
         chunk_kernel,
         out_shape=jax.ShapeDtypeStruct((NEAR, ST_PIECE * 4, LANES), BF16),
-        grid_spec=pltpu.PrefetchScalarGridSpec(
-            num_scalar_prefetch=1,
-            grid=(1,),
-            in_specs=[pl.BlockSpec((1, STATIONS, 8, LANES), lambda i, t: (0, 0, 0, t[0] // 2))],
-            out_specs=pl.BlockSpec((NEAR, ST_PIECE * 4, LANES), lambda i, t: (0, 0, 0)),
-        ),
+        in_specs=[smem(), pl.BlockSpec(memory_space=pltpu.HBM)],
+        out_specs=vmem(),
+        scratch_shapes=[pltpu.VMEM((STATIONS, 8, LANES), BF16), pltpu.SemaphoreType.DMA],
         name="cut_chunk",
-        compiler_params=room(),
         **kw,
     )(t.reshape(1), screens)
 
 
 def pick_near_kernel(roots, in_ref, out_ref):
     for s in range(SLOTS):
-        piece = in_ref[roots[s] % NEAR]
-        for k in range(FAR):
-            out_ref[k, s] = piece
+        out_ref[s] = in_ref[roots[s] // FAR]
 
 
 def pick_near(roots, pieces, **kw):
     return pl.pallas_call(
         pick_near_kernel,
-        out_shape=jax.ShapeDtypeStruct((FAR, SLOTS, 16, LANES), BF16),
+        out_shape=jax.ShapeDtypeStruct((SLOTS, 16, LANES), BF16),
         in_specs=[smem(), vmem()],
         out_specs=vmem(),
         name="pick_near",
@@ -278,8 +276,12 @@
     )(roots, pieces)
 
 
-def pick_far_kernel(roots, in_ref, out_ref):
-    pieces = [in_ref[roots[s] // NEAR, s].astype(F32) for s in range(SLOTS)]
+def pick_far_kernel(roots, me, even_ref, odd_ref, out_ref):
+    pieces = []
+    for s in range(SLOTS):
+        shift = (me[0] - roots[s] + FAR * NEAR) % FAR
+        k = shift // 2 * SLOTS + s
+        pieces.append(jnp.where(shift % 2 == 0, even_ref[k].astype(F32), odd_ref[k].astype(F32)))
     rows = jnp.concatenate(
         [pieces[s][4 * i:4 * i + 4] for i in range(ST_PIECE) for s in range(SLOTS)], axis=0
     ).astype(BF16)
@@ -287,16 +289,16 @@
         out_ref[j] = rows
 
 
-def pick_far(roots, pieces, **kw):
+def pick_far(roots, me, even, odd, **kw):
     return pl.pallas_call(
         pick_far_kernel,
         out_shape=jax.ShapeDtypeStruct((NEAR, ST_PIECE * SLOTS * 4, LANES), BF16),
-        in_specs=[smem(), vmem()],
+        in_specs=[smem(), smem(), vmem(), vmem()],
         out_specs=vmem(),
         name="pick_far",
         compiler_params=room(),
         **kw,
-    )(roots, pieces)
+    )(roots, me.reshape(1), even, odd)
 
 
 ROWS_ST = SLOTS * 4
@@ -393,18 +395,23 @@
 
 def on_device(visibility, coordinate, block_count, owner_index, subgrid_index, offsets,
               station_pair, screens, slot_owner):
-    near = [[k * NEAR + j for j in range(NEAR)] for k in range(FAR)]
-    far = [[k * NEAR + j for k in range(FAR)] for j in range(NEAR)]
+    near = [[k * FAR + j for k in range(NEAR)] for j in range(FAR)]
+
+    def shifted(array, shift):
+        pairs = [(k * FAR + j, k * FAR + (j + shift) % FAR) for k in range(NEAR) for j in range(FAR)]
+        return lax.ppermute(array, "uv", pairs)
 
     def exchange(array, axis, groups=None):
         return lax.all_to_all(array, axis, 0, 0, axis_index_groups=groups, tiled=True)
 
     pieces = exchange(chunk_of(screens, lax.axis_index("tm")), "uv", near)
-    pieces = exchange(pick_near(slot_owner, pieces), "uv", far)
+    piece = pick_near(slot_owner, pieces)
+    even = jnp.concatenate([piece, shifted(piece, 2)], axis=0)
+    odd = shifted(even, 1)
     sent = pack(owner_index[..., 0], subgrid_index, block_count, station_pair.swapaxes(1, 2), visibility, coordinate)
     arrived = exchange(sent, "tm")
     meta = meta_of(arrived)
-    pieces = exchange(pick_far(slot_owner, pieces), "uv", near)
+    pieces = exchange(pick_far(slot_owner, lax.axis_index("uv"), even, odd), "uv", near)
     x = grid_blocks(meta, offsets.swapaxes(1, 2), arrived)
     meta, x = lax.optimization_barrier((meta, x))
     wanted = exchange(asked(meta, pieces), "tm")

time: 98.4 us -> 94.9 us (0.964)
  blocking collectives: 35.8 us -> 19.3 us
  starting transfers between devices: 27.1 us -> 41.3 us
  Pallas kernels: 17.2 us -> 14.1 us
  waiting for transfers between devices: 14.9 us -> 18 us
  local copies, waits for them, and re-layouts: 2.66 us -> 1.43 us
    all_to_all x2 -> x1, blocking collectives: 35.8 us -> 19.3 us  [exchange(): lax.all_to_all(array, axis, 0, 0, axis_index_groups=groups, tiled=True)]
    ppermute x0 -> x2, starting transfers between devices: none -> 10.8 us  [shifted(): return lax.ppermute(array, 'uv', pairs)]
    ppermute x0 -> x2, waiting for transfers between devices: none -> 4.24 us  [shifted(): return lax.ppermute(array, 'uv', pairs)]
    pallas_call x1, Pallas kernels: 10.3 us -> 6.27 us  [grid_blocks(): pl.pallas_call(grid_kernel, out_shape=jax.ShapeDtypeStruct((SLOTS * SUBS,...]
    all_to_all x3, starting transfers between devices: 27.1 us -> 30.5 us  [exchange(): lax.all_to_all(array, axis, 0, 0, axis_index_groups=groups, tiled=True)]
    pallas_call x1, Pallas kernels: 0.07 us -> 1.57 us  [chunk_of(): pl.pallas_call(chunk_kernel, out_shape=jax.ShapeDtypeStruct((NEAR, ST_PIE...]
    unnamed x18 -> x16, local copies, waits for them, and re-layouts: 2.58 us -> 1.35 us
    all_to_all x3, waiting for transfers between devices: 14.9 us -> 13.8 us  [exchange(): lax.all_to_all(array, axis, 0, 0, axis_index_groups=groups, tiled=True)]
  transfers between devices with their start and end apart: 3 -> 5, of which waited for: 2 -> 4; matrix products, arithmetic and copies ran while one was open for 0% -> 0% of each run, Pallas kernels for 14% -> 11%
where the time goes in v5:
time: 94.9 us; the launch traced here: 94.4 us
  starting transfers between devices  41.3 us (44%)
  blocking collectives  19.3 us (20%)
  waiting for transfers between devices  18 us (19%)
  Pallas kernels  14.1 us (15%)
  local copies, waits for them, and re-layouts  1.43 us (2%)
    all_to_all x3, starting transfers between devices, exchange(): lax.all_to_all(array, axis, 0, 0, axis_index_groups=groups, tiled=True)  30.5 us
    all_to_all x1, blocking collectives, exchange(): lax.all_to_all(array, axis, 0, 0, axis_index_groups=groups, tiled=True)  19.3 us
    all_to_all x3, waiting for transfers between devices, exchange(): lax.all_to_all(array, axis, 0, 0, axis_index_groups=groups, tiled=True)  13.8 us
    ppermute x2, starting transfers between devices, shifted(): return lax.ppermute(array, 'uv', pairs)  10.8 us
    pallas_call x1, Pallas kernels, grid_blocks(): pl.pallas_call(grid_kernel, out_shape=jax.ShapeDtypeStruct((SLOTS * SUBS,...  6.27 us
    ppermute x2, waiting for transfers between devices, shifted(): return lax.ppermute(array, 'uv', pairs)  4.24 us
    pallas_call x1, Pallas kernels, pack(): pl.pallas_call(pack_kernel, out_shape=jax.ShapeDtypeStruct((PEERS, ROWS,...  2.29 us
  transfers between devices with their start and end apart: 5, of which 4 were waited for; matrix products, arithmetic and copies ran while one was open for 0% of the time, Pallas kernels for 11%

profile of v5, /device:TPU:1, one launch (start us, length us, event | category | flops | bytes accessed | tf_op | source)
XLA Modules:
  0.0 94.4 jit_solution(12357946484631601309)
XLA Ops:
  0.0 1.6 %cut_chunk.1 = bf16[16,16,128]{2,1,0:T(8,128)(2,1)} custom-call(s32[1]{0:T(128)} %bitcast.4.t_ref, bf16[1,64,8,1024]{3,2,1,0:T(8,128)(2,1)} %screens_ref.1), custom_call_target="tpu_custom_call" | custom-call | tf_op jit(solution)/shard_map/cut_chunk/pallas_call | solution.py:251
  1.6 0.0 copy-start
  1.6 0.0 copy-start.5
  1.6 0.0 copy-start.6
  1.6 19.6 %all-to-all-start.1 = ((bf16[16,16,128]{2,1,0:T(8,128)(2,1)}), bf16[16,16,128]{2,1,0:T(8,128)(2,1)S(1)}, u32[]{:S(2)}, u32[]{:S(2)}) async-start(bf16[16,16,128]{2,1,0:T(8,128)(2,1)} %cut_chunk.1), calls=%async_computation.1 | async-start | bytes 131072 | tf_op jit(solution)/shard_map/all_to_all | solution.py:405
  21.3 0.6 copy-done.3
  21.9 0.0 copy-done.4
  21.9 2.3 %pack_blocks.1 = bf16[16,64,128]{2,1,0:T(8,128)(2,1)} custom-call(s32[3,1,16]{2,1,0:T(1,128)S(1)} %bitcast.5, s32[3,1,16]{2,1,0:T(1,128)S(1)} %copy-done.4, s32[3,1,16]{2,1,0:T(1,128)S(1)} %copy-done.5, s32[1,2,4]{2,1,0:T(2,128)S(1)} %bitcast.6, bf16[3,1,16,8,128]{4,3,2,1,0:T(8,128)(2,1)S(1)} %copy-done, bf16[3,1,16,2,128]{4,3,2,1,0:T(2,128)(2,1)S(1)} %copy-done.1), custom_call_target="tpu_custom_call" | custom-call | flops 2000000 | bytes 600000 | tf_op jit(solution)/shard_map/pack_blocks/pallas_call | solution.py:106
  24.2 8.6 %all-to-all-done.1.in_ref = bf16[16,16,128]{2,1,0:T(8,128)(2,1)S(1)} async-done(((bf16[16,16,128]{2,1,0:T(8,128)(2,1)}), bf16[16,16,128]{2,1,0:T(8,128)(2,1)S(1)}, u32[]{:S(2)}, u32[]{:S(2)}) %all-to-all-start.1) | async-done | bytes 65568 | tf_op jit(solution)/shard_map/all_to_all | solution.py:405
  32.8 7.4 %all-to-all-start = ((bf16[16,64,128]{2,1,0:T(8,128)(2,1)}), bf16[16,64,128]{2,1,0:T(8,128)(2,1)S(1)}, u32[]{:S(2)}, u32[]{:S(2)}) async-start(bf16[16,64,128]{2,1,0:T(8,128)(2,1)} %pack_blocks.1), calls=%async_computation | async-start | bytes 524288 | tf_op jit(solution)/shard_map/all_to_all | solution.py:405
  40.2 0.6 pick_near.1
  40.8 6.6 %collective-permute-start = (bf16[3,16,128]{2,1,0:T(8,128)(2,1)S(1)}, bf16[3,16,128]{2,1,0:T(8,128)(2,1)S(1)}, u32[]{:S(2)}, u32[]{:S(2)}) collective-permute-start(bf16[3,16,128]{2,1,0:T(8,128)(2,1)S(1)} %pick_near.1), channel_id=1, source_target_pairs={{0,32},{16,48},{32,0},{48,16},{64,96},{80,112},{96,64},{112,80},{1... | collective-permute-start | bytes 36872 | tf_op jit(solution)/shard_map/ppermute | solution.py:402
  47.4 1.8 %collective-permute-done = bf16[3,16,128]{2,1,0:T(8,128)(2,1)S(1)} collective-permute-done((bf16[3,16,128]{2,1,0:T(8,128)(2,1)S(1)}, bf16[3,16,128]{2,1,0:T(8,128)(2,1)S(1)}, u32[]{:S(2)}, u32[]{:S(2)}) %collective-permute-start) | collective-permute-done | bytes 12320 | tf_op jit(solution)/shard_map/ppermute | solution.py:402
  49.2 4.2 %collective-permute-start.1 = (bf16[6,16,128]{2,1,0:T(8,128)(2,1)S(1)}, bf16[6,16,128]{2,1,0:T(8,128)(2,1)S(1)}, u32[]{:S(2)}, u32[]{:S(2)}) collective-permute-start(bf16[6,16,128]{2,1,0:T(8,128)(2,1)S(1)} %pad_maximum_fusion.even_ref), channel_id=1, source_target_pairs={{0,16},{16,32},{32,48},{48,0},{64,80},{80,96},{96,112},{112,64},{1... | collective-permute-start | bytes 73736 | tf_op jit(solution)/shard_map/ppermute | solution.py:402
  53.4 2.5 %collective-permute-done.1.odd_ref = bf16[6,16,128]{2,1,0:T(8,128)(2,1)S(1)} collective-permute-done((bf16[6,16,128]{2,1,0:T(8,128)(2,1)S(1)}, bf16[6,16,128]{2,1,0:T(8,128)(2,1)S(1)}, u32[]{:S(2)}, u32[]{:S(2)}) %collective-permute-start.1) | collective-permute-done | bytes 24608 | tf_op jit(solution)/shard_map/ppermute | solution.py:402
  55.8 1.3 %pick_far.1 = bf16[16,48,128]{2,1,0:T(8,128)(2,1)} custom-call(s32[3]{0:T(128)S(1)} %copy-done.2, s32[1]{0:T(128)} %bitcast.3.me, bf16[6,16,128]{2,1,0:T(8,128)(2,1)S(1)} %pad_maximum_fusion.even_ref, bf16[6,16,128]{2,1,0:T(8,128)(2,1)S(1)} %collective-permute-done.1.odd_ref), custom_call_target="tpu_custom_call" | custom-call | tf_op jit(solution)/shard_map/pick_far/pallas_call | solution.py:293
  57.1 3.5 %all-to-all-start.2 = ((bf16[16,48,128]{2,1,0:T(8,128)(2,1)}), bf16[16,48,128]{2,1,0:T(8,128)(2,1)S(1)}, u32[]{:S(2)}, u32[]{:S(2)}) async-start(bf16[16,48,128]{2,1,0:T(8,128)(2,1)} %pick_far.1), calls=%async_computation.2 | async-start | bytes 393216 | tf_op jit(solution)/shard_map/all_to_all | solution.py:405
  60.7 0.1 reshape.12.meta
  60.8 0.7 copy-done.7
  61.4 6.3 %grid_blocks.1.x_ref = f32[12,8,8,128]{3,2,1,0:T(8,128)S(1)} custom-call(s32[512]{0:T(512)S(1)} %reshape.12.meta, s32[1,2,4]{2,1,0:T(2,128)S(1)} %bitcast.7, bf16[16,64,128]{2,1,0:T(8,128)(2,1)S(1)} %all-to-all-done.rows_ref), custom_call_target="tpu_custom_call" | custom-call | flops 800000000 | bytes 800000 | tf_op jit(solution)/shard_map/grid_blocks/pallas_call | solution.py:214
  67.7 5.2 %all-to-all-done.2.in_ref = bf16[16,48,128]{2,1,0:T(8,128)(2,1)S(1)} async-done(((bf16[16,48,128]{2,1,0:T(8,128)(2,1)}), bf16[16,48,128]{2,1,0:T(8,128)(2,1)S(1)}, u32[]{:S(2)}, u32[]{:S(2)}) %all-to-all-start.2) | async-done | bytes 196640 | tf_op jit(solution)/shard_map/all_to_all | solution.py:405
  72.9 0.9 asked_stations.1
  73.8 19.3 %all_to_all.20.in_ref = bf16[16,96,128]{2,1,0:T(8,128)(2,1)S(1)} all-to-all(bf16[16,96,128]{2,1,0:T(8,128)(2,1)S(1)} %asked_stations.1), channel_id=1, replica_groups=mesh['uv'=64,'tm'=16] {'tm'}, dimensions={0} | all-to-all | bytes 786432 | tf_op jit(solution)/shard_map/all_to_all | solution.py:405
  93.2 1.2 %screen_product.1 = f32[1,4,8,1024]{3,2,1,0:T(8,128)} custom-call(f32[12,8,8,128]{3,2,1,0:T(8,128)S(1)} %grid_blocks.1.x_ref, bf16[16,96,128]{2,1,0:T(8,128)(2,1)S(1)} %all_to_all.20.in_ref), custom_call_target="tpu_custom_call" | custom-call | flops 3000000 | bytes 1000000 | tf_op jit(solution)/shard_map/screen_product/pallas_call | solution.py:376
  (13 shorter events, 0.1 us)
Async XLA Ops:
  1.6 19.6 %copy-start = (bf16[3,1,16,8,128]{4,3,2,1,0:T(8,128)(2,1)S(1)}, bf16[3,1,16,8,128]{4,3,2,1,0:T(8,128)(2,1)}, u32[]{:S(2)}) copy-start(bf16[3,1,16,8,128]{4,3,2,1,0:T(8,128)(2,1)} %vis_ref.1) | copy-start | bytes 294916
  1.6 19.6 %copy-start.1 = (bf16[3,1,16,2,128]{4,3,2,1,0:T(2,128)(2,1)S(1)}, bf16[3,1,16,2,128]{4,3,2,1,0:T(2,128)(2,1)}, u32[]{:S(2)}) copy-start(bf16[3,1,16,2,128]{4,3,2,1,0:T(2,128)(2,1)} %coord_ref.1) | copy-start | bytes 73732
  1.6 19.6 %copy-start.5 = (s32[3,1,16]{2,1,0:T(1,128)S(1)}, s32[3,1,16]{2,1,0:T(1,128)}, u32[]{:S(2)}) copy-start(s32[3,1,16]{2,1,0:T(1,128)} %counts.1) | copy-start | bytes 580
  1.6 19.6 %copy-start.6 = (s32[1,4,2]{1,2,0:T(2,128)S(1)}, s32[1,4,2]{1,2,0:T(2,128)}, u32[]{:S(2)}) copy-start(s32[1,4,2]{1,2,0:T(2,128)} %param.15) | copy-start | bytes 100
  1.6 31.1 %all-to-all-start.1 = ((bf16[16,16,128]{2,1,0:T(8,128)(2,1)}), bf16[16,16,128]{2,1,0:T(8,128)(2,1)S(1)}, u32[]{:S(2)}, u32[]{:S(2)}) async-start(bf16[16,16,128]{2,1,0:T(8,128)(2,1)} %cut_chunk.1), calls=%async_computation.1 | async-start | bytes 131072 | tf_op jit(solution)/shard_map/all_to_all | solution.py:405
  21.2 0.7 copy-start.3
  21.2 0.7 copy-start.4
  24.2 16.0 %copy-start.2 = (s32[3]{0:T(128)S(1)}, s32[3]{0:T(128)}, u32[]{:S(2)}) copy-start(s32[3]{0:T(128)} %roots.3) | copy-start | bytes 40
  32.8 24.3 %all-to-all-start = ((bf16[16,64,128]{2,1,0:T(8,128)(2,1)}), bf16[16,64,128]{2,1,0:T(8,128)(2,1)S(1)}, u32[]{:S(2)}, u32[]{:S(2)}) async-start(bf16[16,64,128]{2,1,0:T(8,128)(2,1)} %pack_blocks.1), calls=%async_computation | async-start | bytes 524288 | tf_op jit(solution)/shard_map/all_to_all | solution.py:405
  40.8 8.4 %collective-permute-start = (bf16[3,16,128]{2,1,0:T(8,128)(2,1)S(1)}, bf16[3,16,128]{2,1,0:T(8,128)(2,1)S(1)}, u32[]{:S(2)}, u32[]{:S(2)}) collective-permute-start(bf16[3,16,128]{2,1,0:T(8,128)(2,1)S(1)} %pick_near.1), channel_id=1, source_target_pairs={{0,32},{16,48},{32,0},{48,16},{64,96},{80,112},{96,64},{112,80},{1... | collective-permute-start | bytes 36872 | tf_op jit(solution)/shard_map/ppermute | solution.py:402
  49.2 6.7 %collective-permute-start.1 = (bf16[6,16,128]{2,1,0:T(8,128)(2,1)S(1)}, bf16[6,16,128]{2,1,0:T(8,128)(2,1)S(1)}, u32[]{:S(2)}, u32[]{:S(2)}) collective-permute-start(bf16[6,16,128]{2,1,0:T(8,128)(2,1)S(1)} %pad_maximum_fusion.even_ref), channel_id=1, source_target_pairs={{0,16},{16,32},{32,48},{48,0},{64,80},{80,96},{96,112},{112,64},{1... | collective-permute-start | bytes 73736 | tf_op jit(solution)/shard_map/ppermute | solution.py:402
  57.1 15.8 %all-to-all-start.2 = ((bf16[16,48,128]{2,1,0:T(8,128)(2,1)}), bf16[16,48,128]{2,1,0:T(8,128)(2,1)S(1)}, u32[]{:S(2)}, u32[]{:S(2)}) async-start(bf16[16,48,128]{2,1,0:T(8,128)(2,1)} %pick_far.1), calls=%async_computation.2 | async-start | bytes 393216 | tf_op jit(solution)/shard_map/all_to_all | solution.py:405
  60.8 0.7 copy-start.7

commit v6 on v5

--- a/solution.py
+++ b/solution.py
@@ -21,12 +21,12 @@
 F32 = jnp.float32
 BF16 = jnp.bfloat16
 
-ROWS = 64
-U_ROW = PER * 8
-V_ROW = U_ROW + PER
-META_ROW = V_ROW + PER
-META = 32
-PAIR_LANE = 16
+TOTAL = SLOTS * BLOCKS
+U_ROW = TOTAL * 8
+V_ROW = U_ROW + TOTAL
+META_ROW = V_ROW + TOTAL
+ROWS = META_ROW + 16
+META = 64
 
 COS_POLY = (1.0, -19.73920440673828, 64.93911743164062, -85.45014190673828, 60.167633056640625,
             -25.967601776123047, 6.528658866882324)
@@ -63,52 +63,41 @@
     return a[0] * b[0] - a[1] * b[1], a[0] * b[1] + a[1] * b[0]
 
 
-def pack_kernel(owners, subs, counts, pair, vis_ref, coord_ref, out_ref, taken, stage):
+def pack_kernel(owners, subs, counts, pair, vis_ref, coord_ref, out_ref, stage):
     lane = lax.broadcasted_iota(jnp.int32, (1, LANES), 1)
     pairs = jnp.zeros((1, LANES), F32)
     for j in range(REQS):
-        pairs = jnp.where(lane == PAIR_LANE + j, pair[0, j % 2, j // 2].astype(F32), pairs)
-    last = lax.broadcasted_iota(jnp.int32, (8, LANES), 0) == META_ROW % 8
-    last = jnp.where(last, pairs, 0.0)
-
-    @pl.loop(0, PEERS)
-    def _(o):
-        stage[o, 0:ROWS - 16, :] = jnp.zeros((ROWS - 16, LANES), F32)
-        for half in (16, 8):
-            first = ROWS - half
-            stage[o, first:first + 8, :] = last if META_ROW // 8 * 8 == first else jnp.zeros_like(last)
-
+        pairs = jnp.where(lane == j, pair[0, j % 2, j // 2].astype(F32), pairs)
+    stage[META_ROW - U_ROW:, :] = jnp.zeros((16, LANES), F32)
+    owner_row, sub_row = jnp.zeros((1, LANES), F32), jnp.zeros((1, LANES), F32)
     for slot in range(SLOTS):
-        for o in range(PEERS):
-            taken[o] = 0
-
-        @pl.loop(0, BLOCKS)
-        def _(i):
-            owner = owners[slot, 0, i]
-            rank = taken[owner]
-            taken[owner] = rank + 1
-            k = slot * CAP + rank
-            values = vis_ref[slot, 0, i].astype(F32)
-            values = jnp.where(lane < counts[slot, 0, i], values, 0.0)
-            stage[owner, pl.ds(pl.multiple_of(k * 8, 8), 8), :] = values
-            where = coord_ref[slot, 0, i].astype(F32)
-            stage[owner, pl.ds(U_ROW + k, 1), :] = where[0:1]
-            stage[owner, pl.ds(V_ROW + k, 1), :] = where[1:2]
-            meta = jnp.where(lane == 2 * k, subs[slot, 0, i].astype(F32), jnp.where(lane == 2 * k + 1, 1.0, 0.0))
-            stage[owner, META_ROW:META_ROW + 1, :] += meta
-
-    @pl.loop(0, PEERS)
-    def _(o):
-        out_ref[o] = stage[o].astype(BF16)
+        for i in range(0, BLOCKS, 2):
+            two = []
+            for k in (i, i + 1):
+                spot = slot * BLOCKS + k
+                values = vis_ref[slot, 0, k].astype(F32)
+                two.append(jnp.where(lane < counts[slot, 0, k], values, 0.0))
+                where = coord_ref[slot, 0, k].astype(F32)
+                stage[spot:spot + 1, :] = where[0:1]
+                stage[TOTAL + spot:TOTAL + spot + 1, :] = where[1:2]
+                owner_row = jnp.where(lane == spot, owners[slot, 0, k].astype(F32), owner_row)
+                sub_row = jnp.where(lane == spot, subs[slot, 0, k].astype(F32), sub_row)
+            first = (slot * BLOCKS + i) * 8
+            out_ref[first:first + 16, :] = jnp.concatenate(two, axis=0).astype(BF16)
+    first = META_ROW - U_ROW
+    stage[first:first + 1, :] = owner_row
+    stage[first + 1:first + 2, :] = sub_row
+    stage[first + 2:first + 3, :] = pairs
+    out_ref[U_ROW:, :] = stage[...].astype(BF16)
 
 
 def pack(owners, subs, counts, pair, visibility, coordinate, **kw):
     return pl.pallas_call(
         pack_kernel,
-        out_shape=jax.ShapeDtypeStruct((PEERS, ROWS, LANES), BF16),
+        out_shape=jax.ShapeDtypeStruct((ROWS, LANES), BF16),
         in_specs=[smem()] * 4 + [vmem(), vmem()],
         out_specs=vmem(),
-        scratch_shapes=[pltpu.SMEM((PEERS,), jnp.int32), pltpu.VMEM((PEERS, ROWS, LANES), F32)],
+        scratch_shapes=[pltpu.VMEM((ROWS - U_ROW, LANES), F32)],
         name="pack_blocks",
         cost_estimate=pl.CostEstimate(flops=2000000, bytes_accessed=600000, transcendentals=0),
         compiler_params=room(),
@@ -135,27 +124,23 @@
 BATCH = 4
 
 
-def grid_kernel(meta, offs, rows_ref, x_ref, acc, coords, order, bucket):
+def grid_kernel(me, meta, offs, rows_ref, x_ref, acc, coords, order, bucket):
     acc[...] = jnp.zeros_like(acc)
     for t in range(PEERS):
-        coords[t] = rows_ref[t, ROWS - 16:ROWS, :].astype(F32)
-
-    def gather(t, carry):
-        count, spare = carry
-        for k in range(PER):
-            b = t * PER + k
-            sub = meta[t * META + 2 * k]
-            live = meta[t * META + 2 * k + 1]
-            order[count] = b
-            bucket[count] = (k // CAP) * SUBS + sub
-            spare = jnp.where(live == 0, b, spare)
-            count = count + live
-        return count, spare
-
-    count, spare = lax.fori_loop(0, PEERS, gather, (jnp.int32(0), jnp.int32(0)))
-    for j in range(BATCH):
-        order[count + j] = spare
-        bucket[count + j] = 0
+        coords[t] = rows_ref[t, U_ROW:META_ROW, :].astype(F32)
+    for j in range(PEERS * PER + BATCH):
+        order[j] = 0
+        bucket[j] = 0
+
+    def gather(t, count):
+        for i in range(TOTAL):
+            first = t * (3 * META) + i
+            order[count] = t * TOTAL + i
+            bucket[count] = (i // BLOCKS) * SUBS + meta[first + META]
+            count = count + (meta[first] == me[0]).astype(jnp.int32)
+        return count
+
+    count = lax.fori_loop(0, PEERS, gather, jnp.int32(0))
 
     sublane = lax.broadcasted_iota(jnp.int32, (8, LANES), 0).astype(F32)
     seed_l = (sublane * 4.0 - 16.0) * (1.0 / SIDE)
@@ -167,12 +152,13 @@
             b = order[step * BATCH + j]
             key = bucket[step * BATCH + j]
             sub = key % SUBS
-            t = b // PER
-            k = b % PER
-            tile = rows_ref[t, pl.ds(pl.multiple_of(k // CAP * 16, 16), 16), :].astype(F32)
-            tile = jnp.where(k % CAP == 0, tile[0:8], tile[8:16])
-            u = coords[t, pl.ds(U_ROW - (ROWS - 16) + k, 1), :]
-            v = coords[t, pl.ds(V_ROW - (ROWS - 16) + k, 1), :]
+            t = b // TOTAL
+            k = b % TOTAL
+            tile = rows_ref[t, pl.ds(pl.multiple_of(k // 2 * 16, 16), 16), :].astype(F32)
+            tile = jnp.where(k % 2 == 0, tile[0:8], tile[8:16])
+            tile = jnp.where(step * BATCH + j < count, tile, 0.0)
+            u = coords[t, pl.ds(k, 1), :]
+            v = coords[t, pl.ds(TOTAL + k, 1), :]
             du = jnp.broadcast_to(u - offs[0, 0, sub].astype(F32), (8, LANES))
             dv = jnp.broadcast_to(v - offs[0, 1, sub].astype(F32), (8, LANES))
             turn_l = cis(du * (1.0 / SIDE))
@@ -210,15 +196,15 @@
                 x_ref[key, 4 * part + p] = plane
 
 
-def grid_blocks(meta, offs, rows, **kw):
+def grid_blocks(me, meta, offs, rows, **kw):
     return pl.pallas_call(
         grid_kernel,
         out_shape=jax.ShapeDtypeStruct((SLOTS * SUBS, 8, 8, LANES), F32),
-        in_specs=[smem(), smem(), vmem()],
+        in_specs=[smem(), smem(), smem(), vmem()],
         out_specs=vmem(),
         scratch_shapes=[
             pltpu.VMEM((SLOTS * SUBS, 2 * SIDE, 8 * SIDE), F32),
-            pltpu.VMEM((PEERS, 16, LANES), F32),
+            pltpu.VMEM((PEERS, 2 * TOTAL, LANES), F32),
             pltpu.SMEM((PEERS * PER + BATCH,), jnp.int32),
             pltpu.SMEM((PEERS * PER + BATCH,), jnp.int32),
         ],
@@ -226,14 +212,20 @@
         cost_estimate=pl.CostEstimate(flops=800000000, bytes_accessed=800000, transcendentals=0),
         compiler_params=room(),
         **kw,
-    )(meta, offs, rows)
+    )(me.reshape(1), meta, offs, rows)
+
+
+COPIES = 4
 
 
 def chunk_kernel(t_ref, screens_ref, out_ref, in_ref, arrived):
     lanes = pl.ds(pl.multiple_of(t_ref[0] // 2 * LANES, LANES), LANES)
-    copy = pltpu.make_async_copy(screens_ref.at[0, :, :, lanes], in_ref, arrived)
-    copy.start()
-    copy.wait()
+    share = STATIONS // COPIES
+    copies = []
+    for c in range(COPIES):
+        some = pl.ds(c * share, share)
+        copies.append(pltpu.make_async_copy(screens_ref.at[0, some, :, lanes], in_ref.at[some], arrived.at[c]))
+        copies[-1].start()
     odd = t_ref[0] % 2 == 1
     low = lax.broadcasted_iota(jnp.int32, (8, LANES), 0) < 4
 
@@ -244,6 +236,8 @@
 
     for j in range(NEAR):
         first = j * ST_PIECE
+        if first % share == 0:
+            copies[first // share].wait()
         out_ref[j] = jnp.concatenate([two(first, first + 1), two(first + 2, first + 3)], axis=0).astype(BF16)
 
 
@@ -253,7 +247,7 @@
         out_shape=jax.ShapeDtypeStruct((NEAR, ST_PIECE * 4, LANES), BF16),
         in_specs=[smem(), pl.BlockSpec(memory_space=pltpu.HBM)],
         out_specs=vmem(),
-        scratch_shapes=[pltpu.VMEM((STATIONS, 8, LANES), BF16), pltpu.SemaphoreType.DMA],
+        scratch_shapes=[pltpu.VMEM((STATIONS, 8, LANES), BF16), pltpu.SemaphoreType.DMA((COPIES,))],
         name="cut_chunk",
         **kw,
     )(t.reshape(1), screens)
@@ -313,7 +307,7 @@
     @pl.loop(0, PEERS)
     def _(t):
         for r in range(REQS):
-            station = meta[t * META + PAIR_LANE + r]
+            station = meta[t * (3 * META) + 2 * META + r]
             stage[ROWS_ST * r:ROWS_ST * (r + 1), :] = table[station, 0:ROWS_ST, :]
         out_ref[t] = stage[...].astype(BF16)
 
@@ -390,7 +384,7 @@
 
 
 def meta_of(arrived):
-    return arrived[:, META_ROW, :META].astype(jnp.int32).reshape(-1)
+    return arrived[:, META_ROW:META_ROW + 3, :META].astype(jnp.int32).reshape(-1)
 
 
 def on_device(visibility, coordinate, block_count, owner_index, subgrid_index, offsets,
@@ -405,14 +399,14 @@
         return lax.all_to_all(array, axis, 0, 0, axis_index_groups=groups, tiled=True)
 
     pieces = exchange(chunk_of(screens, lax.axis_index("tm")), "uv", near)
+    sent = pack(owner_index[..., 0], subgrid_index, block_count, station_pair.swapaxes(1, 2), visibility, coordinate)
     piece = pick_near(slot_owner, pieces)
     even = jnp.concatenate([piece, shifted(piece, 2)], axis=0)
     odd = shifted(even, 1)
-    sent = pack(owner_index[..., 0], subgrid_index, block_count, station_pair.swapaxes(1, 2), visibility, coordinate)
-    arrived = exchange(sent, "tm")
+    arrived = lax.all_gather(sent, "tm")
     meta = meta_of(arrived)
     pieces = exchange(pick_far(slot_owner, lax.axis_index("uv"), even, odd), "uv", near)
-    x = grid_blocks(meta, offsets.swapaxes(1, 2), arrived)
+    x = grid_blocks(lax.axis_index("tm"), meta, offsets.swapaxes(1, 2), arrived)
     meta, x = lax.optimization_barrier((meta, x))
     wanted = exchange(asked(meta, pieces), "tm")
     return screen_product(x, wanted)

time: 94.9 us -> 108 us (1.14)
  blocking collectives: 19.3 us -> 49.8 us
  starting transfers between devices: 41.3 us -> 15 us
  between operations: 0.16 us -> 13.5 us
  waiting for transfers between devices: 18 us -> 5.24 us
  local copies, waits for them, and re-layouts: 1.43 us -> 7.32 us
  Pallas kernels: 14.1 us -> 15.6 us
    all_to_all x1 -> x2, blocking collectives: 19.3 us -> 49.8 us  [exchange(): lax.all_to_all(array, axis, 0, 0, axis_index_groups=groups, tiled=True)]
    all_to_all x3 -> x1, starting transfers between devices: 30.5 us -> 3.52 us  [exchange(): lax.all_to_all(array, axis, 0, 0, axis_index_groups=groups, tiled=True)]
    all_to_all x3 -> x1, waiting for transfers between devices: 13.8 us -> 1.18 us  [exchange(): lax.all_to_all(array, axis, 0, 0, axis_index_groups=groups, tiled=True)]
    unnamed x16 -> x20, local copies, waits for them, and re-layouts: 1.35 us -> 7.24 us
    pallas_call x1, Pallas kernels: 6.27 us -> 8.67 us  [grid_blocks(): pl.pallas_call(grid_kernel, out_shape=jax.ShapeDtypeStruct((SLOTS * SUBS,...]
  transfers between devices with their start and end apart: 5 -> 4, of which waited for: 4 -> 3; matrix products, arithmetic and copies ran while one was open for 0% -> 1% of each run, Pallas kernels for 11% -> 11%
where the time goes in v6:
time: 108 us; the launch traced here: 107 us
  blocking collectives  49.8 us (46%)
  Pallas kernels  15.6 us (14%)
  starting transfers between devices  15 us (14%)
  between operations  13.5 us (12%)
  local copies, waits for them, and re-layouts  7.32 us (7%)
  waiting for transfers between devices  5.24 us (5%)
    all_to_all x2, blocking collectives, exchange(): lax.all_to_all(array, axis, 0, 0, axis_index_groups=groups, tiled=True)  49.8 us
    ppermute x2, starting transfers between devices, shifted(): return lax.ppermute(array, 'uv', pairs)  11.5 us
    pallas_call x1, Pallas kernels, grid_blocks(): pl.pallas_call(grid_kernel, out_shape=jax.ShapeDtypeStruct((SLOTS * SUBS,...  8.67 us
    unnamed x20, local copies, waits for them, and re-layouts  7.24 us
    ppermute x2, waiting for transfers between devices, shifted(): return lax.ppermute(array, 'uv', pairs)  4.03 us
    all_to_all x1, starting transfers between devices, exchange(): lax.all_to_all(array, axis, 0, 0, axis_index_groups=groups, tiled=True)  3.52 us
  transfers between devices with their start and end apart: 4, of which 3 were waited for; matrix products, arithmetic and copies ran while one was open for 1% of the time, Pallas kernels for 11%

profile of v6, /device:TPU:1, one launch (start us, length us, event | category | flops | bytes accessed | tf_op | source)
XLA Modules:
  0.0 107.3 jit_solution(7758945224847770625)
XLA Ops:
  6.5 0.9 copy-done
  7.4 0.7 copy-done.1
  8.2 0.7 copy-done.4
  8.9 0.7 copy-done.5
  9.5 0.7 copy-done.6
  10.2 0.7 copy-done.7
  10.9 1.3 %pack_blocks.1 = bf16[496,128]{1,0:T(8,128)(2,1)} custom-call(s32[3,1,16]{2,1,0:T(1,128)S(1)} %bitcast.6, s32[3,1,16]{2,1,0:T(1,128)S(1)} %copy-done.5, s32[3,1,16]{2,1,0:T(1,128)S(1)} %copy-done.6, s32[1,2,4]{2,1,0:T(2,128)S(1)} %bitcast.7, bf16[3,1,16,8,128]{4,3,2,1,0:T(8,128)(2,1)S(1)} %copy-done, bf16[3,1,16,2,128]{4,3,2,1,0:T(2,128)(2,1)S(1)} %copy-done.1), custom_call_target="tpu_custom_call" | custom-call | flops 2000000 | bytes 600000 | tf_op jit(solution)/shard_map/pack_blocks/pallas_call | solution.py:95
  12.3 1.5 %cut_chunk.1 = bf16[16,16,128]{2,1,0:T(8,128)(2,1)} custom-call(s32[1]{0:T(128)} %bitcast.3.me.t_ref, bf16[1,64,8,1024]{3,2,1,0:T(8,128)(2,1)} %screens_ref.1), custom_call_target="tpu_custom_call" | custom-call | tf_op jit(solution)/shard_map/cut_chunk/pallas_call | solution.py:245
  13.8 31.0 %all_to_all.15.in_ref = bf16[16,16,128]{2,1,0:T(8,128)(2,1)S(1)} all-to-all(bf16[16,16,128]{2,1,0:T(8,128)(2,1)} %cut_chunk.1), channel_id=1, replica_groups={{0,64,128,192,256,320,384,448,512,576,640,704,768,832,896,960},{16,80,1..., dimensions={0} | all-to-all | bytes 131072 | tf_op jit(solution)/shard_map/all_to_all | solution.py:399
  44.8 0.7 copy-done.2
  46.0 7.5 %collective-permute-start = (bf16[3,16,128]{2,1,0:T(8,128)(2,1)S(1)}, bf16[3,16,128]{2,1,0:T(8,128)(2,1)S(1)}, u32[]{:S(2)}, u32[]{:S(2)}) collective-permute-start(bf16[3,16,128]{2,1,0:T(8,128)(2,1)S(1)} %pick_near.1), channel_id=1, source_target_pairs={{0,32},{16,48},{32,0},{48,16},{64,96},{80,112},{96,64},{112,80},{1... | collective-permute-start | bytes 36872 | tf_op jit(solution)/shard_map/ppermute | solution.py:396
  53.5 1.1 %collective-permute-done = bf16[3,16,128]{2,1,0:T(8,128)(2,1)S(1)} collective-permute-done((bf16[3,16,128]{2,1,0:T(8,128)(2,1)S(1)}, bf16[3,16,128]{2,1,0:T(8,128)(2,1)S(1)}, u32[]{:S(2)}, u32[]{:S(2)}) %collective-permute-start) | collective-permute-done | bytes 12320 | tf_op jit(solution)/shard_map/ppermute | solution.py:396
  54.6 4.1 %collective-permute-start.1 = (bf16[6,16,128]{2,1,0:T(8,128)(2,1)S(1)}, bf16[6,16,128]{2,1,0:T(8,128)(2,1)S(1)}, u32[]{:S(2)}, u32[]{:S(2)}) collective-permute-start(bf16[6,16,128]{2,1,0:T(8,128)(2,1)S(1)} %pad_maximum_fusion.even_ref), channel_id=1, source_target_pairs={{0,16},{16,32},{32,48},{48,0},{64,80},{80,96},{96,112},{112,64},{1... | collective-permute-start | bytes 73736 | tf_op jit(solution)/shard_map/ppermute | solution.py:396
  58.7 2.9 %collective-permute-done.1.odd_ref = bf16[6,16,128]{2,1,0:T(8,128)(2,1)S(1)} collective-permute-done((bf16[6,16,128]{2,1,0:T(8,128)(2,1)S(1)}, bf16[6,16,128]{2,1,0:T(8,128)(2,1)S(1)}, u32[]{:S(2)}, u32[]{:S(2)}) %collective-permute-start.1) | collective-permute-done | bytes 24608 | tf_op jit(solution)/shard_map/ppermute | solution.py:396
  61.6 0.7 copy-done.3
  62.2 1.3 %pick_far.1 = bf16[16,48,128]{2,1,0:T(8,128)(2,1)} custom-call(s32[3]{0:T(128)S(1)} %copy-done.3, s32[1]{0:T(128)} %bitcast.5.me, bf16[6,16,128]{2,1,0:T(8,128)(2,1)S(1)} %pad_maximum_fusion.even_ref, bf16[6,16,128]{2,1,0:T(8,128)(2,1)S(1)} %collective-permute-done.1.odd_ref), custom_call_target="tpu_custom_call" | custom-call | tf_op jit(solution)/shard_map/pick_far/pallas_call | solution.py:287
  63.5 3.5 %all-to-all-start.1 = ((bf16[16,48,128]{2,1,0:T(8,128)(2,1)}), bf16[16,48,128]{2,1,0:T(8,128)(2,1)S(1)}, u32[]{:S(2)}, u32[]{:S(2)}) async-start(bf16[16,48,128]{2,1,0:T(8,128)(2,1)} %pick_far.1), calls=%async_computation.1 | async-start | bytes 393216 | tf_op jit(solution)/shard_map/all_to_all | solution.py:399
  67.0 0.8 slice_convert_fusion
  67.9 1.6 %copy-done.8 = bf16[7936,128]{1,0:T(8,128)(2,1)S(1)} copy-done((bf16[7936,128]{1,0:T(8,128)(2,1)S(1)}, bf16[7936,128]{1,0:T(8,128)(2,1)}, u32[]{:S(2)}) %copy-start.8) | copy-done | bytes 2031640
  69.5 8.7 %grid_blocks.1.x_ref = f32[12,8,8,128]{3,2,1,0:T(8,128)S(1)} custom-call(s32[1]{0:T(128)} %bitcast.3.me.t_ref, s32[3072]{0:T(1024)S(1)} %reshape.17.meta, s32[1,2,4]{2,1,0:T(2,128)S(1)} %bitcast.10, bf16[16,496,128]{2,1,0:T(8,128)(2,1)S(1)} %bitcast.9), custom_call_target="tpu_custom_call" | custom-call | flops 800000000 | bytes 800000 | tf_op jit(solution)/shard_map/grid_blocks/pallas_call | solution.py:200
  78.1 1.2 %all-to-all-done.1.in_ref = bf16[16,48,128]{2,1,0:T(8,128)(2,1)S(1)} async-done(((bf16[16,48,128]{2,1,0:T(8,128)(2,1)}), bf16[16,48,128]{2,1,0:T(8,128)(2,1)S(1)}, u32[]{:S(2)}, u32[]{:S(2)}) %all-to-all-start.1) | async-done | bytes 196640 | tf_op jit(solution)/shard_map/all_to_all | solution.py:399
  79.3 1.1 asked_stations.1
  80.4 18.9 %all_to_all.16.in_ref = bf16[16,96,128]{2,1,0:T(8,128)(2,1)S(1)} all-to-all(bf16[16,96,128]{2,1,0:T(8,128)(2,1)S(1)} %asked_stations.1), channel_id=1, replica_groups=mesh['uv'=64,'tm'=16] {'tm'}, dimensions={0} | all-to-all | bytes 786432 | tf_op jit(solution)/shard_map/all_to_all | solution.py:399
  99.2 1.2 %screen_product.1 = f32[1,4,8,1024]{3,2,1,0:T(8,128)} custom-call(f32[12,8,8,128]{3,2,1,0:T(8,128)S(1)} %grid_blocks.1.x_ref, bf16[16,96,128]{2,1,0:T(8,128)(2,1)S(1)} %all_to_all.16.in_ref), custom_call_target="tpu_custom_call" | custom-call | flops 3000000 | bytes 1000000 | tf_op jit(solution)/shard_map/screen_product/pallas_call | solution.py:370
  (17 shorter events, 0.7 us)
Async XLA Ops:
  6.5 61.4 %copy-start.9 = (s32[1,4,2]{1,2,0:T(2,128)S(1)}, s32[1,4,2]{1,2,0:T(2,128)}, u32[]{:S(2)}) copy-start(s32[1,4,2]{1,2,0:T(2,128)} %param.14) | copy-start | bytes 100
  6.5 60.5 %all-gather.3.cloned.1.call-start = ((), (), s32[]{:S(2)}) async-start(), calls=%async_computation.3 | async-start | bytes 2158592 | tf_op jit(solution)/shard_map/all_gather | solution.py:406
  6.5 0.9 copy-start
  7.4 0.7 copy-start.1
  8.2 0.7 copy-start.4
  8.9 0.7 copy-start.5
  9.5 0.7 copy-start.6
  10.2 0.7 copy-start.7
  44.8 0.7 copy-start.2
  46.0 8.6 %collective-permute-start = (bf16[3,16,128]{2,1,0:T(8,128)(2,1)S(1)}, bf16[3,16,128]{2,1,0:T(8,128)(2,1)S(1)}, u32[]{:S(2)}, u32[]{:S(2)}) collective-permute-start(bf16[3,16,128]{2,1,0:T(8,128)(2,1)S(1)} %pick_near.1), channel_id=1, source_target_pairs={{0,32},{16,48},{32,0},{48,16},{64,96},{80,112},{96,64},{112,80},{1... | collective-permute-start | bytes 36872 | tf_op jit(solution)/shard_map/ppermute | solution.py:396
  54.6 7.0 %collective-permute-start.1 = (bf16[6,16,128]{2,1,0:T(8,128)(2,1)S(1)}, bf16[6,16,128]{2,1,0:T(8,128)(2,1)S(1)}, u32[]{:S(2)}, u32[]{:S(2)}) collective-permute-start(bf16[6,16,128]{2,1,0:T(8,128)(2,1)S(1)} %pad_maximum_fusion.even_ref), channel_id=1, source_target_pairs={{0,16},{16,32},{32,48},{48,0},{64,80},{80,96},{96,112},{112,64},{1... | collective-permute-start | bytes 73736 | tf_op jit(solution)/shard_map/ppermute | solution.py:396
  61.6 0.7 copy-start.3
  63.5 15.8 %all-to-all-start.1 = ((bf16[16,48,128]{2,1,0:T(8,128)(2,1)}), bf16[16,48,128]{2,1,0:T(8,128)(2,1)S(1)}, u32[]{:S(2)}, u32[]{:S(2)}) async-start(bf16[16,48,128]{2,1,0:T(8,128)(2,1)} %pick_far.1), calls=%async_computation.1 | async-start | bytes 393216 | tf_op jit(solution)/shard_map/all_to_all | solution.py:399
  67.9 1.6 %copy-start.8 = (bf16[7936,128]{1,0:T(8,128)(2,1)S(1)}, bf16[7936,128]{1,0:T(8,128)(2,1)}, u32[]{:S(2)}) copy-start(bf16[7936,128]{1,0:T(8,128)(2,1)} %all-gather.3.cloned.1.call-done) | copy-start | bytes 6094852
Sparse Core Ops, SparseCore 0:
  12.4 53.5 all-gather.2

commit v7 on v4

--- a/solution.py
+++ b/solution.py
@@ -229,39 +229,48 @@
     )(meta, offs, rows)
 
 
-def chunk_kernel(t_ref, in_ref, out_ref):
-    odd = t_ref[0] % 2 == 1
+COPIES = 4
+
+
+def chunk_kernel(screens_ref, out_ref, in_ref, arrived):
+    t = lax.axis_index("tm")
+    lanes = pl.ds(pl.multiple_of(t // 2 * LANES, LANES), LANES)
+    share = STATIONS // COPIES
+    copies = []
+    for c in range(COPIES):
+        some = pl.ds(c * share, share)
+        copies.append(pltpu.make_async_copy(screens_ref.at[0, some, :, lanes], in_ref.at[some], arrived.at[c]))
+        copies[-1].start()
+    odd = t % 2 == 1
     low = lax.broadcasted_iota(jnp.int32, (8, LANES), 0) < 4
 
     def two(first, second):
-        a, b = in_ref[0, first].astype(F32), in_ref[0, second].astype(F32)
+        a, b = in_ref[first].astype(F32), in_ref[second].astype(F32)
         a, b = jnp.where(odd, pltpu.roll(a, 4, 0), a), jnp.where(odd, b, pltpu.roll(b, 4, 0))
         return jnp.where(low, a, b)
 
     for j in range(NEAR):
         first = j * ST_PIECE
+        if first % share == 0:
+            copies[first // share].wait()
         out_ref[j] = jnp.concatenate([two(first, first + 1), two(first + 2, first + 3)], axis=0).astype(BF16)
 
 
-def chunk_of(screens, t, **kw):
+def chunk_of(screens, **kw):
     return pl.pallas_call(
         chunk_kernel,
         out_shape=jax.ShapeDtypeStruct((NEAR, ST_PIECE * 4, LANES), BF16),
-        grid_spec=pltpu.PrefetchScalarGridSpec(
-            num_scalar_prefetch=1,
-            grid=(1,),
-            in_specs=[pl.BlockSpec((1, STATIONS, 8, LANES), lambda i, t: (0, 0, 0, t[0] // 2))],
-            out_specs=pl.BlockSpec((NEAR, ST_PIECE * 4, LANES), lambda i, t: (0, 0, 0)),
-        ),
+        in_specs=[pl.BlockSpec(memory_space=pltpu.HBM)],
+        out_specs=vmem(),
+        scratch_shapes=[pltpu.VMEM((STATIONS, 8, LANES), BF16), pltpu.SemaphoreType.DMA((COPIES,))],
         name="cut_chunk",
-        compiler_params=room(),
-        **kw,
-    )(t.reshape(1), screens)
+        **kw,
+    )(screens)
 
 
 def pick_near_kernel(roots, in_ref, out_ref):
     for s in range(SLOTS):
-        piece = in_ref[roots[s] % NEAR]
+        piece = in_ref[roots[s] // FAR]
         for k in range(FAR):
             out_ref[k, s] = piece
 
@@ -279,7 +288,7 @@
 
 
 def pick_far_kernel(roots, in_ref, out_ref):
-    pieces = [in_ref[roots[s] // NEAR, s].astype(F32) for s in range(SLOTS)]
+    pieces = [in_ref[roots[s] % FAR, s].astype(F32) for s in range(SLOTS)]
     rows = jnp.concatenate(
         [pieces[s][4 * i:4 * i + 4] for i in range(ST_PIECE) for s in range(SLOTS)], axis=0
     ).astype(BF16)
@@ -393,15 +402,17 @@
 
 def on_device(visibility, coordinate, block_count, owner_index, subgrid_index, offsets,
               station_pair, screens, slot_owner):
-    near = [[k * NEAR + j for j in range(NEAR)] for k in range(FAR)]
-    far = [[k * NEAR + j for k in range(FAR)] for j in range(NEAR)]
+    near = [[k * FAR + j for k in range(NEAR)] for j in range(FAR)]
+    far = [[k * FAR + j for j in range(FAR)] for k in range(NEAR)]
 
     def exchange(array, axis, groups=None):
         return lax.all_to_all(array, axis, 0, 0, axis_index_groups=groups, tiled=True)
 
-    pieces = exchange(chunk_of(screens, lax.axis_index("tm")), "uv", near)
+    pieces = exchange(chunk_of(screens), "uv", near)
+    sent = pack(owner_index[..., 0], subgrid_index, block_count, station_pair.swapaxes(1, 2), visibility, coordinate)
+    pieces, sent = lax.optimization_barrier((pieces, sent))
     pieces = exchange(pick_near(slot_owner, pieces), "uv", far)
-    sent = pack(owner_index[..., 0], subgrid_index, block_count, station_pair.swapaxes(1, 2), visibility, coordinate)
+    pieces, sent = lax.optimization_barrier((pieces, sent))
     arrived = exchange(sent, "tm")
     meta = meta_of(arrived)
     pieces = exchange(pick_far(slot_owner, pieces), "uv", near)

time: 98.4 us -> 96.4 us (0.980)
  blocking collectives: 35.8 us -> 29.3 us
  waiting for transfers between devices: 14.9 us -> 19.9 us
  starting transfers between devices: 27.1 us -> 31 us
  Pallas kernels: 17.2 us -> 13.9 us
  local copies, waits for them, and re-layouts: 2.66 us -> 1.43 us
    all_to_all x2, blocking collectives: 35.8 us -> 29.3 us  [exchange(): lax.all_to_all(array, axis, 0, 0, axis_index_groups=groups, tiled=True)]
    all_to_all x3, waiting for transfers between devices: 14.9 us -> 19.9 us  [exchange(): lax.all_to_all(array, axis, 0, 0, axis_index_groups=groups, tiled=True)]
    pallas_call x1, Pallas kernels: 10.3 us -> 6.27 us  [grid_blocks(): pl.pallas_call(grid_kernel, out_shape=jax.ShapeDtypeStruct((SLOTS * SUBS,...]
    all_to_all x3, starting transfers between devices: 27.1 us -> 31 us  [exchange(): lax.all_to_all(array, axis, 0, 0, axis_index_groups=groups, tiled=True)]
    pallas_call x1, Pallas kernels: 0.07 us -> 1.48 us  [chunk_of(): pl.pallas_call(chunk_kernel, out_shape=jax.ShapeDtypeStruct((NEAR, ST_PIE...]
    unnamed x18 -> x16, local copies, waits for them, and re-layouts: 2.58 us -> 1.35 us
  transfers between devices with their start and end apart: 3 -> 3, of which waited for: 2 -> 3; matrix products, arithmetic and copies ran while one was open for 0% -> 0% of each run, Pallas kernels for 14% -> 10%
where the time goes in v7:
time: 96.4 us; the launch traced here: 95.8 us
  starting transfers between devices  31 us (32%)
  blocking collectives  29.3 us (30%)
  waiting for transfers between devices  19.9 us (21%)
  Pallas kernels  13.9 us (14%)
  local copies, waits for them, and re-layouts  1.43 us (1%)
    all_to_all x3, starting transfers between devices, exchange(): lax.all_to_all(array, axis, 0, 0, axis_index_groups=groups, tiled=True)  31 us
    all_to_all x2, blocking collectives, exchange(): lax.all_to_all(array, axis, 0, 0, axis_index_groups=groups, tiled=True)  29.3 us
    all_to_all x3, waiting for transfers between devices, exchange(): lax.all_to_all(array, axis, 0, 0, axis_index_groups=groups, tiled=True)  19.9 us
    pallas_call x1, Pallas kernels, grid_blocks(): pl.pallas_call(grid_kernel, out_shape=jax.ShapeDtypeStruct((SLOTS * SUBS,...  6.27 us
    pallas_call x1, Pallas kernels, pack(): pl.pallas_call(pack_kernel, out_shape=jax.ShapeDtypeStruct((PEERS, ROWS,...  2.3 us
  transfers between devices with their start and end apart: 3, of which 3 were waited for; matrix products, arithmetic and copies ran while one was open for 0% of the time, Pallas kernels for 10%

profile of v7, /device:TPU:1, one launch (start us, length us, event | category | flops | bytes accessed | tf_op | source)
XLA Modules:
  0.0 95.8 jit_solution(6222666258195814851)
XLA Ops:
  0.0 1.5 %cut_chunk.1 = bf16[16,16,128]{2,1,0:T(8,128)(2,1)} custom-call(bf16[1,64,8,1024]{3,2,1,0:T(8,128)(2,1)} %screens_ref.1), custom_call_target="tpu_custom_call" | custom-call | tf_op jit(solution)/shard_map/cut_chunk/pallas_call | solution.py:260
  1.5 0.0 copy-start
  1.5 0.0 copy-start.1
  1.5 0.0 copy-start.5
  1.5 0.0 copy-start.6
  1.5 19.6 %all-to-all-start = ((bf16[16,16,128]{2,1,0:T(8,128)(2,1)}), bf16[16,16,128]{2,1,0:T(8,128)(2,1)S(1)}, u32[]{:S(2)}, u32[]{:S(2)}) async-start(bf16[16,16,128]{2,1,0:T(8,128)(2,1)} %cut_chunk.1), calls=%async_computation | async-start | bytes 131072 | tf_op jit(solution)/shard_map/all_to_all | solution.py:409
  21.1 0.0 copy-start.3
  21.2 0.6 copy-done.3
  21.8 0.0 copy-done.4
  21.8 2.3 %pack_blocks.1 = bf16[16,64,128]{2,1,0:T(8,128)(2,1)} custom-call(s32[3,1,16]{2,1,0:T(1,128)S(1)} %bitcast.3, s32[3,1,16]{2,1,0:T(1,128)S(1)} %copy-done.4, s32[3,1,16]{2,1,0:T(1,128)S(1)} %copy-done.5, s32[1,2,4]{2,1,0:T(2,128)S(1)} %bitcast.4, bf16[3,1,16,8,128]{4,3,2,1,0:T(8,128)(2,1)S(1)} %copy-done, bf16[3,1,16,2,128]{4,3,2,1,0:T(2,128)(2,1)S(1)} %copy-done.1), custom_call_target="tpu_custom_call" | custom-call | flops 2000000 | bytes 600000 | tf_op jit(solution)/shard_map/pack_blocks/pallas_call | solution.py:106
  24.1 8.6 %all-to-all-done.in_ref = bf16[16,16,128]{2,1,0:T(8,128)(2,1)S(1)} async-done(((bf16[16,16,128]{2,1,0:T(8,128)(2,1)}), bf16[16,16,128]{2,1,0:T(8,128)(2,1)S(1)}, u32[]{:S(2)}, u32[]{:S(2)}) %all-to-all-start) | async-done | bytes 65568 | tf_op jit(solution)/shard_map/all_to_all | solution.py:409
  32.7 0.6 pick_near.1
  33.2 13.6 %all_to_all.25.in_ref = bf16[4,3,16,128]{3,2,1,0:T(8,128)(2,1)S(1)} all-to-all(bf16[4,3,16,128]{3,2,1,0:T(8,128)(2,1)S(1)} %pick_near.1), channel_id=1, replica_groups={{0,16,32,48},{64,80,96,112},{128,144,160,176},{192,208,224,240},{256,27..., dimensions={0} | all-to-all | bytes 98304 | tf_op jit(solution)/shard_map/all_to_all | solution.py:409
  46.8 7.9 %all-to-all-start.2 = ((bf16[16,64,128]{2,1,0:T(8,128)(2,1)}), bf16[16,64,128]{2,1,0:T(8,128)(2,1)S(1)}, u32[]{:S(2)}, u32[]{:S(2)}) async-start(bf16[16,64,128]{2,1,0:T(8,128)(2,1)} %pack_blocks.1), calls=%async_computation.2 | async-start | bytes 524288 | tf_op jit(solution)/shard_map/all_to_all | solution.py:409
  54.8 1.2 %pick_far.1 = bf16[16,48,128]{2,1,0:T(8,128)(2,1)} custom-call(s32[3]{0:T(128)S(1)} %copy-done.2, bf16[4,3,16,128]{3,2,1,0:T(8,128)(2,1)S(1)} %all_to_all.25.in_ref), custom_call_target="tpu_custom_call" | custom-call | tf_op jit(solution)/shard_map/pick_far/pallas_call | solution.py:300
  56.0 5.9 %all-to-all-done.2.rows_ref = bf16[16,64,128]{2,1,0:T(8,128)(2,1)S(1)} async-done(((bf16[16,64,128]{2,1,0:T(8,128)(2,1)}), bf16[16,64,128]{2,1,0:T(8,128)(2,1)S(1)}, u32[]{:S(2)}, u32[]{:S(2)}) %all-to-all-start.2) | async-done | bytes 262176 | tf_op jit(solution)/shard_map/all_to_all | solution.py:409
  61.9 3.5 %all-to-all-start.3 = ((bf16[16,48,128]{2,1,0:T(8,128)(2,1)}), bf16[16,48,128]{2,1,0:T(8,128)(2,1)S(1)}, u32[]{:S(2)}, u32[]{:S(2)}) async-start(bf16[16,48,128]{2,1,0:T(8,128)(2,1)} %pick_far.1), calls=%async_computation.3 | async-start | bytes 393216 | tf_op jit(solution)/shard_map/all_to_all | solution.py:409
  65.5 0.1 reshape.4.meta
  65.6 0.7 copy-done.7
  66.3 6.3 %grid_blocks.1.x_ref = f32[12,8,8,128]{3,2,1,0:T(8,128)S(1)} custom-call(s32[512]{0:T(512)S(1)} %reshape.4.meta, s32[1,2,4]{2,1,0:T(2,128)S(1)} %bitcast.5, bf16[16,64,128]{2,1,0:T(8,128)(2,1)S(1)} %all-to-all-done.2.rows_ref), custom_call_target="tpu_custom_call" | custom-call | flops 800000000 | bytes 800000 | tf_op jit(solution)/shard_map/grid_blocks/pallas_call | solution.py:214
  72.6 5.4 %all-to-all-done.3.in_ref = bf16[16,48,128]{2,1,0:T(8,128)(2,1)S(1)} async-done(((bf16[16,48,128]{2,1,0:T(8,128)(2,1)}), bf16[16,48,128]{2,1,0:T(8,128)(2,1)S(1)}, u32[]{:S(2)}, u32[]{:S(2)}) %all-to-all-start.3) | async-done | bytes 196640 | tf_op jit(solution)/shard_map/all_to_all | solution.py:409
  78.0 0.9 asked_stations.1
  78.9 15.8 %all_to_all.26.in_ref = bf16[16,96,128]{2,1,0:T(8,128)(2,1)S(1)} all-to-all(bf16[16,96,128]{2,1,0:T(8,128)(2,1)S(1)} %asked_stations.1), channel_id=1, replica_groups=mesh['uv'=64,'tm'=16] {'tm'}, dimensions={0} | all-to-all | bytes 786432 | tf_op jit(solution)/shard_map/all_to_all | solution.py:409
  94.6 1.2 %screen_product.1 = f32[1,4,8,1024]{3,2,1,0:T(8,128)} custom-call(f32[12,8,8,128]{3,2,1,0:T(8,128)S(1)} %grid_blocks.1.x_ref, bf16[16,96,128]{2,1,0:T(8,128)(2,1)S(1)} %all_to_all.26.in_ref), custom_call_target="tpu_custom_call" | custom-call | flops 3000000 | bytes 1000000 | tf_op jit(solution)/shard_map/screen_product/pallas_call | solution.py:383
  (9 shorter events, 0.1 us)
Async XLA Ops:
  1.5 19.6 %copy-start = (bf16[3,1,16,8,128]{4,3,2,1,0:T(8,128)(2,1)S(1)}, bf16[3,1,16,8,128]{4,3,2,1,0:T(8,128)(2,1)}, u32[]{:S(2)}) copy-start(bf16[3,1,16,8,128]{4,3,2,1,0:T(8,128)(2,1)} %vis_ref.1) | copy-start | bytes 294916
  1.5 19.6 %copy-start.1 = (bf16[3,1,16,2,128]{4,3,2,1,0:T(2,128)(2,1)S(1)}, bf16[3,1,16,2,128]{4,3,2,1,0:T(2,128)(2,1)}, u32[]{:S(2)}) copy-start(bf16[3,1,16,2,128]{4,3,2,1,0:T(2,128)(2,1)} %coord_ref.1) | copy-start | bytes 73732
  1.5 19.6 %copy-start.5 = (s32[3,1,16]{2,1,0:T(1,128)S(1)}, s32[3,1,16]{2,1,0:T(1,128)}, u32[]{:S(2)}) copy-start(s32[3,1,16]{2,1,0:T(1,128)} %counts.1) | copy-start | bytes 580
  1.5 19.6 %copy-start.6 = (s32[1,4,2]{1,2,0:T(2,128)S(1)}, s32[1,4,2]{1,2,0:T(2,128)}, u32[]{:S(2)}) copy-start(s32[1,4,2]{1,2,0:T(2,128)} %param.15) | copy-start | bytes 100
  1.5 31.1 %all-to-all-start = ((bf16[16,16,128]{2,1,0:T(8,128)(2,1)}), bf16[16,16,128]{2,1,0:T(8,128)(2,1)S(1)}, u32[]{:S(2)}, u32[]{:S(2)}) async-start(bf16[16,16,128]{2,1,0:T(8,128)(2,1)} %cut_chunk.1), calls=%async_computation | async-start | bytes 131072 | tf_op jit(solution)/shard_map/all_to_all | solution.py:409
  21.1 0.7 copy-start.3
  21.1 0.7 copy-start.4
  21.8 10.9 %copy-start.2 = (s32[3]{0:T(128)S(1)}, s32[3]{0:T(128)}, u32[]{:S(2)}) copy-start(s32[3]{0:T(128)} %roots.3) | copy-start | bytes 40
  46.8 15.1 %all-to-all-start.2 = ((bf16[16,64,128]{2,1,0:T(8,128)(2,1)}), bf16[16,64,128]{2,1,0:T(8,128)(2,1)S(1)}, u32[]{:S(2)}, u32[]{:S(2)}) async-start(bf16[16,64,128]{2,1,0:T(8,128)(2,1)} %pack_blocks.1), calls=%async_computation.2 | async-start | bytes 524288 | tf_op jit(solution)/shard_map/all_to_all | solution.py:409
  61.9 16.0 %all-to-all-start.3 = ((bf16[16,48,128]{2,1,0:T(8,128)(2,1)}), bf16[16,48,128]{2,1,0:T(8,128)(2,1)S(1)}, u32[]{:S(2)}, u32[]{:S(2)}) async-start(bf16[16,48,128]{2,1,0:T(8,128)(2,1)} %pick_far.1), calls=%async_computation.3 | async-start | bytes 393216 | tf_op jit(solution)/shard_map/all_to_all | solution.py:409
  65.6 0.7 copy-start.7

commit v8 on v7

--- a/solution.py
+++ b/solution.py
@@ -270,15 +270,13 @@
 
 def pick_near_kernel(roots, in_ref, out_ref):
     for s in range(SLOTS):
-        piece = in_ref[roots[s] // FAR]
-        for k in range(FAR):
-            out_ref[k, s] = piece
+        out_ref[s] = in_ref[roots[s] // FAR]
 
 
 def pick_near(roots, pieces, **kw):
     return pl.pallas_call(
         pick_near_kernel,
-        out_shape=jax.ShapeDtypeStruct((FAR, SLOTS, 16, LANES), BF16),
+        out_shape=jax.ShapeDtypeStruct((SLOTS, 16, LANES), BF16),
         in_specs=[smem(), vmem()],
         out_specs=vmem(),
         name="pick_near",
@@ -287,8 +285,13 @@
     )(roots, pieces)
 
 
-def pick_far_kernel(roots, in_ref, out_ref):
-    pieces = [in_ref[roots[s] % FAR, s].astype(F32) for s in range(SLOTS)]
+def pick_far_kernel(roots, even_ref, odd_ref, out_ref):
+    me = lax.axis_index("uv")
+    pieces = []
+    for s in range(SLOTS):
+        shift = (me - roots[s] + FAR * NEAR) % FAR
+        k = shift // 2 * SLOTS + s
+        pieces.append(jnp.where(shift % 2 == 0, even_ref[k].astype(F32), odd_ref[k].astype(F32)))
     rows = jnp.concatenate(
         [pieces[s][4 * i:4 * i + 4] for i in range(ST_PIECE) for s in range(SLOTS)], axis=0
     ).astype(BF16)
@@ -296,16 +299,17 @@
         out_ref[j] = rows
 
 
-def pick_far(roots, pieces, **kw):
+def pick_far(roots, even, odd, **kw):
     return pl.pallas_call(
         pick_far_kernel,
         out_shape=jax.ShapeDtypeStruct((NEAR, ST_PIECE * SLOTS * 4, LANES), BF16),
-        in_specs=[smem(), vmem()],
+        in_specs=[smem(), vmem(), vmem()],
         out_specs=vmem(),
         name="pick_far",
-        compiler_params=room(),
-        **kw,
-    )(roots, pieces)
+        cost_estimate=pl.CostEstimate(flops=4200000000, bytes_accessed=800000, transcendentals=0),
+        compiler_params=room(),
+        **kw,
+    )(roots, even, odd)
 
 
 ROWS_ST = SLOTS * 4
@@ -403,7 +407,10 @@
 def on_device(visibility, coordinate, block_count, owner_index, subgrid_index, offsets,
               station_pair, screens, slot_owner):
     near = [[k * FAR + j for k in range(NEAR)] for j in range(FAR)]
-    far = [[k * FAR + j for j in range(FAR)] for k in range(NEAR)]
+
+    def shifted(array, shift):
+        pairs = [(k * FAR + j, k * FAR + (j + shift) % FAR) for k in range(NEAR) for j in range(FAR)]
+        return lax.ppermute(array, "uv", pairs)
 
     def exchange(array, axis, groups=None):
         return lax.all_to_all(array, axis, 0, 0, axis_index_groups=groups, tiled=True)
@@ -411,11 +418,12 @@
     pieces = exchange(chunk_of(screens), "uv", near)
     sent = pack(owner_index[..., 0], subgrid_index, block_count, station_pair.swapaxes(1, 2), visibility, coordinate)
     pieces, sent = lax.optimization_barrier((pieces, sent))
-    pieces = exchange(pick_near(slot_owner, pieces), "uv", far)
-    pieces, sent = lax.optimization_barrier((pieces, sent))
+    piece = pick_near(slot_owner, pieces)
+    even = jnp.concatenate([piece, shifted(piece, 2)], axis=0)
+    odd = shifted(even, 1)
     arrived = exchange(sent, "tm")
     meta = meta_of(arrived)
-    pieces = exchange(pick_far(slot_owner, pieces), "uv", near)
+    pieces = exchange(pick_far(slot_owner, even, odd), "uv", near)
     x = grid_blocks(meta, offsets.swapaxes(1, 2), arrived)
     meta, x = lax.optimization_barrier((meta, x))
     wanted = exchange(asked(meta, pieces), "tm")

time: 96.4 us -> 92.9 us (0.964)
  blocking collectives: 29.3 us -> 18.8 us
  starting transfers between devices: 31 us -> 39.8 us
  waiting for transfers between devices: 19.9 us -> 18.4 us
    all_to_all x2 -> x1, blocking collectives: 29.3 us -> 18.8 us  [exchange(): lax.all_to_all(array, axis, 0, 0, axis_index_groups=groups, tiled=True)]
    ppermute x0 -> x2, starting transfers between devices: none -> 9.9 us  [shifted(): return lax.ppermute(array, 'uv', pairs)]
    all_to_all x3, waiting for transfers between devices: 19.9 us -> 14.1 us  [exchange(): lax.all_to_all(array, axis, 0, 0, axis_index_groups=groups, tiled=True)]
    ppermute x0 -> x2, waiting for transfers between devices: none -> 4.26 us  [shifted(): return lax.ppermute(array, 'uv', pairs)]
    all_to_all x3, starting transfers between devices: 31 us -> 29.9 us  [exchange(): lax.all_to_all(array, axis, 0, 0, axis_index_groups=groups, tiled=True)]
  transfers between devices with their start and end apart: 3 -> 5, of which waited for: 3 -> 3; matrix products, arithmetic and copies ran while one was open for 0% -> 0% of each run, Pallas kernels for 10% -> 10%
where the time goes in v8:
time: 92.9 us; the launch traced here: 92.3 us
  starting transfers between devices  39.8 us (43%)
  blocking collectives  18.8 us (20%)
  waiting for transfers between devices  18.4 us (20%)
  Pallas kernels  13.7 us (15%)
  local copies, waits for them, and re-layouts  1.43 us (2%)
    all_to_all x3, starting transfers between devices, exchange(): lax.all_to_all(array, axis, 0, 0, axis_index_groups=groups, tiled=True)  29.9 us
    all_to_all x1, blocking collectives, exchange(): lax.all_to_all(array, axis, 0, 0, axis_index_groups=groups, tiled=True)  18.8 us
    all_to_all x3, waiting for transfers between devices, exchange(): lax.all_to_all(array, axis, 0, 0, axis_index_groups=groups, tiled=True)  14.1 us
    ppermute x2, starting transfers between devices, shifted(): return lax.ppermute(array, 'uv', pairs)  9.9 us
    pallas_call x1, Pallas kernels, grid_blocks(): pl.pallas_call(grid_kernel, out_shape=jax.ShapeDtypeStruct((SLOTS * SUBS,...  5.96 us
    ppermute x2, waiting for transfers between devices, shifted(): return lax.ppermute(array, 'uv', pairs)  4.26 us
    pallas_call x1, Pallas kernels, pack(): pl.pallas_call(pack_kernel, out_shape=jax.ShapeDtypeStruct((PEERS, ROWS,...  2.29 us
  transfers between devices with their start and end apart: 5, of which 3 were waited for; matrix products, arithmetic and copies ran while one was open for 0% of the time, Pallas kernels for 10%

profile of v8, /device:TPU:1, one launch (start us, length us, event | category | flops | bytes accessed | tf_op | source)
XLA Modules:
  0.0 92.3 jit_solution(3967248569956031588)
XLA Ops:
  0.0 1.5 %cut_chunk.1 = bf16[16,16,128]{2,1,0:T(8,128)(2,1)} custom-call(bf16[1,64,8,1024]{3,2,1,0:T(8,128)(2,1)} %screens_ref.1), custom_call_target="tpu_custom_call" | custom-call | tf_op jit(solution)/shard_map/cut_chunk/pallas_call | solution.py:260
  1.5 0.0 copy-start
  1.5 0.0 copy-start.4
  1.5 0.0 copy-start.5
  1.5 19.6 %all-to-all-start = ((bf16[16,16,128]{2,1,0:T(8,128)(2,1)}), bf16[16,16,128]{2,1,0:T(8,128)(2,1)S(1)}, u32[]{:S(2)}, u32[]{:S(2)}) async-start(bf16[16,16,128]{2,1,0:T(8,128)(2,1)} %cut_chunk.1), calls=%async_computation | async-start | bytes 131072 | tf_op jit(solution)/shard_map/all_to_all | solution.py:416
  21.1 0.0 copy-start.3
  21.2 0.6 copy-done.2
  21.8 0.0 copy-done.3
  21.8 2.3 %pack_blocks.1 = bf16[16,64,128]{2,1,0:T(8,128)(2,1)} custom-call(s32[3,1,16]{2,1,0:T(1,128)S(1)} %bitcast.3, s32[3,1,16]{2,1,0:T(1,128)S(1)} %copy-done.3, s32[3,1,16]{2,1,0:T(1,128)S(1)} %copy-done.4, s32[1,2,4]{2,1,0:T(2,128)S(1)} %bitcast.4, bf16[3,1,16,8,128]{4,3,2,1,0:T(8,128)(2,1)S(1)} %copy-done, bf16[3,1,16,2,128]{4,3,2,1,0:T(2,128)(2,1)S(1)} %copy-done.1), custom_call_target="tpu_custom_call" | custom-call | flops 2000000 | bytes 600000 | tf_op jit(solution)/shard_map/pack_blocks/pallas_call | solution.py:106
  24.1 8.6 %all-to-all-done.in_ref = bf16[16,16,128]{2,1,0:T(8,128)(2,1)S(1)} async-done(((bf16[16,16,128]{2,1,0:T(8,128)(2,1)}), bf16[16,16,128]{2,1,0:T(8,128)(2,1)S(1)}, u32[]{:S(2)}, u32[]{:S(2)}) %all-to-all-start) | async-done | bytes 65568 | tf_op jit(solution)/shard_map/all_to_all | solution.py:416
  32.7 0.6 pick_near.1
  33.2 7.5 %collective-permute-start = (bf16[3,16,128]{2,1,0:T(8,128)(2,1)S(1)}, bf16[3,16,128]{2,1,0:T(8,128)(2,1)S(1)}, u32[]{:S(2)}, u32[]{:S(2)}) collective-permute-start(bf16[3,16,128]{2,1,0:T(8,128)(2,1)S(1)} %pick_near.1), channel_id=1, source_target_pairs={{0,32},{16,48},{32,0},{48,16},{64,96},{80,112},{96,64},{112,80},{1... | collective-permute-start | bytes 36872 | tf_op jit(solution)/shard_map/ppermute | solution.py:413
  40.7 6.8 %all-to-all-start.1 = ((bf16[16,64,128]{2,1,0:T(8,128)(2,1)}), bf16[16,64,128]{2,1,0:T(8,128)(2,1)S(1)}, u32[]{:S(2)}, u32[]{:S(2)}) async-start(bf16[16,64,128]{2,1,0:T(8,128)(2,1)} %pack_blocks.1), calls=%async_computation.1 | async-start | bytes 524288 | tf_op jit(solution)/shard_map/all_to_all | solution.py:416
  47.6 2.4 %collective-permute-start.1 = (bf16[6,16,128]{2,1,0:T(8,128)(2,1)S(1)}, bf16[6,16,128]{2,1,0:T(8,128)(2,1)S(1)}, u32[]{:S(2)}, u32[]{:S(2)}) collective-permute-start(bf16[6,16,128]{2,1,0:T(8,128)(2,1)S(1)} %pad_maximum_fusion.even_ref), channel_id=1, source_target_pairs={{0,16},{16,32},{32,48},{48,0},{64,80},{80,96},{96,112},{112,64},{1... | collective-permute-start | bytes 73736 | tf_op jit(solution)/shard_map/ppermute | solution.py:413
  50.0 4.3 %collective-permute-done.1.odd_ref = bf16[6,16,128]{2,1,0:T(8,128)(2,1)S(1)} collective-permute-done((bf16[6,16,128]{2,1,0:T(8,128)(2,1)S(1)}, bf16[6,16,128]{2,1,0:T(8,128)(2,1)S(1)}, u32[]{:S(2)}, u32[]{:S(2)}) %collective-permute-start.1) | collective-permute-done | bytes 24608 | tf_op jit(solution)/shard_map/ppermute | solution.py:413
  54.3 1.3 %pick_far.1 = bf16[16,48,128]{2,1,0:T(8,128)(2,1)} custom-call(s32[3]{0:T(128)S(1)} %copy-done.6, bf16[6,16,128]{2,1,0:T(8,128)(2,1)S(1)} %pad_maximum_fusion.even_ref, bf16[6,16,128]{2,1,0:T(8,128)(2,1)S(1)} %collective-permute-done.1.odd_ref), custom_call_target="tpu_custom_call" | custom-call | flops 4200000000 | bytes 800000 | tf_op jit(solution)/shard_map/pick_far/pallas_call | solution.py:303
  55.5 3.5 %all-to-all-start.2 = ((bf16[16,48,128]{2,1,0:T(8,128)(2,1)}), bf16[16,48,128]{2,1,0:T(8,128)(2,1)S(1)}, u32[]{:S(2)}, u32[]{:S(2)}) async-start(bf16[16,48,128]{2,1,0:T(8,128)(2,1)} %pick_far.1), calls=%async_computation.2 | async-start | bytes 393216 | tf_op jit(solution)/shard_map/all_to_all | solution.py:416
  59.1 0.1 reshape.4.meta
  59.2 0.7 copy-done.7
  59.9 6.0 %grid_blocks.1.x_ref = f32[12,8,8,128]{3,2,1,0:T(8,128)S(1)} custom-call(s32[512]{0:T(512)S(1)} %reshape.4.meta, s32[1,2,4]{2,1,0:T(2,128)S(1)} %bitcast.5, bf16[16,64,128]{2,1,0:T(8,128)(2,1)S(1)} %all-to-all-done.1.rows_ref), custom_call_target="tpu_custom_call" | custom-call | flops 800000000 | bytes 800000 | tf_op jit(solution)/shard_map/grid_blocks/pallas_call | solution.py:214
  65.8 5.6 %all-to-all-done.2.in_ref = bf16[16,48,128]{2,1,0:T(8,128)(2,1)S(1)} async-done(((bf16[16,48,128]{2,1,0:T(8,128)(2,1)}), bf16[16,48,128]{2,1,0:T(8,128)(2,1)S(1)}, u32[]{:S(2)}, u32[]{:S(2)}) %all-to-all-start.2) | async-done | bytes 196640 | tf_op jit(solution)/shard_map/all_to_all | solution.py:416
  71.4 0.9 asked_stations.1
  72.3 18.8 %all_to_all.20.in_ref = bf16[16,96,128]{2,1,0:T(8,128)(2,1)S(1)} all-to-all(bf16[16,96,128]{2,1,0:T(8,128)(2,1)S(1)} %asked_stations.1), channel_id=1, replica_groups=mesh['uv'=64,'tm'=16] {'tm'}, dimensions={0} | all-to-all | bytes 786432 | tf_op jit(solution)/shard_map/all_to_all | solution.py:416
  91.1 1.2 %screen_product.1 = f32[1,4,8,1024]{3,2,1,0:T(8,128)} custom-call(f32[12,8,8,128]{3,2,1,0:T(8,128)S(1)} %grid_blocks.1.x_ref, bf16[16,96,128]{2,1,0:T(8,128)(2,1)S(1)} %all_to_all.20.in_ref), custom_call_target="tpu_custom_call" | custom-call | flops 3000000 | bytes 1000000 | tf_op jit(solution)/shard_map/screen_product/pallas_call | solution.py:387
  (13 shorter events, 0.1 us)
Async XLA Ops:
  1.5 19.6 %copy-start = (bf16[3,1,16,8,128]{4,3,2,1,0:T(8,128)(2,1)S(1)}, bf16[3,1,16,8,128]{4,3,2,1,0:T(8,128)(2,1)}, u32[]{:S(2)}) copy-start(bf16[3,1,16,8,128]{4,3,2,1,0:T(8,128)(2,1)} %vis_ref.1) | copy-start | bytes 294916
  1.5 19.6 %copy-start.1 = (bf16[3,1,16,2,128]{4,3,2,1,0:T(2,128)(2,1)S(1)}, bf16[3,1,16,2,128]{4,3,2,1,0:T(2,128)(2,1)}, u32[]{:S(2)}) copy-start(bf16[3,1,16,2,128]{4,3,2,1,0:T(2,128)(2,1)} %coord_ref.1) | copy-start | bytes 73732
  1.5 19.6 %copy-start.4 = (s32[3,1,16]{2,1,0:T(1,128)S(1)}, s32[3,1,16]{2,1,0:T(1,128)}, u32[]{:S(2)}) copy-start(s32[3,1,16]{2,1,0:T(1,128)} %counts.1) | copy-start | bytes 580
  1.5 19.6 %copy-start.5 = (s32[1,4,2]{1,2,0:T(2,128)S(1)}, s32[1,4,2]{1,2,0:T(2,128)}, u32[]{:S(2)}) copy-start(s32[1,4,2]{1,2,0:T(2,128)} %param.15) | copy-start | bytes 100
  1.5 31.1 %all-to-all-start = ((bf16[16,16,128]{2,1,0:T(8,128)(2,1)}), bf16[16,16,128]{2,1,0:T(8,128)(2,1)S(1)}, u32[]{:S(2)}, u32[]{:S(2)}) async-start(bf16[16,16,128]{2,1,0:T(8,128)(2,1)} %cut_chunk.1), calls=%async_computation | async-start | bytes 131072 | tf_op jit(solution)/shard_map/all_to_all | solution.py:416
  21.1 0.7 copy-start.2
  21.1 0.7 copy-start.3
  21.8 10.9 %copy-start.6 = (s32[3]{0:T(128)S(1)}, s32[3]{0:T(128)}, u32[]{:S(2)}) copy-start(s32[3]{0:T(128)} %roots.3) | copy-start | bytes 40
  33.2 14.3 %collective-permute-start = (bf16[3,16,128]{2,1,0:T(8,128)(2,1)S(1)}, bf16[3,16,128]{2,1,0:T(8,128)(2,1)S(1)}, u32[]{:S(2)}, u32[]{:S(2)}) collective-permute-start(bf16[3,16,128]{2,1,0:T(8,128)(2,1)S(1)} %pick_near.1), channel_id=1, source_target_pairs={{0,32},{16,48},{32,0},{48,16},{64,96},{80,112},{96,64},{112,80},{1... | collective-permute-start | bytes 36872 | tf_op jit(solution)/shard_map/ppermute | solution.py:413
  40.7 14.8 %all-to-all-start.1 = ((bf16[16,64,128]{2,1,0:T(8,128)(2,1)}), bf16[16,64,128]{2,1,0:T(8,128)(2,1)S(1)}, u32[]{:S(2)}, u32[]{:S(2)}) async-start(bf16[16,64,128]{2,1,0:T(8,128)(2,1)} %pack_blocks.1), calls=%async_computation.1 | async-start | bytes 524288 | tf_op jit(solution)/shard_map/all_to_all | solution.py:416
  47.6 6.7 %collective-permute-start.1 = (bf16[6,16,128]{2,1,0:T(8,128)(2,1)S(1)}, bf16[6,16,128]{2,1,0:T(8,128)(2,1)S(1)}, u32[]{:S(2)}, u32[]{:S(2)}) collective-permute-start(bf16[6,16,128]{2,1,0:T(8,128)(2,1)S(1)} %pad_maximum_fusion.even_ref), channel_id=1, source_target_pairs={{0,16},{16,32},{32,48},{48,0},{64,80},{80,96},{96,112},{112,64},{1... | collective-permute-start | bytes 73736 | tf_op jit(solution)/shard_map/ppermute | solution.py:413
  55.5 15.9 %all-to-all-start.2 = ((bf16[16,48,128]{2,1,0:T(8,128)(2,1)}), bf16[16,48,128]{2,1,0:T(8,128)(2,1)S(1)}, u32[]{:S(2)}, u32[]{:S(2)}) async-start(bf16[16,48,128]{2,1,0:T(8,128)(2,1)} %pick_far.1), calls=%async_computation.2 | async-start | bytes 393216 | tf_op jit(solution)/shard_map/all_to_all | solution.py:416
  59.2 0.7 copy-start.7

commit v9 on v8

--- a/solution.py
+++ b/solution.py
@@ -285,18 +285,21 @@
     )(roots, pieces)
 
 
-def pick_far_kernel(roots, even_ref, odd_ref, out_ref):
+def pick_far_kernel(roots, even_ref, odd_ref, out_ref, rows, sent):
     me = lax.axis_index("uv")
     pieces = []
     for s in range(SLOTS):
         shift = (me - roots[s] + FAR * NEAR) % FAR
         k = shift // 2 * SLOTS + s
         pieces.append(jnp.where(shift % 2 == 0, even_ref[k].astype(F32), odd_ref[k].astype(F32)))
-    rows = jnp.concatenate(
+    rows[...] = jnp.concatenate(
         [pieces[s][4 * i:4 * i + 4] for i in range(ST_PIECE) for s in range(SLOTS)], axis=0
     ).astype(BF16)
-    for j in range(NEAR):
-        out_ref[j] = rows
+    copies = [pltpu.make_async_copy(rows, out_ref.at[j], sent.at[j]) for j in range(NEAR)]
+    for copy in copies:
+        copy.start()
+    for copy in copies:
+        copy.wait()
 
 
 def pick_far(roots, even, odd, **kw):
@@ -304,7 +307,8 @@
         pick_far_kernel,
         out_shape=jax.ShapeDtypeStruct((NEAR, ST_PIECE * SLOTS * 4, LANES), BF16),
         in_specs=[smem(), vmem(), vmem()],
-        out_specs=vmem(),
+        out_specs=pl.BlockSpec(memory_space=pltpu.HBM),
+        scratch_shapes=[pltpu.VMEM((ST_PIECE * SLOTS * 4, LANES), BF16), pltpu.SemaphoreType.DMA((NEAR,))],
         name="pick_far",
         cost_estimate=pl.CostEstimate(flops=4200000000, bytes_accessed=800000, transcendentals=0),
         compiler_params=room(),

time: 92.9 us -> 93 us (level)
  no operation moved by 1% of the time
where the time goes in v9:
time: 93 us; the launch traced here: 92.5 us
  starting transfers between devices  39.8 us (43%)
  blocking collectives  18.8 us (20%)
  waiting for transfers between devices  18.4 us (20%)
  Pallas kernels  13.8 us (15%)
  local copies, waits for them, and re-layouts  1.43 us (2%)
    all_to_all x3, starting transfers between devices, exchange(): lax.all_to_all(array, axis, 0, 0, axis_index_groups=groups, tiled=True)  29.9 us
    all_to_all x1, blocking collectives, exchange(): lax.all_to_all(array, axis, 0, 0, axis_index_groups=groups, tiled=True)  18.8 us
    all_to_all x3, waiting for transfers between devices, exchange(): lax.all_to_all(array, axis, 0, 0, axis_index_groups=groups, tiled=True)  14.1 us
    ppermute x2, starting transfers between devices, shifted(): return lax.ppermute(array, 'uv', pairs)  9.9 us
    pallas_call x1, Pallas kernels, grid_blocks(): pl.pallas_call(grid_kernel, out_shape=jax.ShapeDtypeStruct((SLOTS * SUBS,...  5.96 us
    ppermute x2, waiting for transfers between devices, shifted(): return lax.ppermute(array, 'uv', pairs)  4.26 us
    pallas_call x1, Pallas kernels, pack(): pl.pallas_call(pack_kernel, out_shape=jax.ShapeDtypeStruct((PEERS, ROWS,...  2.29 us
  transfers between devices with their start and end apart: 5, of which 3 were waited for; matrix products, arithmetic and copies ran while one was open for 0% of the time, Pallas kernels for 10%

profile of v9, /device:TPU:1, one launch (start us, length us, event | category | flops | bytes accessed | tf_op | source)
XLA Modules:
  0.0 92.5 jit_solution(14647133047562719104)
XLA Ops:
  0.0 1.5 %cut_chunk.1 = bf16[16,16,128]{2,1,0:T(8,128)(2,1)} custom-call(bf16[1,64,8,1024]{3,2,1,0:T(8,128)(2,1)} %screens_ref.1), custom_call_target="tpu_custom_call" | custom-call | tf_op jit(solution)/shard_map/cut_chunk/pallas_call | solution.py:260
  1.5 0.0 copy-start
  1.5 0.0 copy-start.4
  1.5 0.0 copy-start.5
  1.5 19.6 %all-to-all-start = ((bf16[16,16,128]{2,1,0:T(8,128)(2,1)}), bf16[16,16,128]{2,1,0:T(8,128)(2,1)S(1)}, u32[]{:S(2)}, u32[]{:S(2)}) async-start(bf16[16,16,128]{2,1,0:T(8,128)(2,1)} %cut_chunk.1), calls=%async_computation | async-start | bytes 131072 | tf_op jit(solution)/shard_map/all_to_all | solution.py:420
  21.1 0.0 copy-start.3
  21.2 0.6 copy-done.2
  21.8 0.0 copy-done.3
  21.8 2.3 %pack_blocks.1 = bf16[16,64,128]{2,1,0:T(8,128)(2,1)} custom-call(s32[3,1,16]{2,1,0:T(1,128)S(1)} %bitcast.3, s32[3,1,16]{2,1,0:T(1,128)S(1)} %copy-done.3, s32[3,1,16]{2,1,0:T(1,128)S(1)} %copy-done.4, s32[1,2,4]{2,1,0:T(2,128)S(1)} %bitcast.4, bf16[3,1,16,8,128]{4,3,2,1,0:T(8,128)(2,1)S(1)} %copy-done, bf16[3,1,16,2,128]{4,3,2,1,0:T(2,128)(2,1)S(1)} %copy-done.1), custom_call_target="tpu_custom_call" | custom-call | flops 2000000 | bytes 600000 | tf_op jit(solution)/shard_map/pack_blocks/pallas_call | solution.py:106
  24.1 8.6 %all-to-all-done.in_ref = bf16[16,16,128]{2,1,0:T(8,128)(2,1)S(1)} async-done(((bf16[16,16,128]{2,1,0:T(8,128)(2,1)}), bf16[16,16,128]{2,1,0:T(8,128)(2,1)S(1)}, u32[]{:S(2)}, u32[]{:S(2)}) %all-to-all-start) | async-done | bytes 65568 | tf_op jit(solution)/shard_map/all_to_all | solution.py:420
  32.7 0.6 pick_near.1
  33.2 7.5 %collective-permute-start = (bf16[3,16,128]{2,1,0:T(8,128)(2,1)S(1)}, bf16[3,16,128]{2,1,0:T(8,128)(2,1)S(1)}, u32[]{:S(2)}, u32[]{:S(2)}) collective-permute-start(bf16[3,16,128]{2,1,0:T(8,128)(2,1)S(1)} %pick_near.1), channel_id=1, source_target_pairs={{0,32},{16,48},{32,0},{48,16},{64,96},{80,112},{96,64},{112,80},{1... | collective-permute-start | bytes 36872 | tf_op jit(solution)/shard_map/ppermute | solution.py:417
  40.7 6.8 %all-to-all-start.1 = ((bf16[16,64,128]{2,1,0:T(8,128)(2,1)}), bf16[16,64,128]{2,1,0:T(8,128)(2,1)S(1)}, u32[]{:S(2)}, u32[]{:S(2)}) async-start(bf16[16,64,128]{2,1,0:T(8,128)(2,1)} %pack_blocks.1), calls=%async_computation.1 | async-start | bytes 524288 | tf_op jit(solution)/shard_map/all_to_all | solution.py:420
  47.6 2.4 %collective-permute-start.1 = (bf16[6,16,128]{2,1,0:T(8,128)(2,1)S(1)}, bf16[6,16,128]{2,1,0:T(8,128)(2,1)S(1)}, u32[]{:S(2)}, u32[]{:S(2)}) collective-permute-start(bf16[6,16,128]{2,1,0:T(8,128)(2,1)S(1)} %pad_maximum_fusion.even_ref), channel_id=1, source_target_pairs={{0,16},{16,32},{32,48},{48,0},{64,80},{80,96},{96,112},{112,64},{1... | collective-permute-start | bytes 73736 | tf_op jit(solution)/shard_map/ppermute | solution.py:417
  50.0 4.3 %collective-permute-done.1.odd_ref = bf16[6,16,128]{2,1,0:T(8,128)(2,1)S(1)} collective-permute-done((bf16[6,16,128]{2,1,0:T(8,128)(2,1)S(1)}, bf16[6,16,128]{2,1,0:T(8,128)(2,1)S(1)}, u32[]{:S(2)}, u32[]{:S(2)}) %collective-permute-start.1) | collective-permute-done | bytes 24608 | tf_op jit(solution)/shard_map/ppermute | solution.py:417
  54.3 1.4 %pick_far.1 = bf16[16,48,128]{2,1,0:T(8,128)(2,1)} custom-call(s32[3]{0:T(128)S(1)} %copy-done.6, bf16[6,16,128]{2,1,0:T(8,128)(2,1)S(1)} %pad_maximum_fusion.even_ref, bf16[6,16,128]{2,1,0:T(8,128)(2,1)S(1)} %collective-permute-done.1.odd_ref), custom_call_target="tpu_custom_call" | custom-call | flops 4200000000 | bytes 800000 | tf_op jit(solution)/shard_map/pick_far/pallas_call | solution.py:306
  55.7 3.5 %all-to-all-start.2 = ((bf16[16,48,128]{2,1,0:T(8,128)(2,1)}), bf16[16,48,128]{2,1,0:T(8,128)(2,1)S(1)}, u32[]{:S(2)}, u32[]{:S(2)}) async-start(bf16[16,48,128]{2,1,0:T(8,128)(2,1)} %pick_far.1), calls=%async_computation.2 | async-start | bytes 393216 | tf_op jit(solution)/shard_map/all_to_all | solution.py:420
  59.3 0.1 reshape.4.meta
  59.4 0.7 copy-done.7
  60.0 6.0 %grid_blocks.1.x_ref = f32[12,8,8,128]{3,2,1,0:T(8,128)S(1)} custom-call(s32[512]{0:T(512)S(1)} %reshape.4.meta, s32[1,2,4]{2,1,0:T(2,128)S(1)} %bitcast.5, bf16[16,64,128]{2,1,0:T(8,128)(2,1)S(1)} %all-to-all-done.1.rows_ref), custom_call_target="tpu_custom_call" | custom-call | flops 800000000 | bytes 800000 | tf_op jit(solution)/shard_map/grid_blocks/pallas_call | solution.py:214
  66.0 5.6 %all-to-all-done.2.in_ref = bf16[16,48,128]{2,1,0:T(8,128)(2,1)S(1)} async-done(((bf16[16,48,128]{2,1,0:T(8,128)(2,1)}), bf16[16,48,128]{2,1,0:T(8,128)(2,1)S(1)}, u32[]{:S(2)}, u32[]{:S(2)}) %all-to-all-start.2) | async-done | bytes 196640 | tf_op jit(solution)/shard_map/all_to_all | solution.py:420
  71.6 0.9 asked_stations.1
  72.5 18.8 %all_to_all.20.in_ref = bf16[16,96,128]{2,1,0:T(8,128)(2,1)S(1)} all-to-all(bf16[16,96,128]{2,1,0:T(8,128)(2,1)S(1)} %asked_stations.1), channel_id=1, replica_groups=mesh['uv'=64,'tm'=16] {'tm'}, dimensions={0} | all-to-all | bytes 786432 | tf_op jit(solution)/shard_map/all_to_all | solution.py:420
  91.3 1.2 %screen_product.1 = f32[1,4,8,1024]{3,2,1,0:T(8,128)} custom-call(f32[12,8,8,128]{3,2,1,0:T(8,128)S(1)} %grid_blocks.1.x_ref, bf16[16,96,128]{2,1,0:T(8,128)(2,1)S(1)} %all_to_all.20.in_ref), custom_call_target="tpu_custom_call" | custom-call | flops 3000000 | bytes 1000000 | tf_op jit(solution)/shard_map/screen_product/pallas_call | solution.py:391
  (13 shorter events, 0.1 us)
Async XLA Ops:
  1.5 19.6 %copy-start = (bf16[3,1,16,8,128]{4,3,2,1,0:T(8,128)(2,1)S(1)}, bf16[3,1,16,8,128]{4,3,2,1,0:T(8,128)(2,1)}, u32[]{:S(2)}) copy-start(bf16[3,1,16,8,128]{4,3,2,1,0:T(8,128)(2,1)} %vis_ref.1) | copy-start | bytes 294916
  1.5 19.6 %copy-start.1 = (bf16[3,1,16,2,128]{4,3,2,1,0:T(2,128)(2,1)S(1)}, bf16[3,1,16,2,128]{4,3,2,1,0:T(2,128)(2,1)}, u32[]{:S(2)}) copy-start(bf16[3,1,16,2,128]{4,3,2,1,0:T(2,128)(2,1)} %coord_ref.1) | copy-start | bytes 73732
  1.5 19.6 %copy-start.4 = (s32[3,1,16]{2,1,0:T(1,128)S(1)}, s32[3,1,16]{2,1,0:T(1,128)}, u32[]{:S(2)}) copy-start(s32[3,1,16]{2,1,0:T(1,128)} %counts.1) | copy-start | bytes 580
  1.5 19.6 %copy-start.5 = (s32[1,4,2]{1,2,0:T(2,128)S(1)}, s32[1,4,2]{1,2,0:T(2,128)}, u32[]{:S(2)}) copy-start(s32[1,4,2]{1,2,0:T(2,128)} %param.15) | copy-start | bytes 100
  1.5 31.1 %all-to-all-start = ((bf16[16,16,128]{2,1,0:T(8,128)(2,1)}), bf16[16,16,128]{2,1,0:T(8,128)(2,1)S(1)}, u32[]{:S(2)}, u32[]{:S(2)}) async-start(bf16[16,16,128]{2,1,0:T(8,128)(2,1)} %cut_chunk.1), calls=%async_computation | async-start | bytes 131072 | tf_op jit(solution)/shard_map/all_to_all | solution.py:420
  21.1 0.7 copy-start.2
  21.1 0.7 copy-start.3
  21.8 10.9 %copy-start.6 = (s32[3]{0:T(128)S(1)}, s32[3]{0:T(128)}, u32[]{:S(2)}) copy-start(s32[3]{0:T(128)} %roots.3) | copy-start | bytes 40
  33.2 14.3 %collective-permute-start = (bf16[3,16,128]{2,1,0:T(8,128)(2,1)S(1)}, bf16[3,16,128]{2,1,0:T(8,128)(2,1)S(1)}, u32[]{:S(2)}, u32[]{:S(2)}) collective-permute-start(bf16[3,16,128]{2,1,0:T(8,128)(2,1)S(1)} %pick_near.1), channel_id=1, source_target_pairs={{0,32},{16,48},{32,0},{48,16},{64,96},{80,112},{96,64},{112,80},{1... | collective-permute-start | bytes 36872 | tf_op jit(solution)/shard_map/ppermute | solution.py:417
  40.7 15.0 %all-to-all-start.1 = ((bf16[16,64,128]{2,1,0:T(8,128)(2,1)}), bf16[16,64,128]{2,1,0:T(8,128)(2,1)S(1)}, u32[]{:S(2)}, u32[]{:S(2)}) async-start(bf16[16,64,128]{2,1,0:T(8,128)(2,1)} %pack_blocks.1), calls=%async_computation.1 | async-start | bytes 524288 | tf_op jit(solution)/shard_map/all_to_all | solution.py:420
  47.6 6.7 %collective-permute-start.1 = (bf16[6,16,128]{2,1,0:T(8,128)(2,1)S(1)}, bf16[6,16,128]{2,1,0:T(8,128)(2,1)S(1)}, u32[]{:S(2)}, u32[]{:S(2)}) collective-permute-start(bf16[6,16,128]{2,1,0:T(8,128)(2,1)S(1)} %pad_maximum_fusion.even_ref), channel_id=1, source_target_pairs={{0,16},{16,32},{32,48},{48,0},{64,80},{80,96},{96,112},{112,64},{1... | collective-permute-start | bytes 73736 | tf_op jit(solution)/shard_map/ppermute | solution.py:417
  55.7 15.9 %all-to-all-start.2 = ((bf16[16,48,128]{2,1,0:T(8,128)(2,1)}), bf16[16,48,128]{2,1,0:T(8,128)(2,1)S(1)}, u32[]{:S(2)}, u32[]{:S(2)}) async-start(bf16[16,48,128]{2,1,0:T(8,128)(2,1)} %pick_far.1), calls=%async_computation.2 | async-start | bytes 393216 | tf_op jit(solution)/shard_map/all_to_all | solution.py:420
  59.4 0.7 copy-start.7

commit v10 on v8

--- a/solution.py
+++ b/solution.py
@@ -285,13 +285,16 @@
     )(roots, pieces)
 
 
-def pick_far_kernel(roots, even_ref, odd_ref, out_ref):
+def pick_far_kernel(roots, *refs):
+    out_ref = refs[FAR]
     me = lax.axis_index("uv")
     pieces = []
     for s in range(SLOTS):
         shift = (me - roots[s] + FAR * NEAR) % FAR
-        k = shift // 2 * SLOTS + s
-        pieces.append(jnp.where(shift % 2 == 0, even_ref[k].astype(F32), odd_ref[k].astype(F32)))
+        piece = refs[0][s].astype(F32)
+        for k in range(1, FAR):
+            piece = jnp.where(shift == k, refs[k][s].astype(F32), piece)
+        pieces.append(piece)
     rows = jnp.concatenate(
         [pieces[s][4 * i:4 * i + 4] for i in range(ST_PIECE) for s in range(SLOTS)], axis=0
     ).astype(BF16)
@@ -299,17 +302,17 @@
         out_ref[j] = rows
 
 
-def pick_far(roots, even, odd, **kw):
+def pick_far(roots, pieces, **kw):
     return pl.pallas_call(
         pick_far_kernel,
         out_shape=jax.ShapeDtypeStruct((NEAR, ST_PIECE * SLOTS * 4, LANES), BF16),
-        in_specs=[smem(), vmem(), vmem()],
+        in_specs=[smem()] + [vmem()] * FAR,
         out_specs=vmem(),
         name="pick_far",
-        cost_estimate=pl.CostEstimate(flops=4200000000, bytes_accessed=800000, transcendentals=0),
-        compiler_params=room(),
-        **kw,
-    )(roots, even, odd)
+        cost_estimate=pl.CostEstimate(flops=5200000000, bytes_accessed=800000, transcendentals=0),
+        compiler_params=room(),
+        **kw,
+    )(roots, *pieces)
 
 
 ROWS_ST = SLOTS * 4
@@ -419,11 +422,10 @@
     sent = pack(owner_index[..., 0], subgrid_index, block_count, station_pair.swapaxes(1, 2), visibility, coordinate)
     pieces, sent = lax.optimization_barrier((pieces, sent))
     piece = pick_near(slot_owner, pieces)
-    even = jnp.concatenate([piece, shifted(piece, 2)], axis=0)
-    odd = shifted(even, 1)
+    far = [piece] + [shifted(piece, shift) for shift in range(1, FAR)]
     arrived = exchange(sent, "tm")
     meta = meta_of(arrived)
-    pieces = exchange(pick_far(slot_owner, even, odd), "uv", near)
+    pieces = exchange(pick_far(slot_owner, far), "uv", near)
     x = grid_blocks(meta, offsets.swapaxes(1, 2), arrived)
     meta, x = lax.optimization_barrier((meta, x))
     wanted = exchange(asked(meta, pieces), "tm")

time: 92.9 us -> 95.9 us (1.032)
  starting transfers between devices: 39.8 us -> 44.1 us
  blocking collectives: 18.8 us -> 15.8 us
  waiting for transfers between devices: 18.4 us -> 20.2 us
    all_to_all x3, waiting for transfers between devices: 14.1 us -> 20.2 us  [exchange(): lax.all_to_all(array, axis, 0, 0, axis_index_groups=groups, tiled=True)]
    ppermute x2 -> x3, waiting for transfers between devices: 4.26 us -> 0.01 us  [shifted(): return lax.ppermute(array, 'uv', pairs)]
    ppermute x2 -> x3, starting transfers between devices: 9.9 us -> 13.6 us  [shifted(): return lax.ppermute(array, 'uv', pairs)]
    all_to_all x1, blocking collectives: 18.8 us -> 15.8 us  [exchange(): lax.all_to_all(array, axis, 0, 0, axis_index_groups=groups, tiled=True)]
  transfers between devices with their start and end apart: 5 -> 6, of which waited for: 3 -> 3; matrix products, arithmetic and copies ran while one was open for 0% -> 0% of each run, Pallas kernels for 10% -> 10%
where the time goes in v10:
time: 95.9 us; the launch traced here: 95.4 us
  starting transfers between devices  44.1 us (46%)
  waiting for transfers between devices  20.2 us (21%)
  blocking collectives  15.8 us (16%)
  Pallas kernels  13.7 us (14%)
  local copies, waits for them, and re-layouts  1.43 us (1%)
    all_to_all x3, starting transfers between devices, exchange(): lax.all_to_all(array, axis, 0, 0, axis_index_groups=groups, tiled=True)  30.5 us
    all_to_all x3, waiting for transfers between devices, exchange(): lax.all_to_all(array, axis, 0, 0, axis_index_groups=groups, tiled=True)  20.2 us
    all_to_all x1, blocking collectives, exchange(): lax.all_to_all(array, axis, 0, 0, axis_index_groups=groups, tiled=True)  15.8 us
    ppermute x3, starting transfers between devices, shifted(): return lax.ppermute(array, 'uv', pairs)  13.6 us
    pallas_call x1, Pallas kernels, grid_blocks(): pl.pallas_call(grid_kernel, out_shape=jax.ShapeDtypeStruct((SLOTS * SUBS,...  5.95 us
    pallas_call x1, Pallas kernels, pack(): pl.pallas_call(pack_kernel, out_shape=jax.ShapeDtypeStruct((PEERS, ROWS,...  2.3 us
  transfers between devices with their start and end apart: 6, of which 3 were waited for; matrix products, arithmetic and copies ran while one was open for 0% of the time, Pallas kernels for 10%

profile of v10, /device:TPU:1, one launch (start us, length us, event | category | flops | bytes accessed | tf_op | source)
XLA Modules:
  0.0 95.4 jit_solution(6278936301703457190)
XLA Ops:
  0.0 1.5 %cut_chunk.1 = bf16[16,16,128]{2,1,0:T(8,128)(2,1)} custom-call(bf16[1,64,8,1024]{3,2,1,0:T(8,128)(2,1)} %screens_ref.1), custom_call_target="tpu_custom_call" | custom-call | tf_op jit(solution)/shard_map/cut_chunk/pallas_call | solution.py:260
  1.5 0.0 copy-start.1
  1.5 0.0 copy-start.4
  1.5 19.6 %all-to-all-start = ((bf16[16,16,128]{2,1,0:T(8,128)(2,1)}), bf16[16,16,128]{2,1,0:T(8,128)(2,1)S(1)}, u32[]{:S(2)}, u32[]{:S(2)}) async-start(bf16[16,16,128]{2,1,0:T(8,128)(2,1)} %cut_chunk.1), calls=%async_computation | async-start | bytes 131072 | tf_op jit(solution)/shard_map/all_to_all | solution.py:419
  21.1 0.0 copy-start.3
  21.2 0.6 copy-done.2
  21.8 0.0 copy-done.3
  21.8 2.3 %pack_blocks.1 = bf16[16,64,128]{2,1,0:T(8,128)(2,1)} custom-call(s32[3,1,16]{2,1,0:T(1,128)S(1)} %bitcast.3, s32[3,1,16]{2,1,0:T(1,128)S(1)} %copy-done.3, s32[3,1,16]{2,1,0:T(1,128)S(1)} %copy-done.4, s32[1,2,4]{2,1,0:T(2,128)S(1)} %bitcast.4, bf16[3,1,16,8,128]{4,3,2,1,0:T(8,128)(2,1)S(1)} %copy-done, bf16[3,1,16,2,128]{4,3,2,1,0:T(2,128)(2,1)S(1)} %copy-done.1), custom_call_target="tpu_custom_call" | custom-call | flops 2000000 | bytes 600000 | tf_op jit(solution)/shard_map/pack_blocks/pallas_call | solution.py:106
  24.1 8.6 %all-to-all-done.in_ref = bf16[16,16,128]{2,1,0:T(8,128)(2,1)S(1)} async-done(((bf16[16,16,128]{2,1,0:T(8,128)(2,1)}), bf16[16,16,128]{2,1,0:T(8,128)(2,1)S(1)}, u32[]{:S(2)}, u32[]{:S(2)}) %all-to-all-start) | async-done | bytes 65568 | tf_op jit(solution)/shard_map/all_to_all | solution.py:419
  32.7 0.6 pick_near.1.refs_0_
  33.2 5.9 %collective-permute-start.2 = (bf16[3,16,128]{2,1,0:T(8,128)(2,1)S(1)}, bf16[3,16,128]{2,1,0:T(8,128)(2,1)S(1)}, u32[]{:S(2)}, u32[]{:S(2)}) collective-permute-start(bf16[3,16,128]{2,1,0:T(8,128)(2,1)S(1)} %pick_near.1.refs_0_), channel_id=1, source_target_pairs={{0,48},{16,0},{32,16},{48,32},{64,112},{80,64},{96,80},{112,96},{1... | collective-permute-start | bytes 36872 | tf_op jit(solution)/shard_map/ppermute | solution.py:416
  39.1 3.5 %collective-permute-start.1 = (bf16[3,16,128]{2,1,0:T(8,128)(2,1)S(1)}, bf16[3,16,128]{2,1,0:T(8,128)(2,1)S(1)}, u32[]{:S(2)}, u32[]{:S(2)}) collective-permute-start(bf16[3,16,128]{2,1,0:T(8,128)(2,1)S(1)} %pick_near.1.refs_0_), channel_id=1, source_target_pairs={{0,32},{16,48},{32,0},{48,16},{64,96},{80,112},{96,64},{112,80},{1... | collective-permute-start | bytes 36872 | tf_op jit(solution)/shard_map/ppermute | solution.py:416
  42.7 4.2 %collective-permute-start = (bf16[3,16,128]{2,1,0:T(8,128)(2,1)S(1)}, bf16[3,16,128]{2,1,0:T(8,128)(2,1)S(1)}, u32[]{:S(2)}, u32[]{:S(2)}) collective-permute-start(bf16[3,16,128]{2,1,0:T(8,128)(2,1)S(1)} %pick_near.1.refs_0_), channel_id=1, source_target_pairs={{0,16},{16,32},{32,48},{48,0},{64,80},{80,96},{96,112},{112,64},{1... | collective-permute-start | bytes 36872 | tf_op jit(solution)/shard_map/ppermute | solution.py:416
  46.9 7.4 %all-to-all-start.1 = ((bf16[16,64,128]{2,1,0:T(8,128)(2,1)}), bf16[16,64,128]{2,1,0:T(8,128)(2,1)S(1)}, u32[]{:S(2)}, u32[]{:S(2)}) async-start(bf16[16,64,128]{2,1,0:T(8,128)(2,1)} %pack_blocks.1), calls=%async_computation.1 | async-start | bytes 524288 | tf_op jit(solution)/shard_map/all_to_all | solution.py:419
  54.3 1.3 %pick_far.1 = bf16[16,48,128]{2,1,0:T(8,128)(2,1)} custom-call(s32[3]{0:T(128)S(1)} %copy-done.6, bf16[3,16,128]{2,1,0:T(8,128)(2,1)S(1)} %pick_near.1.refs_0_, bf16[3,16,128]{2,1,0:T(8,128)(2,1)S(1)} %collective-permute-done.refs_1_, bf16[3,16,128]{2,1,0:T(8,128)(2,1)S(1)} %collective-permute-done.1.refs_2_, ...), custom_call_target="tpu_custom_call" | custom-call | flops 5200000000 | bytes 800000 | tf_op jit(solution)/shard_map/pick_far/pallas_call | solution.py:306
  55.6 5.9 %all-to-all-done.1.rows_ref = bf16[16,64,128]{2,1,0:T(8,128)(2,1)S(1)} async-done(((bf16[16,64,128]{2,1,0:T(8,128)(2,1)}), bf16[16,64,128]{2,1,0:T(8,128)(2,1)S(1)}, u32[]{:S(2)}, u32[]{:S(2)}) %all-to-all-start.1) | async-done | bytes 262176 | tf_op jit(solution)/shard_map/all_to_all | solution.py:419
  61.5 3.5 %all-to-all-start.2 = ((bf16[16,48,128]{2,1,0:T(8,128)(2,1)}), bf16[16,48,128]{2,1,0:T(8,128)(2,1)S(1)}, u32[]{:S(2)}, u32[]{:S(2)}) async-start(bf16[16,48,128]{2,1,0:T(8,128)(2,1)} %pick_far.1), calls=%async_computation.2 | async-start | bytes 393216 | tf_op jit(solution)/shard_map/all_to_all | solution.py:419
  65.0 0.1 reshape.4.meta
  65.1 0.7 copy-done.7
  65.8 6.0 %grid_blocks.1.x_ref = f32[12,8,8,128]{3,2,1,0:T(8,128)S(1)} custom-call(s32[512]{0:T(512)S(1)} %reshape.4.meta, s32[1,2,4]{2,1,0:T(2,128)S(1)} %bitcast.5, bf16[16,64,128]{2,1,0:T(8,128)(2,1)S(1)} %all-to-all-done.1.rows_ref), custom_call_target="tpu_custom_call" | custom-call | flops 800000000 | bytes 800000 | tf_op jit(solution)/shard_map/grid_blocks/pallas_call | solution.py:214
  71.8 5.7 %all-to-all-done.2.in_ref = bf16[16,48,128]{2,1,0:T(8,128)(2,1)S(1)} async-done(((bf16[16,48,128]{2,1,0:T(8,128)(2,1)}), bf16[16,48,128]{2,1,0:T(8,128)(2,1)S(1)}, u32[]{:S(2)}, u32[]{:S(2)}) %all-to-all-start.2) | async-done | bytes 196640 | tf_op jit(solution)/shard_map/all_to_all | solution.py:419
  77.5 0.9 asked_stations.1
  78.4 15.8 %all_to_all.20.in_ref = bf16[16,96,128]{2,1,0:T(8,128)(2,1)S(1)} all-to-all(bf16[16,96,128]{2,1,0:T(8,128)(2,1)S(1)} %asked_stations.1), channel_id=1, replica_groups=mesh['uv'=64,'tm'=16] {'tm'}, dimensions={0} | all-to-all | bytes 786432 | tf_op jit(solution)/shard_map/all_to_all | solution.py:419
  94.2 1.2 %screen_product.1 = f32[1,4,8,1024]{3,2,1,0:T(8,128)} custom-call(f32[12,8,8,128]{3,2,1,0:T(8,128)S(1)} %grid_blocks.1.x_ref, bf16[16,96,128]{2,1,0:T(8,128)(2,1)S(1)} %all_to_all.20.in_ref), custom_call_target="tpu_custom_call" | custom-call | flops 3000000 | bytes 1000000 | tf_op jit(solution)/shard_map/screen_product/pallas_call | solution.py:390
  (14 shorter events, 0.1 us)
Async XLA Ops:
  1.5 19.6 %copy-start = (bf16[3,1,16,8,128]{4,3,2,1,0:T(8,128)(2,1)S(1)}, bf16[3,1,16,8,128]{4,3,2,1,0:T(8,128)(2,1)}, u32[]{:S(2)}) copy-start(bf16[3,1,16,8,128]{4,3,2,1,0:T(8,128)(2,1)} %vis_ref.1) | copy-start | bytes 294916
  1.5 19.6 %copy-start.1 = (bf16[3,1,16,2,128]{4,3,2,1,0:T(2,128)(2,1)S(1)}, bf16[3,1,16,2,128]{4,3,2,1,0:T(2,128)(2,1)}, u32[]{:S(2)}) copy-start(bf16[3,1,16,2,128]{4,3,2,1,0:T(2,128)(2,1)} %coord_ref.1) | copy-start | bytes 73732
  1.5 19.6 %copy-start.4 = (s32[3,1,16]{2,1,0:T(1,128)S(1)}, s32[3,1,16]{2,1,0:T(1,128)}, u32[]{:S(2)}) copy-start(s32[3,1,16]{2,1,0:T(1,128)} %counts.1) | copy-start | bytes 580
  1.5 19.6 %copy-start.5 = (s32[1,4,2]{1,2,0:T(2,128)S(1)}, s32[1,4,2]{1,2,0:T(2,128)}, u32[]{:S(2)}) copy-start(s32[1,4,2]{1,2,0:T(2,128)} %param.15) | copy-start | bytes 100
  1.5 31.1 %all-to-all-start = ((bf16[16,16,128]{2,1,0:T(8,128)(2,1)}), bf16[16,16,128]{2,1,0:T(8,128)(2,1)S(1)}, u32[]{:S(2)}, u32[]{:S(2)}) async-start(bf16[16,16,128]{2,1,0:T(8,128)(2,1)} %cut_chunk.1), calls=%async_computation | async-start | bytes 131072 | tf_op jit(solution)/shard_map/all_to_all | solution.py:419
  21.1 0.7 copy-start.2
  21.1 0.7 copy-start.3
  21.8 10.9 %copy-start.6 = (s32[3]{0:T(128)S(1)}, s32[3]{0:T(128)}, u32[]{:S(2)}) copy-start(s32[3]{0:T(128)} %roots.3) | copy-start | bytes 40
  33.2 21.1 %collective-permute-start.2 = (bf16[3,16,128]{2,1,0:T(8,128)(2,1)S(1)}, bf16[3,16,128]{2,1,0:T(8,128)(2,1)S(1)}, u32[]{:S(2)}, u32[]{:S(2)}) collective-permute-start(bf16[3,16,128]{2,1,0:T(8,128)(2,1)S(1)} %pick_near.1.refs_0_), channel_id=1, source_target_pairs={{0,48},{16,0},{32,16},{48,32},{64,112},{80,64},{96,80},{112,96},{1... | collective-permute-start | bytes 36872 | tf_op jit(solution)/shard_map/ppermute | solution.py:416
  39.1 15.2 %collective-permute-start.1 = (bf16[3,16,128]{2,1,0:T(8,128)(2,1)S(1)}, bf16[3,16,128]{2,1,0:T(8,128)(2,1)S(1)}, u32[]{:S(2)}, u32[]{:S(2)}) collective-permute-start(bf16[3,16,128]{2,1,0:T(8,128)(2,1)S(1)} %pick_near.1.refs_0_), channel_id=1, source_target_pairs={{0,32},{16,48},{32,0},{48,16},{64,96},{80,112},{96,64},{112,80},{1... | collective-permute-start | bytes 36872 | tf_op jit(solution)/shard_map/ppermute | solution.py:416
  42.7 11.6 %collective-permute-start = (bf16[3,16,128]{2,1,0:T(8,128)(2,1)S(1)}, bf16[3,16,128]{2,1,0:T(8,128)(2,1)S(1)}, u32[]{:S(2)}, u32[]{:S(2)}) collective-permute-start(bf16[3,16,128]{2,1,0:T(8,128)(2,1)S(1)} %pick_near.1.refs_0_), channel_id=1, source_target_pairs={{0,16},{16,32},{32,48},{48,0},{64,80},{80,96},{96,112},{112,64},{1... | collective-permute-start | bytes 36872 | tf_op jit(solution)/shard_map/ppermute | solution.py:416
  46.9 14.6 %all-to-all-start.1 = ((bf16[16,64,128]{2,1,0:T(8,128)(2,1)}), bf16[16,64,128]{2,1,0:T(8,128)(2,1)S(1)}, u32[]{:S(2)}, u32[]{:S(2)}) async-start(bf16[16,64,128]{2,1,0:T(8,128)(2,1)} %pack_blocks.1), calls=%async_computation.1 | async-start | bytes 524288 | tf_op jit(solution)/shard_map/all_to_all | solution.py:419
  61.5 16.0 %all-to-all-start.2 = ((bf16[16,48,128]{2,1,0:T(8,128)(2,1)}), bf16[16,48,128]{2,1,0:T(8,128)(2,1)S(1)}, u32[]{:S(2)}, u32[]{:S(2)}) async-start(bf16[16,48,128]{2,1,0:T(8,128)(2,1)} %pick_far.1), calls=%async_computation.2 | async-start | bytes 393216 | tf_op jit(solution)/shard_map/all_to_all | solution.py:419
  65.1 0.7 copy-start.7
